TPU v7x, 256 devices: a whole 4x4x8 slice. The times are simulated.
256 devices in a mesh: vocab: 128 (over y, x, z), rows: 2 (over core).
Axes of the slice: x: 4, y: 4, z: 8, core: 2. Of those that a mesh axis runs over, the one named last changes fastest.
Arguments:
- hidden: bfloat16 [512, 4096], P('rows', 'vocab'), may hold values from -64 to 64
- head_weight: bfloat16 [4096, 131072], P(None, 'vocab'), may hold values from -0.09375 to 0.09375
- mentor_outputs: bfloat16 [512, 131072], P('rows', 'vocab'), may hold values from -480 to 480
Outputs:
- hidden_grad: bfloat16 [512, 4096], P('rows', 'vocab')
- weight_grad: bfloat16 [4096, 131072], P('rows', 'vocab')
- per_position_mismatch: float32 [512], P('rows')
All inputs are finite; a program needn't handle non-finite values.
Results may differ from a plain program's by a relative error of at most 0.0043.
Values may be sent and summed in bfloat16 or wider, within the bound.
No kernel may reach another device: no remote copies, remote signals or barrier semaphores. Data moves between devices by JAX's collectives and lax.ppermute only.
A program may use at most 128 MiB of HBM per device.

v0:
```python
import jax
import jax.numpy as jnp
from jax import lax
from jax.sharding import PartitionSpec as P

sharpness_divisor = 2.0
objective_factor = 32.0


def shards(hidden, head_weight, mentor_outputs):
    full_hidden = lax.all_gather(hidden, "vocab", axis=1, tiled=True)
    unnormalized_outputs = jnp.dot(full_hidden, head_weight, preferred_element_type=jnp.float32)
    learner_raw_outputs = unnormalized_outputs / sharpness_divisor
    mentor_raw_outputs = mentor_outputs.astype(jnp.float32) / sharpness_divisor
    top_s, top_t = lax.pmax(
        (jnp.max(learner_raw_outputs, axis=1), jnp.max(mentor_raw_outputs, axis=1)), "vocab"
    )
    exp_s = jnp.exp(learner_raw_outputs - top_s[:, None])
    exp_t = jnp.exp(mentor_raw_outputs - top_t[:, None])
    total_s, total_t, weighted = lax.psum(
        (
            jnp.sum(exp_s, axis=1),
            jnp.sum(exp_t, axis=1),
            jnp.sum(exp_t * (mentor_raw_outputs - learner_raw_outputs), axis=1),
        ),
        "vocab",
    )
    learner_partition_value = top_s + jnp.log(total_s)
    mentor_partition_value = top_t + jnp.log(total_t)
    mismatch_summand = weighted / total_t
    per_position_mismatch = (
        sharpness_divisor
        * sharpness_divisor
        * (mismatch_summand + learner_partition_value - mentor_partition_value)
    )
    learner_likelihood = jnp.exp(learner_raw_outputs - learner_partition_value[:, None])
    mentor_likelihood = jnp.exp(mentor_raw_outputs - mentor_partition_value[:, None])
    raw_score_derivative = (
        objective_factor * sharpness_divisor * (learner_likelihood - mentor_likelihood)
    ).astype(jnp.bfloat16)
    hidden_part = lax.psum_scatter(
        lax.dot_general(
            head_weight,
            raw_score_derivative,
            (((1,), (1,)), ((), ())),
            preferred_element_type=jnp.float32,
        ),
        "vocab",
        scatter_dimension=0,
        tiled=True,
    )
    hidden_grad = hidden_part.T.astype(jnp.bfloat16)
    weight_grad = lax.psum_scatter(
        lax.dot_general(
            full_hidden,
            raw_score_derivative,
            (((0,), (0,)), ((), ())),
            preferred_element_type=jnp.float32,
        ),
        "rows",
        scatter_dimension=0,
        tiled=True,
    ).astype(jnp.bfloat16)
    return (hidden_grad, weight_grad, per_position_mismatch)


def solution(mesh):
    placed = (P("rows", "vocab"), P(None, "vocab"), P("rows", "vocab"))
    return jax.shard_map(
        shards,
        mesh=mesh,
        in_specs=placed,
        out_specs=(P("rows", "vocab"), P("rows", "vocab"), P("rows")),
        check_vma=False,
    )
```

profile of v0, /device:TPU:2, one launch (start us, length us, event | category | flops | bytes accessed | tf_op | source)
XLA Modules:
  0.0 1578.3 jit_solution(3627062798192049260)
XLA Ops:
  7.2 0.0 all-gather.2.cloned.1.call-start
  7.2 0.7 all-gather.2.cloned.1.call-update
  7.9 0.0 reduce-scatter.7.cloned.1.call-start
  7.9 1.2 fusion.1
  9.2 0.0 copy-start.1
  9.2 119.6 %all-gather.2.cloned.1.call-done = bf16[256,4096]{0,1:T(8,128)(2,1)} async-done(((bf16[256,32]{0,1:T(8,128)(2,1)}), bf16[256,4096]{0,1:T(8,128)(2,1)}) %all-gather.2.cloned.1.call-update) | async-done | bytes 2097168 | tf_op jit(solution)/shard_map/all_gather | solution.py:11
  128.7 6.5 fusion.2
  135.2 326.1 %all-reduce.1 = (f32[256]{0:T(256)S(1)}, f32[256]{0:T(256)S(1)}) all-reduce(f32[256]{0:T(256)S(1)} %fusion.1, f32[256]{0:T(256)S(1)} %get-tuple-element.20), channel_id=1, replica_groups=mesh['vocab'=128,'rows'=2] {'vocab'}, use_global_device_ids=true, to_apply=%region_5.0 | all-reduce | flops 512 | bytes 4096 | tf_op jit(solution)/shard_map/pmax | solution.py:15
  461.3 0.0 copy-done.1
  461.3 0.7 multiply_reduce_fusion
  461.9 342.1 %all-reduce = (f32[256]{0:T(256)S(1)}, f32[256]{0:T(256)S(1)}, f32[256]{0:T(256)S(1)}) all-reduce(f32[256]{0:T(256)S(1)} %get-tuple-element.11, f32[256]{0:T(256)S(1)} %get-tuple-element.10, f32[256]{0:T(256)S(1)} %get-tuple-element.9), channel_id=1, replica_groups=mesh['vocab'=128,'rows'=2] {'vocab'}, use_global_device_ids=true, to_apply=%region_7.0 | all-reduce | flops 768 | bytes 6144 | tf_op jit(solution)/shard_map/psum | solution.py:20
  804.0 0.6 subtract_multiply_fusion
  804.6 8.0 convolution_bitcast_fusion.1
  812.6 5.6 copy.10
  818.2 0.0 copy-start
  818.2 0.0 reduce-scatter.7.cloned.1.call-update
  818.2 0.0 reduce-scatter.5.cloned.1.call-start
  818.3 1.5 copy-done
  819.8 9.5 convolution_bitcast_fusion
  829.3 0.0 reduce-scatter.5.cloned.1.call-update
  829.3 683.0 %reduce-scatter.7.cloned.1.call-done = f32[32,256]{1,0:T(8,128)} async-done(((f32[4096,256]{1,0:T(8,128)}), f32[32,256]{1,0:T(8,128)}) %reduce-scatter.7.cloned.1.call-update) | async-done | bytes 32784
  1512.3 0.9 copy.11
  1513.2 0.7 copy.8
  1513.9 45.6 %reduce-scatter.5.cloned.1.call-done = f32[2048,1024]{0,1:T(8,128)} async-done(((f32[4096,1024]{0,1:T(8,128)}), f32[2048,1024]{0,1:T(8,128)}) %reduce-scatter.5.cloned.1.call-update) | async-done | bytes 8388624 | tf_op jit(solution)/shard_map/reduce_scatter | solution.py:53
  1559.4 6.0 convert_element_type.19
  1565.4 6.4 copy.9
Async XLA Ops:
  7.2 121.6 %all-gather.2.cloned.1.call-start = ((), (), s32[]{:S(2)}) async-start(), calls=%async_computation.2 | async-start | bytes 2113536 | tf_op jit(solution)/shard_map/all_gather | solution.py:11
  7.9 1504.4 %reduce-scatter.7.cloned.1.call-start = ((), (), s32[]{:S(2)}) async-start(), calls=%async_computation.4 | async-start | bytes 4227072
  9.2 452.1 %copy-start.1 = (bf16[256,1024]{1,0:T(8,128)(2,1)S(1)}, bf16[256,1024]{1,0:T(8,128)(2,1)}, u32[]{:S(2)}) copy-start(bf16[256,1024]{1,0:T(8,128)(2,1)} %param.5) | copy-start | bytes 1572868
  818.2 1.6 copy-start
  818.2 741.2 %reduce-scatter.5.cloned.1.call-start = ((), (), s32[]{:S(2)}) async-start(), calls=%async_computation.3 | async-start | bytes 25165824 | tf_op jit(solution)/shard_map/reduce_scatter | solution.py:53
Sparse Core Ops, SparseCore 0:
  11.6 117.0 all-gather.1
  818.3 693.9 reduce-scatter.6
  1515.0 44.3 reduce-scatter.4
where the time goes:
time: 1580 us
  waiting for transfers between devices  849 us (54%)
  blocking collectives  668 us (42%)
  matrix products  23.9 us (2%)
    unnamed x4, waiting for transfers between devices  684 us
    psum x1, blocking collectives, shards(): lax.psum((jnp.sum(exp_s, axis=1), jnp.sum(exp_t, axis=1), jnp.sum(exp_t *...  342 us
    pmax x1, blocking collectives, shards(): lax.pmax((jnp.max(learner_raw_outputs, axis=1), jnp.max(mentor_raw_output...  326 us
    all_gather x1, waiting for transfers between devices, shards(): full_hidden = lax.all_gather(hidden, 'vocab', axis=1, tiled=True)  120 us
    reduce_scatter x1, waiting for transfers between devices, shards(): lax.psum_scatter(lax.dot_general(full_hidden, raw_score_derivative, (((0,...  45.6 us
  transfers between devices with their start and end apart: 3, of which 3 were waited for; matrix products, arithmetic and copies ran while one was open for 1% of the time, Pallas kernels for 0%

commit v1 on v0

v1 whole, which is shorter than its diff:
```python
import jax
import jax.numpy as jnp
from jax import lax
from jax.sharding import PartitionSpec as P

sharpness_divisor = 2.0
objective_factor = 32.0

NY, NX, NZ = 4, 4, 8


def place(y, x, z):
    return (y * NX + x) * NZ + z


z_groups = [[place(y, x, z) for z in range(NZ)] for y in range(NY) for x in range(NX)]
xy_groups = [[place(y, x, z) for y in range(NY) for x in range(NX)] for z in range(NZ)]


def trade(chunks, groups):
    return lax.all_to_all(chunks, "vocab", 0, 0, tiled=True, axis_index_groups=groups)


def spread(block, count, groups):
    return trade(jnp.broadcast_to(block[None], (count,) + block.shape), groups)


def other_core(value):
    return lax.ppermute(value, "rows", [(0, 1), (1, 0)])


def local_lse(scores):
    top = jnp.max(scores, axis=1)
    return top + jnp.log(jnp.sum(jnp.exp(scores - top[:, None]), axis=1))


def lse_of_shards(parts):
    top = jnp.max(parts, axis=0)
    return top + jnp.log(jnp.sum(jnp.exp(parts - top[None]), axis=0))


def shards(hidden, head_weight, mentor_outputs):
    core = lax.axis_index("rows")
    slab = spread(hidden.T, NZ, z_groups).reshape(256, 256)
    hidden_t = spread(slab, NX * NY, xy_groups).reshape(4096, 256)
    mine = lax.dynamic_slice_in_dim(hidden_t, core * 2048, 2048, 0)
    theirs = other_core(lax.dynamic_slice_in_dim(hidden_t, (1 - core) * 2048, 2048, 0))

    target = mentor_outputs.astype(jnp.float32) / sharpness_divisor
    lse_t = local_lse(target)
    student = (
        lax.dot_general(
            hidden_t, head_weight, (((0,), (0,)), ((), ())), preferred_element_type=jnp.float32
        )
        / sharpness_divisor
    )
    lse_s = local_lse(student)
    cross = jnp.sum(jnp.exp(target - lse_t[:, None]) * (target - student), axis=1)
    stats = jnp.stack([lse_s, lse_t, cross]).reshape(6, 128)
    stats = spread(stats, NX * NY * NZ, None).reshape(128, 3, 256)
    all_s, all_t = lse_of_shards(stats[:, 0]), lse_of_shards(stats[:, 1])
    all_cross = jnp.sum(jnp.exp(stats[:, 1] - all_t[None]) * stats[:, 2], axis=0)
    mismatch = sharpness_divisor * sharpness_divisor * (all_cross + all_s - all_t)

    score = (
        objective_factor
        * sharpness_divisor
        * (jnp.exp(student - all_s[:, None]) - jnp.exp(target - all_t[:, None]))
    ).astype(jnp.bfloat16)
    score_theirs = other_core(score)

    part = lax.dot_general(
        head_weight, score, (((1,), (1,)), ((), ())), preferred_element_type=jnp.float32
    ).astype(jnp.bfloat16)
    part = trade(part.reshape(16, 256, 256), xy_groups)
    part = jnp.sum(part.astype(jnp.float32), axis=0).astype(jnp.bfloat16)
    part = trade(part.reshape(8, 32, 256), z_groups)
    hidden_grad = jnp.sum(part.astype(jnp.float32), axis=0).astype(jnp.bfloat16).T

    weight_grad = jnp.dot(
        jnp.concatenate([mine, theirs], axis=1),
        jnp.concatenate([score, score_theirs], axis=0),
        preferred_element_type=jnp.float32,
    ).astype(jnp.bfloat16)
    return (hidden_grad, weight_grad, mismatch)


def solution(mesh):
    return jax.shard_map(
        shards,
        mesh=mesh,
        in_specs=(P("rows", "vocab"), P(None, "vocab"), P("rows", "vocab")),
        out_specs=(P("rows", "vocab"), P("rows", "vocab"), P("rows")),
        check_vma=False,
    )
```

time: 1580 us -> 151 us (0.10)
  waiting for transfers between devices: 849 us -> 52.8 us
  blocking collectives: 668 us -> 44.5 us
  starting transfers between devices: 0.12 us -> 18.9 us
    unnamed x4 -> x0, waiting for transfers between devices: 684 us -> none
    psum x1 -> x0, blocking collectives: 342 us -> none  [shards(): lax.psum((jnp.sum(exp_s, axis=1), jnp.sum(exp_t, axis=1), jnp.sum(exp_t *...]
    pmax x1 -> x0, blocking collectives: 326 us -> none  [shards(): lax.pmax((jnp.max(learner_raw_outputs, axis=1), jnp.max(mentor_raw_output...]
    all_gather x1 -> x0, waiting for transfers between devices: 120 us -> none  [shards(): full_hidden = lax.all_gather(hidden, 'vocab', axis=1, tiled=True)]
    all_to_all x0 -> x3, waiting for transfers between devices: none -> 52.8 us  [trade(): lax.all_to_all(chunks, 'vocab', 0, 0, tiled=True, axis_index_groups=groups)]
    reduce_scatter x1 -> x0, waiting for transfers between devices: 45.6 us -> none  [shards(): lax.psum_scatter(lax.dot_general(full_hidden, raw_score_derivative, (((0,...]
    all_to_all x0 -> x2, blocking collectives: none -> 44.5 us  [trade(): lax.all_to_all(chunks, 'vocab', 0, 0, tiled=True, axis_index_groups=groups)]
    all_to_all x0 -> x3, starting transfers between devices: none -> 18.4 us  [trade(): lax.all_to_all(chunks, 'vocab', 0, 0, tiled=True, axis_index_groups=groups)]
  transfers between devices with their start and end apart: 3 -> 5, of which waited for: 3 -> 3; matrix products, arithmetic and copies ran while one was open for 1% -> 7% of each run, Pallas kernels for 0% -> 0%
where the time goes in v1:
time: 151 us; the launch traced here: 148 us
  waiting for transfers between devices  52.8 us (35%)
  blocking collectives  44.5 us (29%)
  starting transfers between devices  18.9 us (13%)
  matrix products  17.2 us (11%)
  other arithmetic  7.05 us (5%)
  local copies, waits for them, and re-layouts  6.9 us (5%)
    all_to_all x3, waiting for transfers between devices, trade(): lax.all_to_all(chunks, 'vocab', 0, 0, tiled=True, axis_index_groups=groups)  52.8 us
    all_to_all x2, blocking collectives, trade(): lax.all_to_all(chunks, 'vocab', 0, 0, tiled=True, axis_index_groups=groups)  44.5 us
    all_to_all x3, starting transfers between devices, trade(): lax.all_to_all(chunks, 'vocab', 0, 0, tiled=True, axis_index_groups=groups)  18.4 us
    dot_general x1, matrix products, shards(): lax.dot_general(head_weight, score, (((1,), (1,)), ((), ())), preferred_e...  5.93 us
    dot_general x1, matrix products, shards(): lax.dot_general(hidden_t, head_weight, (((0,), (0,)), ((), ())), preferre...  5.88 us
    dot_general x1, matrix products, shards(): jnp.dot(jnp.concatenate([mine, theirs], axis=1), jnp.concatenate([score,...  5.4 us
  transfers between devices with their start and end apart: 5, of which 3 were waited for; matrix products, arithmetic and copies ran while one was open for 7% of the time, Pallas kernels for 0%

profile of v1, /device:TPU:2, one launch (start us, length us, event | category | flops | bytes accessed | tf_op | source)
XLA Modules:
  0.0 148.1 jit_solution(2432725242345564195)
XLA Ops:
  0.6 0.7 broadcast_in_dim.10
  1.4 17.4 %all_to_all.25 = bf16[8,32,256]{2,1,0:T(8,128)(2,1)S(1)} all-to-all(bf16[8,32,256]{2,1,0:T(8,128)(2,1)S(1)} %broadcast_in_dim.10), channel_id=1, replica_groups={{0,2,4,6,8,10,12,14},{16,18,20,22,24,26,28,30},{32,34,36,38,40,42,44,46..., dimensions={0} | all-to-all | bytes 262144 | tf_op jit(solution)/shard_map/all_to_all | solution.py:21
  18.7 1.5 %broadcast_in_dim.12 = bf16[16,256,256]{2,1,0:T(8,128)(2,1)} broadcast(bf16[256,256]{1,0:T(8,128)(2,1)S(1)} %bitcast.48), dimensions={1,2} | broadcast | bytes 2228224 | tf_op jit(solution)/shard_map/broadcast_in_dim | solution.py:25
  20.2 0.0 copy-start
  20.2 7.6 %all-to-all-start.1 = ((bf16[16,256,256]{2,1,0:T(8,128)(2,1)}), bf16[16,256,256]{2,1,0:T(8,128)(2,1)S(1)}, u32[]{:S(2)}, u32[]{:S(2)}) async-start(bf16[16,256,256]{2,1,0:T(8,128)(2,1)} %broadcast_in_dim.12), calls=%async_computation.1 | async-start | bytes 4194304 | tf_op jit(solution)/shard_map/all_to_all | solution.py:21
  27.9 0.0 copy-done
  27.9 0.2 fusion.6
  28.0 0.3 exponential_reduce_fusion
  28.4 25.0 %all-to-all-done.1 = bf16[16,256,256]{2,1,0:T(8,128)(2,1)S(1)} async-done(((bf16[16,256,256]{2,1,0:T(8,128)(2,1)}), bf16[16,256,256]{2,1,0:T(8,128)(2,1)S(1)}, u32[]{:S(2)}, u32[]{:S(2)}) %all-to-all-start.1) | async-done | bytes 2097184 | tf_op jit(solution)/shard_map/all_to_all | solution.py:21
  53.4 0.0 copy-start.1
  53.4 5.9 %fusion.15 = (f32[256]{0:T(256)S(1)}, f32[256,1024]{1,0:T(8,128)S(1)}) fusion(bf16[4096,256]{1,0:T(8,128)(2,1)S(1)} %bitcast.41, bf16[4096,1024]{1,0:T(8,128)(2,1)} %param.4), kind=kOutput, calls=%fused_computation.38 | convolution fusion | flops 2148007680 | bytes 11535360 | tf_op jit(solution)/shard_map/dot_general | solution.py:52
  59.3 0.0 copy-done.1
  59.3 0.6 exponential_reduce_fusion.1
  59.9 27.2 %all_to_all.26 = f32[128,6,128]{2,1,0:T(8,128)} all-to-all(f32[128,6,128]{2,1,0:T(8,128)S(1)} %broadcast_in_dim.14), channel_id=1, replica_groups=mesh['vocab'=128,'rows'=2] {'vocab'}, dimensions={0} | all-to-all | bytes 786432 | tf_op jit(solution)/shard_map/all_to_all | solution.py:21
  87.1 1.2 copy.10
  88.3 0.1 slice_reduce_fusion
  88.4 0.2 fusion.10
  88.6 0.3 fusion.8
  88.9 0.6 subtract_multiply_fusion
  89.5 2.2 %multiply_convert_fusion = bf16[256,1024]{1,0:T(8,128)(2,1)} fusion(f32[256,1024]{1,0:T(8,128)S(1)} %get-tuple-element.14, bf16[256,1024]{1,0:T(8,128)(2,1)} %param.5, f32[256]{0:T(256)S(1)} %log_add_fusion, f32[256]{0:T(256)S(1)} %get-tuple-element.10), kind=kLoop, calls=%fused_computation.10 | loop fusion | flops 1835008 | bytes 2099200 | tf_op jit(solution)/shard_map/convert_element_type | solution.py:69
  91.7 5.9 %convolution_convert_fusion = bf16[256,4096]{1,0:T(8,128)(2,1)S(1)} fusion(bf16[256,1024]{1,0:T(8,128)(2,1)} %multiply_convert_fusion, bf16[4096,1024]{1,0:T(8,128)(2,1)} %param.4), kind=kOutput, calls=%fused_computation | convolution fusion | flops 2148532224 | bytes 11010048 | tf_op jit(solution)/shard_map/dot_general | solution.py:72
  97.7 1.5 %copy.17 = bf16[32,16,8,256]{3,2,0,1:T(8,128)(2,1)} copy(bf16[32,16,8,256]{3,2,1,0:T(8,128)(2,1)S(1)} %bitcast.47) | data formatting | bytes 4194304 | tf_op jit(solution)/shard_map/reshape | solution.py:75
  99.2 7.4 %all-to-all-start.3 = ((bf16[16,256,256]{1,2,0:T(8,128)(2,1)}), bf16[16,256,256]{1,2,0:T(8,128)(2,1)}, u32[]{:S(2)}, u32[]{:S(2)}) async-start(bf16[16,256,256]{1,2,0:T(8,128)(2,1)} %bitcast.43), calls=%async_computation.3 | async-start | bytes 4194304 | tf_op jit(solution)/shard_map/all_to_all | solution.py:21
  106.6 1.1 constant_dynamic-slice_fusion.1
  107.7 0.0 collective-permute-start
  107.7 0.5 collective-permute-start.1
  108.2 24.2 %all-to-all-done.3 = bf16[16,256,256]{1,2,0:T(8,128)(2,1)} async-done(((bf16[16,256,256]{1,2,0:T(8,128)(2,1)}), bf16[16,256,256]{1,2,0:T(8,128)(2,1)}, u32[]{:S(2)}, u32[]{:S(2)}) %all-to-all-start.3) | async-done | bytes 2097184 | tf_op jit(solution)/shard_map/all_to_all | solution.py:21
  132.4 1.9 %reduce_sum.83 = bf16[256,256]{0,1:T(8,128)(2,1)S(1)} reduce(bf16[16,256,256]{1,2,0:T(8,128)(2,1)} %all-to-all-done.3, bf16[]{:T(256)} %constant.9.clone.1), dimensions={0}, to_apply=%region_9.0 | reduce | flops 983040 | bytes 2228226 | tf_op jit(solution)/shard_map/reduce_sum | solution.py:76
  134.3 0.7 copy.13
  135.1 3.4 %all-to-all-start.4 = ((bf16[8,32,256]{2,1,0:T(8,128)(2,1)}), bf16[8,32,256]{2,1,0:T(8,128)(2,1)S(1)}, u32[]{:S(2)}, u32[]{:S(2)}) async-start(bf16[8,32,256]{2,1,0:T(8,128)(2,1)} %bitcast.10), calls=%async_computation.4 | async-start | bytes 262144 | tf_op jit(solution)/shard_map/all_to_all | solution.py:21
  138.5 0.0 collective-permute-done
  138.5 0.0 collective-permute-done.1
  138.5 5.4 %convolution_convert_fusion.1 = bf16[2048,1024]{1,0:T(8,128)(2,1)} fusion(bf16[2048,256]{1,0:T(8,128)(2,1)S(1)} %collective-permute-done, bf16[2048,256]{1,0:T(8,128)(2,1)S(1)} %get-tuple-element.11, bf16[256,1024]{1,0:T(8,128)(2,1)S(1)} %collective-permute-done.1, bf16[256,1024]{1,0:T(8,128)(2,1)} %multiply_convert_fusion), kind=kOutput, calls=%fused_computation.1 | convolution fusion | flops 2155872256 | bytes 7340032 | tf_op jit(solution)/shard_map/dot_general | solution.py:80
  143.9 3.6 %all-to-all-done.4 = bf16[8,32,256]{2,1,0:T(8,128)(2,1)S(1)} async-done(((bf16[8,32,256]{2,1,0:T(8,128)(2,1)}), bf16[8,32,256]{2,1,0:T(8,128)(2,1)S(1)}, u32[]{:S(2)}, u32[]{:S(2)}) %all-to-all-start.4) | async-done | bytes 131104 | tf_op jit(solution)/shard_map/all_to_all | solution.py:21
  147.4 0.6 reduce_sum.84
  (6 shorter events, 0.1 us)
Async XLA Ops:
  20.2 7.6 %copy-start = (bf16[256,1024]{1,0:T(8,128)(2,1)S(1)}, bf16[256,1024]{1,0:T(8,128)(2,1)}, u32[]{:S(2)}) copy-start(bf16[256,1024]{1,0:T(8,128)(2,1)} %param.5) | copy-start | bytes 1572868
  20.2 33.1 %all-to-all-start.1 = ((bf16[16,256,256]{2,1,0:T(8,128)(2,1)}), bf16[16,256,256]{2,1,0:T(8,128)(2,1)S(1)}, u32[]{:S(2)}, u32[]{:S(2)}) async-start(bf16[16,256,256]{2,1,0:T(8,128)(2,1)} %broadcast_in_dim.12), calls=%async_computation.1 | async-start | bytes 4194304 | tf_op jit(solution)/shard_map/all_to_all | solution.py:21
  53.4 5.9 %copy-start.1 = (bf16[256,1024]{1,0:T(8,128)(2,1)S(1)}, bf16[256,1024]{1,0:T(8,128)(2,1)}, u32[]{:S(2)}) copy-start(bf16[256,1024]{1,0:T(8,128)(2,1)} %param.5) | copy-start | bytes 1572868
  99.2 33.2 %all-to-all-start.3 = ((bf16[16,256,256]{1,2,0:T(8,128)(2,1)}), bf16[16,256,256]{1,2,0:T(8,128)(2,1)}, u32[]{:S(2)}, u32[]{:S(2)}) async-start(bf16[16,256,256]{1,2,0:T(8,128)(2,1)} %bitcast.43), calls=%async_computation.3 | async-start | bytes 4194304 | tf_op jit(solution)/shard_map/all_to_all | solution.py:21
  107.7 30.7 %collective-permute-start = (bf16[2048,256]{1,0:T(8,128)(2,1)}, bf16[2048,256]{1,0:T(8,128)(2,1)S(1)}, u32[]{:S(2)}, u32[]{:S(2)}) collective-permute-start(bf16[2048,256]{1,0:T(8,128)(2,1)} %get-tuple-element.12), channel_id=1, source_target_pairs={{0,1},{1,0},{2,3},{3,2},{4,5},{5,4},{6,7},{7,6},{8,9},{9,8},{10,11... | collective-permute-start | bytes 3145736 | tf_op jit(solution)/shard_map/ppermute | solution.py:29
  107.7 30.7 %collective-permute-start.1 = (bf16[256,1024]{1,0:T(8,128)(2,1)}, bf16[256,1024]{1,0:T(8,128)(2,1)S(1)}, u32[]{:S(2)}, u32[]{:S(2)}) collective-permute-start(bf16[256,1024]{1,0:T(8,128)(2,1)} %multiply_convert_fusion), channel_id=1, source_target_pairs={{0,1},{1,0},{2,3},{3,2},{4,5},{5,4},{6,7},{7,6},{8,9},{9,8},{10,11... | collective-permute-start | bytes 1572872 | tf_op jit(solution)/shard_map/ppermute | solution.py:29
  135.1 12.4 %all-to-all-start.4 = ((bf16[8,32,256]{2,1,0:T(8,128)(2,1)}), bf16[8,32,256]{2,1,0:T(8,128)(2,1)S(1)}, u32[]{:S(2)}, u32[]{:S(2)}) async-start(bf16[8,32,256]{2,1,0:T(8,128)(2,1)} %bitcast.10), calls=%async_computation.4 | async-start | bytes 262144 | tf_op jit(solution)/shard_map/all_to_all | solution.py:21

commit v2 on v1

v2 whole, which is shorter than its diff:
```python
import functools

import jax
import jax.numpy as jnp
from jax import lax
from jax.experimental import pallas as pl
from jax.experimental.pallas import tpu as pltpu
from jax.sharding import PartitionSpec as P

sharpness_divisor = 2.0
objective_factor = 32.0

NY, NX, NZ = 4, 4, 8
ROWS, FULL, COLS, SLAB = 256, 4096, 1024, 256
f32, bf16 = jnp.float32, jnp.bfloat16
MIB = 1 << 20


def place(y, x, z):
    return ((y % NY) * NX + x % NX) * NZ + z % NZ


class_groups = [
    [place(y, c - 2 * y, z) for y in range(NY) for z in range(NZ)] for c in range(4)
]


def trade(chunks, groups):
    return lax.all_to_all(chunks, "vocab", 0, 0, tiled=True, axis_index_groups=groups)


def step(value, dy, dx):
    pairs = [
        (place(y, x, z), place(y + dy, x + dx, z))
        for y in range(NY)
        for x in range(NX)
        for z in range(NZ)
    ]
    return lax.ppermute(value, "vocab", pairs)


def other_core(value):
    return lax.ppermute(value, "rows", [(0, 1), (1, 0)])


def slab_row(own, offset, j):
    slab = 4 * j + lax.rem(own + offset - 2 * j + 8, 4)
    return pl.multiple_of(slab * SLAB, SLAB)


def call(body, outs, ins, flops, traffic, scratch=(), limit=32):
    smem, vmem, hbm = pltpu.SMEM, pltpu.VMEM, pl.ANY
    spaces = {"s": smem, "v": vmem, "h": hbm}
    return pl.pallas_call(
        body,
        out_shape=[jax.ShapeDtypeStruct(shape, dtype) for shape, dtype in outs],
        in_specs=[pl.BlockSpec(memory_space=spaces[kind]) for kind, _ in ins],
        out_specs=[pl.BlockSpec(memory_space=vmem) for _ in outs],
        scratch_shapes=list(scratch),
        compiler_params=pltpu.CompilerParams(vmem_limit_bytes=limit * MIB),
        cost_estimate=pl.CostEstimate(flops=flops, bytes_accessed=traffic, transcendentals=0),
    )(*[value for _, value in ins])


def target_kernel(mentor, prob, lse):
    target = mentor[...].astype(f32) / sharpness_divisor
    top = jnp.max(target, axis=1, keepdims=True)
    value = top + jnp.log(jnp.sum(jnp.exp(target - top), axis=1, keepdims=True))
    prob[...] = jnp.exp(target - value)
    lse[...] = jnp.broadcast_to(value, lse.shape)


def student_kernel(own, a, b, c, d0, d1, head, mentor, prob, lse_t, student, stats, held, sems):
    pieces = [(0, [a.at[pl.ds(j * SLAB, SLAB)] for j in range(4)])]
    pieces.append((1, [b.at[pl.ds(j * SLAB, SLAB)] for j in range(4)]))
    pieces.append((3, [c.at[pl.ds(j * SLAB, SLAB)] for j in range(4)]))
    pieces.append((2, [d.at[pl.ds(j * SLAB, SLAB)] for d in (d0, d1) for j in range(2)]))
    slabs = [(offset, j, ref) for offset, refs in pieces for j, ref in enumerate(refs)]

    def fetch(k):
        offset, j, _ = slabs[k]
        rows = pl.ds(slab_row(own[0], offset, j), SLAB)
        return pltpu.make_async_copy(head.at[rows], held.at[k], sems.at[k])

    for k in range(16):
        fetch(k).start()
    for k in range(16):
        fetch(k).wait()
        product = lax.dot_general(
            slabs[k][2][...], held[k], (((0,), (0,)), ((), ())), preferred_element_type=f32
        )
        if k == 0:
            student[...] = product
        else:
            student[...] += product
    scores = student[...] / sharpness_divisor
    student[...] = scores
    top = jnp.max(scores, axis=1, keepdims=True)
    lse_s = top + jnp.log(jnp.sum(jnp.exp(scores - top), axis=1, keepdims=True))
    target = mentor[...].astype(f32) / sharpness_divisor
    cross = jnp.sum(prob[...] * (target - scores), axis=1, keepdims=True)
    lane = lax.broadcasted_iota(jnp.int32, (ROWS, 128), 1)
    columns = jnp.where(lane == 0, lse_s, jnp.where(lane == 1, lse_t[...], cross))
    flat = jnp.transpose(columns)
    lines = [flat[i : i + 1, h * 128 : (h + 1) * 128] for i in range(3) for h in range(2)]
    chunk = jnp.concatenate(lines, axis=0)
    stats[...] = jnp.broadcast_to(chunk[None], stats.shape)


def halves_kernel(core, a, b, c, d0, d1, own, mine, theirs):
    pieces = [(0, a, 0, 4), (1, b, 0, 4), (3, c, 0, 4), (2, d0, 0, 2), (2, d1, 2, 2)]
    for offset, ref, first, count in pieces:
        for i in range(count):
            j = first + i
            slab = 4 * (j % 2) + lax.rem(own[0] + offset - 2 * j + 8, 4)
            rows = pl.ds(pl.multiple_of(slab * SLAB, SLAB), SLAB)

            @pl.when(core[0] == j // 2)
            def _(ref=ref, rows=rows, i=i):
                mine[rows] = ref[pl.ds(i * SLAB, SLAB)]

            @pl.when(core[0] != j // 2)
            def _(ref=ref, rows=rows, i=i):
                theirs[rows] = ref[pl.ds(i * SLAB, SLAB)]


def lse_of_shards(parts):
    top = jnp.max(parts, axis=0)
    return top + jnp.log(jnp.sum(jnp.exp(parts - top[None]), axis=0))


def as_column(lines):
    flat = jnp.concatenate([lines[0:1], lines[1:2]], axis=1)
    return jnp.transpose(jnp.broadcast_to(flat, (128, ROWS)))[:, 0:1]


def times_head(held, sems, fetch, score, outs):
    for k, ref in outs:
        fetch(k).wait()
        ref[...] = lax.dot_general(
            held[k], score, (((1,), (1,)), ((), ())), preferred_element_type=f32
        ).astype(ref.dtype)


def fetcher(own, head, held, sems, places):
    def fetch(k):
        offset, j = places[k]
        rows = pl.ds(slab_row(own[0], offset, j), SLAB)
        return pltpu.make_async_copy(head.at[rows], held.at[k], sems.at[k])

    return fetch


def score_kernel(own, student, mentor, stats, head, score, b, c, mismatch, held, sems):
    places = [(1, j) for j in range(4)] + [(3, j) for j in range(4)]
    fetch = fetcher(own, head, held, sems, places)
    for k in range(8):
        fetch(k).start()
    parts = stats[...]
    all_s, all_t = lse_of_shards(parts[:, 0:2]), lse_of_shards(parts[:, 2:4])
    cross = jnp.sum(jnp.exp(parts[:, 2:4] - all_t[None]) * parts[:, 4:6], axis=0)
    mismatch[...] = sharpness_divisor * sharpness_divisor * (cross + all_s - all_t)
    target = mentor[...].astype(f32) / sharpness_divisor
    gap = jnp.exp(student[...] - as_column(all_s)) - jnp.exp(target - as_column(all_t))
    rounded = (objective_factor * sharpness_divisor * gap).astype(bf16)
    score[...] = rounded
    outs = [(k, (b, c)[k // 4].at[pl.ds((k % 4) * SLAB, SLAB)]) for k in range(8)]
    times_head(held, sems, fetch, rounded, outs)


def rest_kernel(own, score, head, d0, d1, a, held, sems):
    places = [(2, j) for j in range(4)] + [(0, j) for j in range(4)]
    fetch = fetcher(own, head, held, sems, places)
    for k in range(8):
        fetch(k).start()
    outs = [(k, (d0, d1)[k // 2].at[pl.ds((k % 2) * SLAB, SLAB)]) for k in range(4)]
    outs += [(4 + j, a.at[pl.ds(j * SLAB, SLAB)]) for j in range(4)]
    times_head(held, sems, fetch, score[...], outs)


def weight_kernel(mine, theirs, score, score_theirs, out):
    total = jnp.dot(mine[...], score[...], preferred_element_type=f32)
    total += jnp.dot(theirs[...], score_theirs[...], preferred_element_type=f32)
    out[...] = total.astype(out.dtype)


def weight_grad_of(mine, theirs, score, score_theirs):
    tile = 256
    rows = pl.BlockSpec((tile, ROWS), lambda i: (i, 0))
    whole = pl.BlockSpec((ROWS, COLS), lambda i: (0, 0))
    return pl.pallas_call(
        weight_kernel,
        grid=(FULL // 2 // tile,),
        out_shape=jax.ShapeDtypeStruct((FULL // 2, COLS), bf16),
        in_specs=[rows, rows, whole, whole],
        out_specs=pl.BlockSpec((tile, COLS), lambda i: (i, 0)),
        compiler_params=pltpu.CompilerParams(vmem_limit_bytes=16 * MIB),
        cost_estimate=pl.CostEstimate(flops=2 * FULL * ROWS * COLS, bytes_accessed=7 * MIB, transcendentals=0),
    )(mine, theirs, score, score_theirs)


def shards(hidden, head_weight, mentor_outputs):
    here = lax.axis_index("vocab")
    core = lax.axis_index("rows").astype(jnp.int32)[None]
    own = lax.rem(here // NZ % NX + 2 * (here // (NZ * NX)), 4).astype(jnp.int32)[None]

    a = trade(jnp.broadcast_to(hidden.T[None], (32, 32, ROWS)), class_groups).reshape(1024, ROWS)
    prob, lse_t = call(
        target_kernel,
        [((ROWS, COLS), f32), ((ROWS, 128), f32)],
        [("v", mentor_outputs)],
        10 * ROWS * COLS,
        2 * MIB,
    )
    b, c = step(a, 0, -1), step(a, 0, 1)
    d0, d1 = step(a[:512], 1, 0), step(a[512:], -1, 0)

    slots = [pltpu.VMEM((16, SLAB, COLS), bf16), pltpu.SemaphoreType.DMA((16,))]
    student, stats = call(
        student_kernel,
        [((ROWS, COLS), f32), ((128, 6, 128), f32)],
        [("s", own), ("v", a), ("v", b), ("v", c), ("v", d0), ("v", d1), ("h", head_weight)]
        + [("v", mentor_outputs), ("v", prob), ("v", lse_t)],
        2 * FULL * ROWS * COLS,
        12 * MIB,
        slots,
    )
    stats = trade(stats, None)
    mine, theirs = call(
        halves_kernel,
        [((FULL // 2, ROWS), bf16)] * 2,
        [("s", core), ("v", a), ("v", b), ("v", c), ("v", d0), ("v", d1), ("s", own)],
        0,
        4 * MIB,
    )
    theirs = other_core(theirs)

    slots = [pltpu.VMEM((8, SLAB, COLS), bf16), pltpu.SemaphoreType.DMA((8,))]
    score, b, c, mismatch = call(
        score_kernel,
        [((ROWS, COLS), bf16), ((1024, ROWS), bf16), ((1024, ROWS), bf16), ((2, 128), f32)],
        [("s", own), ("v", student), ("v", mentor_outputs), ("v", stats), ("h", head_weight)],
        FULL * ROWS * COLS,
        8 * MIB,
        slots,
    )
    b, c = step(b, 0, 1), step(c, 0, -1)
    score_theirs = other_core(score)
    d0, d1, a = call(
        rest_kernel,
        [((512, ROWS), bf16), ((512, ROWS), bf16), ((1024, ROWS), f32)],
        [("s", own), ("v", score), ("h", head_weight)],
        FULL * ROWS * COLS,
        7 * MIB,
        slots,
    )
    d0, d1 = step(d0, 1, 0), step(d1, -1, 0)
    weight_grad = weight_grad_of(mine, theirs, score, score_theirs)
    part = a + b.astype(f32) + c.astype(f32) + jnp.concatenate([d0, d1], axis=0).astype(f32)
    part = trade(part.astype(bf16).reshape(32, 32, ROWS), class_groups)
    hidden_grad = jnp.sum(part.astype(f32), axis=0).astype(bf16).T
    return (hidden_grad, weight_grad, mismatch.reshape(ROWS))


def solution(mesh):
    return jax.shard_map(
        shards,
        mesh=mesh,
        in_specs=(P("rows", "vocab"), P(None, "vocab"), P("rows", "vocab")),
        out_specs=(P("rows", "vocab"), P("rows", "vocab"), P("rows")),
        check_vma=False,
    )
```

time: 151 us -> 132 us (0.87)
  waiting for transfers between devices: 52.8 us -> 14 us
  Pallas kernels: 0 us -> 21.8 us
  blocking collectives: 44.5 us -> 62.1 us
  matrix products: 17.2 us -> 0 us
  other arithmetic: 7.05 us -> 3.06 us
  local copies, waits for them, and re-layouts: 6.9 us -> 9.69 us
    all_to_all x3 -> x1, waiting for transfers between devices: 52.8 us -> 5.54 us  [trade(): lax.all_to_all(chunks, 'vocab', 0, 0, tiled=True, axis_index_groups=groups)]
    pallas_call x0 -> x6, Pallas kernels: none -> 21.8 us  [the longest x5 16.4 us: call(): pl.pallas_call(body, out_shape=[jax.ShapeDtypeStruct(shape, dtype) for sh...]
    all_to_all x2, blocking collectives: 44.5 us -> 62.1 us  [trade(): lax.all_to_all(chunks, 'vocab', 0, 0, tiled=True, axis_index_groups=groups)]
    dot_general x3 -> x0, matrix products: 17.2 us -> none  [the longest x1 5.93 us: shards(): lax.dot_general(head_weight, score, (((1,), (1,)), ((), ())), preferred_e...]
    all_to_all x3 -> x1, starting transfers between devices: 18.4 us -> 6.17 us  [trade(): lax.all_to_all(chunks, 'vocab', 0, 0, tiled=True, axis_index_groups=groups)]
    ppermute x0 -> x8, starting transfers between devices: none -> 12.2 us  [step(): return lax.ppermute(value, 'vocab', pairs)]
    unnamed x4 -> x18, local copies, waits for them, and re-layouts: 0.01 us -> 8.89 us
    ppermute x0 -> x8, waiting for transfers between devices: none -> 7.32 us  [step(): return lax.ppermute(value, 'vocab', pairs)]
  transfers between devices with their start and end apart: 5 -> 11, of which waited for: 3 -> 5; matrix products, arithmetic and copies ran while one was open for 7% -> 2% of each run, Pallas kernels for 0% -> 9%
where the time goes in v2:
time: 132 us; the launch traced here: 130 us
  blocking collectives  62.1 us (47%)
  Pallas kernels  21.8 us (17%)
  starting transfers between devices  18.4 us (14%)
  waiting for transfers between devices  14 us (11%)
  local copies, waits for them, and re-layouts  9.69 us (7%)
  other arithmetic  3.06 us (2%)
    all_to_all x2, blocking collectives, trade(): lax.all_to_all(chunks, 'vocab', 0, 0, tiled=True, axis_index_groups=groups)  62.1 us
    pallas_call x5, Pallas kernels, call(): pl.pallas_call(body, out_shape=[jax.ShapeDtypeStruct(shape, dtype) for sh...  16.4 us
    ppermute x8, starting transfers between devices, step(): return lax.ppermute(value, 'vocab', pairs)  12.2 us
    unnamed x18, local copies, waits for them, and re-layouts  8.89 us
    ppermute x8, waiting for transfers between devices, step(): return lax.ppermute(value, 'vocab', pairs)  7.32 us
    all_to_all x1, starting transfers between devices, trade(): lax.all_to_all(chunks, 'vocab', 0, 0, tiled=True, axis_index_groups=groups)  6.17 us
    all_to_all x1, waiting for transfers between devices, trade(): lax.all_to_all(chunks, 'vocab', 0, 0, tiled=True, axis_index_groups=groups)  5.54 us
    pallas_call x1, Pallas kernels, weight_grad_of(): pl.pallas_call(weight_kernel, grid=(FULL // 2 // tile,), out_shape=jax.Sh...  5.38 us
  transfers between devices with their start and end apart: 11, of which 5 were waited for; matrix products, arithmetic and copies ran while one was open for 2% of the time, Pallas kernels for 9%

profile of v2, /device:TPU:2, one launch (start us, length us, event | category | flops | bytes accessed | tf_op | source)
XLA Modules:
  0.0 129.8 jit_solution(7335265616732896911)
XLA Ops:
  0.6 0.8 broadcast_in_dim.13
  1.4 31.9 %all_to_all.15 = bf16[32,32,256]{2,1,0:T(8,128)(2,1)S(1)} all-to-all(bf16[32,32,256]{2,1,0:T(8,128)(2,1)S(1)} %broadcast_in_dim.13), channel_id=1, replica_groups={{0,2,4,6,8,10,12,14,96,98,100,102,104,106,108,110,128,130,132,134,136,1..., dimensions={0} | all-to-all | bytes 1048576 | tf_op jit(solution)/shard_map/all_to_all | solution.py:29
  33.3 0.1 collective-permute-start.1
  33.4 1.9 %collective-permute-start = (bf16[1024,256]{1,0:T(8,128)(2,1)S(1)}, bf16[1024,256]{1,0:T(8,128)(2,1)S(1)}, u32[]{:S(2)}, u32[]{:S(2)}) collective-permute-start(bf16[1024,256]{1,0:T(8,128)(2,1)S(1)} %bitcast.10), channel_id=1, source_target_pairs={{0,48},{2,50},{4,52},{6,54},{8,56},{10,58},{12,60},{14,62},{16,0},... | collective-permute-start | bytes 1572872 | tf_op jit(solution)/shard_map/ppermute | solution.py:39
  35.4 0.1 collective-permute-start.2
  35.5 3.2 %collective-permute-start.3 = (bf16[512,256]{1,0:T(8,128)(2,1)S(1)}, bf16[512,256]{1,0:T(8,128)(2,1)S(1)}, u32[]{:S(2)}, u32[]{:S(2)}) collective-permute-start(bf16[512,256]{1,0:T(8,128)(2,1)S(1)} %bitcast.13), channel_id=1, source_target_pairs={{0,192},{2,194},{4,196},{6,198},{8,200},{10,202},{12,204},{14,206}... | collective-permute-start | bytes 786440 | tf_op jit(solution)/shard_map/ppermute | solution.py:39
  38.7 0.0 copy-start.2
  38.7 1.0 copy-done.2
  39.8 0.4 shard_map.58
  40.2 2.9 %collective-permute-done.2.d0 = bf16[512,256]{1,0:T(8,128)(2,1)S(1)} collective-permute-done((bf16[512,256]{1,0:T(8,128)(2,1)S(1)}, bf16[512,256]{1,0:T(8,128)(2,1)S(1)}, u32[]{:S(2)}, u32[]{:S(2)}) %collective-permute-start.2) | collective-permute-done | bytes 262176 | tf_op jit(solution)/shard_map/ppermute | solution.py:39
  43.1 0.0 collective-permute-done.3.d1
  43.1 1.1 collective-permute-done.1.c
  44.2 0.0 collective-permute-done.b
  44.2 0.0 copy-start
  44.2 3.4 %copy-done = bf16[4096,1024]{1,0:T(8,128)(2,1)S(1)} copy-done((bf16[4096,1024]{1,0:T(8,128)(2,1)S(1)}, bf16[4096,1024]{1,0:T(8,128)(2,1)}, u32[]{:S(2)}) %copy-start) | copy-done | bytes 8388632
  47.6 0.0 copy-start.1
  47.6 4.7 %shard_map.59 = (f32[256,1024]{1,0:T(8,128)S(1)}, f32[128,6,128]{2,1,0:T(8,128)S(1)}) custom-call(s32[1]{0:T(128)} %bitcast.own, bf16[1024,256]{1,0:T(8,128)(2,1)S(1)} %bitcast.11, bf16[1024,256]{1,0:T(8,128)(2,1)S(1)} %collective-permute-done.b, bf16[1024,256]{1,0:T(8,128)(2,1)S(1)} %collective-permute-done.1.c, ...), custom_call_target="tpu_custom_call" | custom-call | flops 2147483648 | bytes 12582912 | tf_op jit(solution)/shard_map/pallas_call | solution.py:54
  52.2 30.2 %all_to_all.16.stats = f32[128,6,128]{2,1,0:T(8,128)S(1)} all-to-all(f32[128,6,128]{2,1,0:T(8,128)S(1)} %get-tuple-element.19), channel_id=1, replica_groups=mesh['vocab'=128,'rows'=2] {'vocab'}, dimensions={0} | all-to-all | bytes 786432 | tf_op jit(solution)/shard_map/all_to_all | solution.py:29
  82.4 0.0 copy-done.1
  82.5 5.7 %shard_map.60 = (bf16[256,1024]{1,0:T(8,128)(2,1)S(1)}, bf16[1024,256]{1,0:T(8,128)(2,1)}, bf16[1024,256]{1,0:T(8,128)(2,1)}, f32[2,128]{1,0:T(2,128)}) custom-call(s32[1]{0:T(128)} %bitcast.own, f32[256,1024]{1,0:T(8,128)S(1)} %get-tuple-element.18.student, bf16[256,1024]{1,0:T(8,128)(2,1)S(1)} %copy-done.2, f32[128,6,128]{2,1,0:T(8,128)S(1)} %all_to_all.16.stats, ...), custom_call_target="tpu_custom_call" | custom-call | flops 1073741824 | bytes 8388608 | tf_op jit(solution)/shard_map/pallas_call | solution.py:54
  88.1 0.0 copy-start.3
  88.1 1.5 %collective-permute-start.4 = (bf16[1024,256]{1,0:T(8,128)(2,1)}, bf16[1024,256]{1,0:T(8,128)(2,1)}, u32[]{:S(2)}, u32[]{:S(2)}) collective-permute-start(bf16[1024,256]{1,0:T(8,128)(2,1)} %get-tuple-element.22), channel_id=1, source_target_pairs={{0,16},{2,18},{4,20},{6,22},{8,24},{10,26},{12,28},{14,30},{16,32}... | collective-permute-start | bytes 1572872 | tf_op jit(solution)/shard_map/ppermute | solution.py:39
  89.6 2.0 %collective-permute-start.5 = (bf16[1024,256]{1,0:T(8,128)(2,1)}, bf16[1024,256]{1,0:T(8,128)(2,1)}, u32[]{:S(2)}, u32[]{:S(2)}) collective-permute-start(bf16[1024,256]{1,0:T(8,128)(2,1)} %get-tuple-element.23), channel_id=1, source_target_pairs={{0,48},{2,50},{4,52},{6,54},{8,56},{10,58},{12,60},{14,62},{16,0},... | collective-permute-start | bytes 1572872 | tf_op jit(solution)/shard_map/ppermute | solution.py:39
  91.7 4.3 %shard_map.61 = (bf16[512,256]{1,0:T(8,128)(2,1)}, bf16[512,256]{1,0:T(8,128)(2,1)S(1)}, f32[1024,256]{1,0:T(8,128)S(1)}) custom-call(s32[1]{0:T(128)} %bitcast.own, bf16[256,1024]{1,0:T(8,128)(2,1)S(1)} %get-tuple-element.20.score, bf16[4096,1024]{1,0:T(8,128)(2,1)S(1)} %copy-done.1), custom_call_target="tpu_custom_call" | custom-call | flops 1073741824 | bytes 7340032 | tf_op jit(solution)/shard_map/pallas_call | solution.py:54
  96.0 0.0 copy-done.3
  96.0 0.1 collective-permute-start.6
  96.1 3.2 %collective-permute-start.7 = (bf16[512,256]{1,0:T(8,128)(2,1)S(1)}, bf16[512,256]{1,0:T(8,128)(2,1)}, u32[]{:S(2)}, u32[]{:S(2)}) collective-permute-start(bf16[512,256]{1,0:T(8,128)(2,1)S(1)} %get-tuple-element.25), channel_id=1, source_target_pairs={{0,192},{2,194},{4,196},{6,198},{8,200},{10,202},{12,204},{14,206}... | collective-permute-start | bytes 786440 | tf_op jit(solution)/shard_map/ppermute | solution.py:39
  99.3 1.3 %shard_map.62 = (bf16[2048,256]{1,0:T(8,128)(2,1)S(1)}, bf16[2048,256]{1,0:T(8,128)(2,1)}) custom-call(s32[1]{0:T(128)} %bitcast.7.core, bf16[1024,256]{1,0:T(8,128)(2,1)S(1)} %bitcast.12, bf16[1024,256]{1,0:T(8,128)(2,1)S(1)} %collective-permute-done.b, bf16[1024,256]{1,0:T(8,128)(2,1)S(1)} %collective-permute-done.1.c, ...), custom_call_target="tpu_custom_call" | custom-call | bytes 4194304 | tf_op jit(solution)/shard_map/pallas_call | solution.py:54
  100.7 0.0 copy-start.5
  100.7 0.0 collective-permute-start.8
  100.7 3.3 %collective-permute-done.6 = bf16[512,256]{1,0:T(8,128)(2,1)} collective-permute-done((bf16[512,256]{1,0:T(8,128)(2,1)}, bf16[512,256]{1,0:T(8,128)(2,1)}, u32[]{:S(2)}, u32[]{:S(2)}) %collective-permute-start.6) | collective-permute-done | bytes 262176 | tf_op jit(solution)/shard_map/ppermute | solution.py:39
  104.0 0.0 collective-permute-done.7
  104.0 0.0 collective-permute-done.4
  104.0 0.0 collective-permute-done.5
  104.0 2.4 %add_convert_fusion = bf16[1024,256]{1,0:T(8,128)(2,1)} fusion(bf16[1024,256]{1,0:T(8,128)(2,1)} %collective-permute-done.5, f32[1024,256]{1,0:T(8,128)S(1)} %get-tuple-element.21, bf16[1024,256]{1,0:T(8,128)(2,1)} %collective-permute-done.4, bf16[512,256]{1,0:T(8,128)(2,1)} %collective-permute-done.7, bf16[512,256]{1,0:T(8,128)(2,1)} %collective-permute-done.6), kind=kLoop, calls=%fused_computation | loop fusion | flops 2621440 | bytes 3145728 | tf_op jit(solution)/shard_map/convert_element_type | solution.py:260
  106.4 0.0 copy-done.5
  106.4 6.2 %all-to-all-start.2 = ((bf16[32,32,256]{2,1,0:T(8,128)(2,1)}), bf16[32,32,256]{2,1,0:T(8,128)(2,1)S(1)}, u32[]{:S(2)}, u32[]{:S(2)}) async-start(bf16[32,32,256]{2,1,0:T(8,128)(2,1)} %bitcast.5), calls=%async_computation.2 | async-start | bytes 1048576 | tf_op jit(solution)/shard_map/all_to_all | solution.py:29
  112.5 0.1 collective-permute-start.9
  112.6 0.0 collective-permute-done.8.theirs
  112.6 0.0 copy-start.7
  112.7 1.0 copy-done.7
  113.6 1.1 collective-permute-done.9.score_theirs
  114.7 0.0 copy-start.4
  114.7 1.0 copy-done.4
  115.8 0.0 copy-start.6
  115.8 1.2 copy-done.6
  117.0 0.0 copy-start.8
  117.0 1.2 copy-done.8
  118.2 5.4 %shard_map.63 = bf16[2048,1024]{1,0:T(8,128)(2,1)} custom-call(bf16[2048,256]{1,0:T(8,128)(2,1)S(1)} %copy-done.6, bf16[2048,256]{1,0:T(8,128)(2,1)S(1)} %copy-done.8, bf16[256,1024]{1,0:T(8,128)(2,1)S(1)} %copy-done.4, bf16[256,1024]{1,0:T(8,128)(2,1)S(1)} %collective-permute-done.9.score_theirs), custom_call_target="tpu_custom_call" | custom-call | flops 2147483648 | bytes 7340032 | tf_op jit(solution)/shard_map/pallas_call | solution.py:191
  123.6 5.5 %all-to-all-done.2 = bf16[32,32,256]{2,1,0:T(8,128)(2,1)S(1)} async-done(((bf16[32,32,256]{2,1,0:T(8,128)(2,1)}), bf16[32,32,256]{2,1,0:T(8,128)(2,1)S(1)}, u32[]{:S(2)}, u32[]{:S(2)}) %all-to-all-start.2) | async-done | bytes 524320 | tf_op jit(solution)/shard_map/all_to_all | solution.py:29
  129.2 0.7 reduce_sum.12
  (1 shorter events, 0.0 us)
Async XLA Ops:
  33.3 10.8 %collective-permute-start.1 = (bf16[1024,256]{1,0:T(8,128)(2,1)S(1)}, bf16[1024,256]{1,0:T(8,128)(2,1)S(1)}, u32[]{:S(2)}, u32[]{:S(2)}) collective-permute-start(bf16[1024,256]{1,0:T(8,128)(2,1)S(1)} %bitcast.9), channel_id=1, source_target_pairs={{0,16},{2,18},{4,20},{6,22},{8,24},{10,26},{12,28},{14,30},{16,32}... | collective-permute-start | bytes 1572872 | tf_op jit(solution)/shard_map/ppermute | solution.py:39
  33.4 10.7 %collective-permute-start = (bf16[1024,256]{1,0:T(8,128)(2,1)S(1)}, bf16[1024,256]{1,0:T(8,128)(2,1)S(1)}, u32[]{:S(2)}, u32[]{:S(2)}) collective-permute-start(bf16[1024,256]{1,0:T(8,128)(2,1)S(1)} %bitcast.10), channel_id=1, source_target_pairs={{0,48},{2,50},{4,52},{6,54},{8,56},{10,58},{12,60},{14,62},{16,0},... | collective-permute-start | bytes 1572872 | tf_op jit(solution)/shard_map/ppermute | solution.py:39
  35.4 7.7 %collective-permute-start.2 = (bf16[512,256]{1,0:T(8,128)(2,1)S(1)}, bf16[512,256]{1,0:T(8,128)(2,1)S(1)}, u32[]{:S(2)}, u32[]{:S(2)}) collective-permute-start(bf16[512,256]{1,0:T(8,128)(2,1)S(1)} %bitcast.14), channel_id=1, source_target_pairs={{0,64},{2,66},{4,68},{6,70},{8,72},{10,74},{12,76},{14,78},{16,80}... | collective-permute-start | bytes 786440 | tf_op jit(solution)/shard_map/ppermute | solution.py:39
  35.5 7.6 %collective-permute-start.3 = (bf16[512,256]{1,0:T(8,128)(2,1)S(1)}, bf16[512,256]{1,0:T(8,128)(2,1)S(1)}, u32[]{:S(2)}, u32[]{:S(2)}) collective-permute-start(bf16[512,256]{1,0:T(8,128)(2,1)S(1)} %bitcast.13), channel_id=1, source_target_pairs={{0,192},{2,194},{4,196},{6,198},{8,200},{10,202},{12,204},{14,206}... | collective-permute-start | bytes 786440 | tf_op jit(solution)/shard_map/ppermute | solution.py:39
  38.7 1.0 copy-start.2
  44.2 3.4 %copy-start = (bf16[4096,1024]{1,0:T(8,128)(2,1)S(1)}, bf16[4096,1024]{1,0:T(8,128)(2,1)}, u32[]{:S(2)}) copy-start(bf16[4096,1024]{1,0:T(8,128)(2,1)} %head.5) | copy-start | bytes 25165828
  47.6 34.9 %copy-start.1 = (bf16[4096,1024]{1,0:T(8,128)(2,1)S(1)}, bf16[4096,1024]{1,0:T(8,128)(2,1)}, u32[]{:S(2)}) copy-start(bf16[4096,1024]{1,0:T(8,128)(2,1)} %head.5) | copy-start | bytes 25165828
  88.1 7.9 %copy-start.3 = (bf16[256,1024]{1,0:T(8,128)(2,1)}, bf16[256,1024]{1,0:T(8,128)(2,1)S(1)}, u32[]{:S(2)}) copy-start(bf16[256,1024]{1,0:T(8,128)(2,1)S(1)} %get-tuple-element.20.score) | copy-start | bytes 1572868
  88.1 15.9 %collective-permute-start.4 = (bf16[1024,256]{1,0:T(8,128)(2,1)}, bf16[1024,256]{1,0:T(8,128)(2,1)}, u32[]{:S(2)}, u32[]{:S(2)}) collective-permute-start(bf16[1024,256]{1,0:T(8,128)(2,1)} %get-tuple-element.22), channel_id=1, source_target_pairs={{0,16},{2,18},{4,20},{6,22},{8,24},{10,26},{12,28},{14,30},{16,32}... | collective-permute-start | bytes 1572872 | tf_op jit(solution)/shard_map/ppermute | solution.py:39
  89.6 14.4 %collective-permute-start.5 = (bf16[1024,256]{1,0:T(8,128)(2,1)}, bf16[1024,256]{1,0:T(8,128)(2,1)}, u32[]{:S(2)}, u32[]{:S(2)}) collective-permute-start(bf16[1024,256]{1,0:T(8,128)(2,1)} %get-tuple-element.23), channel_id=1, source_target_pairs={{0,48},{2,50},{4,52},{6,54},{8,56},{10,58},{12,60},{14,62},{16,0},... | collective-permute-start | bytes 1572872 | tf_op jit(solution)/shard_map/ppermute | solution.py:39
  96.0 8.0 %collective-permute-start.6 = (bf16[512,256]{1,0:T(8,128)(2,1)}, bf16[512,256]{1,0:T(8,128)(2,1)}, u32[]{:S(2)}, u32[]{:S(2)}) collective-permute-start(bf16[512,256]{1,0:T(8,128)(2,1)} %get-tuple-element.24), channel_id=1, source_target_pairs={{0,64},{2,66},{4,68},{6,70},{8,72},{10,74},{12,76},{14,78},{16,80}... | collective-permute-start | bytes 786440 | tf_op jit(solution)/shard_map/ppermute | solution.py:39
  96.1 7.9 %collective-permute-start.7 = (bf16[512,256]{1,0:T(8,128)(2,1)S(1)}, bf16[512,256]{1,0:T(8,128)(2,1)}, u32[]{:S(2)}, u32[]{:S(2)}) collective-permute-start(bf16[512,256]{1,0:T(8,128)(2,1)S(1)} %get-tuple-element.25), channel_id=1, source_target_pairs={{0,192},{2,194},{4,196},{6,198},{8,200},{10,202},{12,204},{14,206}... | collective-permute-start | bytes 786440 | tf_op jit(solution)/shard_map/ppermute | solution.py:39
  100.7 5.7 %copy-start.5 = (bf16[2048,256]{1,0:T(8,128)(2,1)}, bf16[2048,256]{1,0:T(8,128)(2,1)S(1)}, u32[]{:S(2)}) copy-start(bf16[2048,256]{1,0:T(8,128)(2,1)S(1)} %get-tuple-element.26.mine) | copy-start | bytes 3145732
  100.7 12.0 %collective-permute-start.8 = (bf16[2048,256]{1,0:T(8,128)(2,1)}, bf16[2048,256]{1,0:T(8,128)(2,1)S(1)}, u32[]{:S(2)}, u32[]{:S(2)}) collective-permute-start(bf16[2048,256]{1,0:T(8,128)(2,1)} %get-tuple-element.27), channel_id=1, source_target_pairs={{0,1},{1,0},{2,3},{3,2},{4,5},{5,4},{6,7},{7,6},{8,9},{9,8},{10,11... | collective-permute-start | bytes 3145736 | tf_op jit(solution)/shard_map/ppermute | solution.py:43
  106.4 22.8 %all-to-all-start.2 = ((bf16[32,32,256]{2,1,0:T(8,128)(2,1)}), bf16[32,32,256]{2,1,0:T(8,128)(2,1)S(1)}, u32[]{:S(2)}, u32[]{:S(2)}) async-start(bf16[32,32,256]{2,1,0:T(8,128)(2,1)} %bitcast.5), calls=%async_computation.2 | async-start | bytes 1048576 | tf_op jit(solution)/shard_map/all_to_all | solution.py:29
  112.5 2.2 %collective-permute-start.9 = (bf16[256,1024]{1,0:T(8,128)(2,1)}, bf16[256,1024]{1,0:T(8,128)(2,1)S(1)}, u32[]{:S(2)}, u32[]{:S(2)}) collective-permute-start(bf16[256,1024]{1,0:T(8,128)(2,1)} %copy-done.3), channel_id=1, source_target_pairs={{0,1},{1,0},{2,3},{3,2},{4,5},{5,4},{6,7},{7,6},{8,9},{9,8},{10,11... | collective-permute-start | bytes 1572872 | tf_op jit(solution)/shard_map/ppermute | solution.py:43
  112.6 1.0 copy-start.7
  114.7 1.0 copy-start.4
  115.8 1.2 copy-start.6
  117.0 1.2 copy-start.8

commit v3 on v2

v3 whole, which is shorter than its diff:
```python
import jax
import jax.numpy as jnp
from jax import lax
from jax.experimental import pallas as pl
from jax.experimental.pallas import tpu as pltpu
from jax.sharding import PartitionSpec as P

sharpness_divisor = 2.0
objective_factor = 32.0

NY, NX, NZ = 4, 4, 8
ROWS, FULL, COLS, SLAB = 256, 4096, 1024, 256
f32, bf16 = jnp.float32, jnp.bfloat16
MIB = 1 << 20


def place(y, x, z):
    return ((y % NY) * NX + x % NX) * NZ + z % NZ


class_groups = [
    [place(y, c - 2 * y, z) for y in range(NY) for z in range(NZ)] for c in range(4)
]


def trade(chunks, groups):
    return lax.all_to_all(chunks, "vocab", 0, 0, tiled=True, axis_index_groups=groups)


def step(value, dy, dx):
    pairs = [
        (place(y, x, z), place(y + dy, x + dx, z))
        for y in range(NY)
        for x in range(NX)
        for z in range(NZ)
    ]
    return lax.ppermute(value, "vocab", pairs)


def other_core(value):
    return lax.ppermute(value, "rows", [(0, 1), (1, 0)])


def slab_row(own, offset, j):
    slab = 4 * j + lax.rem(own + offset - 2 * j + 8, 4)
    return pl.multiple_of(slab * SLAB, SLAB)


def call(body, outs, ins, flops, traffic, scratch=(), limit=8):
    smem, vmem, hbm = pltpu.SMEM, pltpu.VMEM, pltpu.HBM
    spaces = {"s": smem, "v": vmem, "h": hbm}
    return pl.pallas_call(
        body,
        out_shape=[jax.ShapeDtypeStruct(shape, dtype) for shape, dtype in outs],
        in_specs=[pl.BlockSpec(memory_space=spaces[kind]) for kind, _ in ins],
        out_specs=[pl.BlockSpec(memory_space=vmem) for _ in outs],
        scratch_shapes=list(scratch),
        compiler_params=pltpu.CompilerParams(vmem_limit_bytes=limit * MIB),
        cost_estimate=pl.CostEstimate(flops=flops, bytes_accessed=traffic, transcendentals=0),
    )(*[value for _, value in ins])


def target_kernel(mentor, head, prob, lse):
    target = mentor[...].astype(f32) / sharpness_divisor
    top = jnp.max(target, axis=1, keepdims=True)
    value = top + jnp.log(jnp.sum(jnp.exp(target - top), axis=1, keepdims=True))
    prob[...] = jnp.exp(target - value)
    lse[...] = jnp.broadcast_to(value, lse.shape)


def student_kernel(
    own, core, a, b, c, d0, d1, head, mentor, prob, lse_t, student, stats, mine, theirs
):
    for offset, ref, first, count in [(0, a, 0, 4), (1, b, 0, 4), (3, c, 0, 4), (2, d0, 0, 2), (2, d1, 2, 2)]:
        for i in range(count):
            j = first + i
            slab = 4 * (j % 2) + lax.rem(own[0] + offset - 2 * j + 8, 4)
            rows = pl.ds(pl.multiple_of(slab * SLAB, SLAB), SLAB)

            @pl.when(core[0] == j // 2)
            def _(ref=ref, rows=rows, i=i):
                mine[rows] = ref[pl.ds(i * SLAB, SLAB)]

            @pl.when(core[0] != j // 2)
            def _(ref=ref, rows=rows, i=i):
                theirs[rows] = ref[pl.ds(i * SLAB, SLAB)]

    half = FULL // 2

    def product(part, which):
        rows = pl.ds(pl.multiple_of(which * half, half), half)
        return lax.dot_general(
            part[...], head[rows], (((0,), (0,)), ((), ())), preferred_element_type=f32
        )

    scores = (product(mine, core[0]) + product(theirs, 1 - core[0])) / sharpness_divisor
    student[...] = scores
    top = jnp.max(scores, axis=1, keepdims=True)
    lse_s = top + jnp.log(jnp.sum(jnp.exp(scores - top), axis=1, keepdims=True))
    target = mentor[...].astype(f32) / sharpness_divisor
    cross = jnp.sum(prob[...] * (target - scores), axis=1, keepdims=True)
    lane = lax.broadcasted_iota(jnp.int32, (ROWS, 128), 1)
    columns = jnp.where(lane == 0, lse_s, jnp.where(lane == 1, lse_t[...], cross))
    flat = jnp.transpose(columns)
    lines = [flat[i : i + 1, h * 128 : (h + 1) * 128] for i in range(3) for h in range(2)]
    chunk = jnp.concatenate(lines, axis=0)
    stats[...] = jnp.broadcast_to(chunk[None], stats.shape)


def as_column(lines):
    flat = jnp.concatenate([lines[0:1], lines[1:2]], axis=1)
    return jnp.transpose(jnp.broadcast_to(flat, (128, ROWS)))[:, 0:1]


def times_head(own, head, score_t, outs):
    for offset, j, ref in outs:
        rows = pl.ds(slab_row(own[0], offset, j), SLAB)
        ref[...] = jnp.dot(head[rows], score_t, preferred_element_type=f32).astype(ref.dtype)


def score_kernel(own, student, mentor, stats, head, score, score_t, b, c, mismatch):
    parts = stats[...]
    top = jnp.max(parts, axis=0)
    weight = jnp.exp(parts - top[None])
    total = jnp.sum(weight, axis=0)
    lse = top + jnp.log(total)
    all_s, all_t = lse[0:2], lse[2:4]
    cross = jnp.sum(weight[:, 2:4] * parts[:, 4:6], axis=0) / total[2:4]
    mismatch[...] = sharpness_divisor * sharpness_divisor * (cross + all_s - all_t)
    target = mentor[...].astype(f32) / sharpness_divisor
    gap = jnp.exp(student[...] - as_column(all_s)) - jnp.exp(target - as_column(all_t))
    rounded = (objective_factor * sharpness_divisor * gap).astype(bf16)
    score[...] = rounded
    score_t[...] = jnp.transpose(rounded)
    outs = [(o, j, r.at[pl.ds(j * SLAB, SLAB)]) for o, r in ((1, b), (3, c)) for j in range(4)]
    times_head(own, head, score_t[...], outs)


def rest_kernel(own, score_t, head, d0, d1, a):
    outs = [(2, j, (d0, d1)[j // 2].at[pl.ds((j % 2) * SLAB, SLAB)]) for j in range(4)]
    outs += [(0, j, a.at[pl.ds(j * SLAB, SLAB)]) for j in range(4)]
    times_head(own, head, score_t[...], outs)


def weight_kernel(mine, theirs, score, score_theirs, out):
    total = jnp.dot(mine[...], score[...], preferred_element_type=f32)
    total += jnp.dot(theirs[...], score_theirs[...], preferred_element_type=f32)
    out[...] = total.astype(out.dtype)


def weight_grad_of(mine, theirs, score, score_theirs):
    tile = 256
    rows = pl.BlockSpec((tile, ROWS), lambda i: (i, 0))
    whole = pl.BlockSpec((ROWS, COLS), lambda i: (0, 0))
    return pl.pallas_call(
        weight_kernel,
        grid=(FULL // 2 // tile,),
        out_shape=jax.ShapeDtypeStruct((FULL // 2, COLS), bf16),
        in_specs=[rows, rows, whole, whole],
        out_specs=pl.BlockSpec((tile, COLS), lambda i: (i, 0)),
        compiler_params=pltpu.CompilerParams(vmem_limit_bytes=8 * MIB),
        cost_estimate=pl.CostEstimate(flops=2 * FULL * ROWS * COLS, bytes_accessed=7 * MIB, transcendentals=0),
    )(mine, theirs, score, score_theirs)


def shards(hidden, head_weight, mentor_outputs):
    here = lax.axis_index("vocab")
    core = lax.axis_index("rows").astype(jnp.int32)[None]
    own = lax.rem(here // NZ % NX + 2 * (here // (NZ * NX)), 4).astype(jnp.int32)[None]

    a = trade(jnp.broadcast_to(hidden.T[None], (32, 32, ROWS)), class_groups).reshape(1024, ROWS)
    prob, lse_t = call(
        target_kernel,
        [((ROWS, COLS), f32), ((ROWS, 128), f32)],
        [("v", mentor_outputs), ("v", head_weight)],
        10 * ROWS * COLS,
        2 * MIB,
    )
    b, c = step(a, 0, -1), step(a, 0, 1)
    d0, d1 = step(a[:512], 1, 0), step(a[512:], -1, 0)

    student, stats, mine, theirs = call(
        student_kernel,
        [((ROWS, COLS), f32), ((128, 6, 128), f32)] + [((FULL // 2, ROWS), bf16)] * 2,
        [("s", own), ("s", core), ("v", a), ("v", b), ("v", c), ("v", d0), ("v", d1), ("v", head_weight)]
        + [("v", mentor_outputs), ("v", prob), ("v", lse_t)],
        2 * FULL * ROWS * COLS,
        12 * MIB,
    )
    stats, theirs = lax.optimization_barrier((trade(stats, None), theirs))
    theirs = other_core(theirs)

    score, score_t, b, c, mismatch = call(
        score_kernel,
        [((ROWS, COLS), bf16), ((COLS, ROWS), bf16)] + [((1024, ROWS), bf16)] * 2 + [((2, 128), f32)],
        [("s", own), ("v", student), ("v", mentor_outputs), ("v", stats), ("v", head_weight)],
        FULL * ROWS * COLS,
        8 * MIB,
    )
    b, c = step(b, 0, 1), step(c, 0, -1)
    score_theirs = other_core(score)
    d0, d1, a = call(
        rest_kernel,
        [((512, ROWS), bf16), ((512, ROWS), bf16), ((1024, ROWS), f32)],
        [("s", own), ("v", score_t), ("v", head_weight)],
        FULL * ROWS * COLS,
        7 * MIB,
    )
    d0, d1 = step(d0, 1, 0), step(d1, -1, 0)
    weight_grad = weight_grad_of(mine, theirs, score, score_theirs)
    b, c, d0, d1, weight_grad = lax.optimization_barrier((b, c, d0, d1, weight_grad))
    part = a + b.astype(f32) + c.astype(f32) + jnp.concatenate([d0, d1], axis=0).astype(f32)
    part = trade(part.astype(bf16).reshape(32, 32, ROWS), class_groups)
    hidden_grad = jnp.sum(part.astype(f32), axis=0).astype(bf16).T
    return (hidden_grad, weight_grad, mismatch.reshape(ROWS))


def solution(mesh):
    return jax.shard_map(
        shards,
        mesh=mesh,
        in_specs=(P("rows", "vocab"), P(None, "vocab"), P("rows", "vocab")),
        out_specs=(P("rows", "vocab"), P("rows", "vocab"), P("rows")),
        check_vma=False,
    )
```

time: 132 us -> 121 us (0.917); the launches traced: 130 us -> 121 us
  blocking collectives: 62.1 us -> 84.7 us
  waiting for transfers between devices: 14 us -> 3.88 us
  Pallas kernels: 21.8 us -> 12.8 us
  starting transfers between devices: 18.4 us -> 12.3 us
  local copies, waits for them, and re-layouts: 9.69 us -> 5.23 us
  other arithmetic: 3.06 us -> 0.98 us
    all_to_all x2 -> x3, blocking collectives: 62.1 us -> 84.7 us  [trade(): lax.all_to_all(chunks, 'vocab', 0, 0, tiled=True, axis_index_groups=groups)]
    pallas_call x5 -> x4, Pallas kernels: 16.4 us -> 7.45 us  [call(): pl.pallas_call(body, out_shape=[jax.ShapeDtypeStruct(shape, dtype) for sh...]
    all_to_all x1 -> x0, starting transfers between devices: 6.17 us -> none  [trade(): lax.all_to_all(chunks, 'vocab', 0, 0, tiled=True, axis_index_groups=groups)]
    all_to_all x1 -> x0, waiting for transfers between devices: 5.54 us -> none  [trade(): lax.all_to_all(chunks, 'vocab', 0, 0, tiled=True, axis_index_groups=groups)]
    unnamed x18 -> x8, local copies, waits for them, and re-layouts: 8.89 us -> 4.43 us
    ppermute x8, waiting for transfers between devices: 7.32 us -> 3.88 us  [step(): return lax.ppermute(value, 'vocab', pairs)]
    convert_element_type x1, other arithmetic: 2.37 us -> 0.29 us  [shards(): part = trade(part.astype(bf16).reshape(32, 32, ROWS), class_groups)]
  transfers between devices with their start and end apart: 11 -> 10, of which waited for: 5 -> 4; matrix products, arithmetic and copies ran while one was open for 2% -> 0% of each run, Pallas kernels for 9% -> 8%
where the time goes in v3:
time: 121 us
  blocking collectives  84.7 us (70%)
  Pallas kernels  12.8 us (11%)
  starting transfers between devices  12.3 us (10%)
  local copies, waits for them, and re-layouts  5.23 us (4%)
  waiting for transfers between devices  3.88 us (3%)
    all_to_all x3, blocking collectives, trade(): lax.all_to_all(chunks, 'vocab', 0, 0, tiled=True, axis_index_groups=groups)  84.7 us
    ppermute x8, starting transfers between devices, step(): return lax.ppermute(value, 'vocab', pairs)  11.8 us
    pallas_call x4, Pallas kernels, call(): pl.pallas_call(body, out_shape=[jax.ShapeDtypeStruct(shape, dtype) for sh...  7.45 us
    pallas_call x1, Pallas kernels, weight_grad_of(): pl.pallas_call(weight_kernel, grid=(FULL // 2 // tile,), out_shape=jax.Sh...  5.38 us
    unnamed x8, local copies, waits for them, and re-layouts  4.43 us
    ppermute x8, waiting for transfers between devices, step(): return lax.ppermute(value, 'vocab', pairs)  3.88 us
  transfers between devices with their start and end apart: 10, of which 4 were waited for; matrix products, arithmetic and copies ran while one was open for 0% of the time, Pallas kernels for 8%

profile of v3, /device:TPU:2, one launch (start us, length us, event | category | flops | bytes accessed | tf_op | source)
XLA Modules:
  0.0 120.7 jit_solution(5207846732100666312)
XLA Ops:
  0.6 0.8 broadcast_in_dim.14
  1.4 31.9 %all_to_all.15 = bf16[32,32,256]{2,1,0:T(8,128)(2,1)S(1)} all-to-all(bf16[32,32,256]{2,1,0:T(8,128)(2,1)S(1)} %broadcast_in_dim.14), channel_id=1, replica_groups={{0,2,4,6,8,10,12,14,96,98,100,102,104,106,108,110,128,130,132,134,136,1..., dimensions={0} | all-to-all | bytes 1048576 | tf_op jit(solution)/shard_map/all_to_all | solution.py:27
  33.3 1.4 %collective-permute-start = (bf16[1024,256]{1,0:T(8,128)(2,1)S(1)}, bf16[1024,256]{1,0:T(8,128)(2,1)S(1)}, u32[]{:S(2)}, u32[]{:S(2)}) collective-permute-start(bf16[1024,256]{1,0:T(8,128)(2,1)S(1)} %bitcast.11), channel_id=1, source_target_pairs={{0,48},{2,50},{4,52},{6,54},{8,56},{10,58},{12,60},{14,62},{16,0},... | collective-permute-start | bytes 1572872 | tf_op jit(solution)/shard_map/ppermute | solution.py:37
  34.8 0.6 collective-permute-start.1
  35.4 0.1 collective-permute-start.2
  35.5 3.2 %collective-permute-start.3 = (bf16[512,256]{1,0:T(8,128)(2,1)S(1)}, bf16[512,256]{1,0:T(8,128)(2,1)S(1)}, u32[]{:S(2)}, u32[]{:S(2)}) collective-permute-start(bf16[512,256]{1,0:T(8,128)(2,1)S(1)} %bitcast.15), channel_id=1, source_target_pairs={{0,192},{2,194},{4,196},{6,198},{8,200},{10,202},{12,204},{14,206}... | collective-permute-start | bytes 786440 | tf_op jit(solution)/shard_map/ppermute | solution.py:37
  38.7 0.0 copy-start
  38.7 3.4 %copy-done = bf16[4096,1024]{1,0:T(8,128)(2,1)S(1)} copy-done((bf16[4096,1024]{1,0:T(8,128)(2,1)S(1)}, bf16[4096,1024]{1,0:T(8,128)(2,1)}, u32[]{:S(2)}) %copy-start) | copy-done | bytes 8388632
  42.1 0.0 copy-start.1
  42.1 1.0 copy-done.1
  43.1 0.4 shard_map.58
  43.6 0.0 collective-permute-done.2.d0
  43.6 0.0 collective-permute-done.3.d1
  43.6 0.6 collective-permute-done.b
  44.2 1.2 collective-permute-done.1.c
  45.3 0.0 slice-start
  45.3 0.0 slice-start.1
  45.3 3.2 %shard_map.59 = (f32[256,1024]{1,0:T(8,128)S(1)}, f32[128,6,128]{2,1,0:T(8,128)S(1)}, bf16[2048,256]{1,0:T(8,128)(2,1)S(1)}, bf16[2048,256]{1,0:T(8,128)(2,1)S(1)}) custom-call(s32[1]{0:T(128)} %bitcast.own, s32[1]{0:T(128)} %bitcast.1.core, bf16[1024,256]{1,0:T(8,128)(2,1)S(1)} %bitcast.13, bf16[1024,256]{1,0:T(8,128)(2,1)S(1)} %collective-permute-done.b, ...), custom_call_target="tpu_custom_call" | custom-call | flops 2147483648 | bytes 12582912 | tf_op jit(solution)/shard_map/pallas_call | solution.py:52
  48.5 27.5 %all_to_all.16.stats = f32[128,6,128]{2,1,0:T(8,128)S(1)} all-to-all(f32[128,6,128]{2,1,0:T(8,128)S(1)} %get-tuple-element.27), channel_id=1, replica_groups=mesh['vocab'=128,'rows'=2] {'vocab'}, dimensions={0} | all-to-all | bytes 786432 | tf_op jit(solution)/shard_map/all_to_all | solution.py:27
  76.1 0.0 collective-permute-start.8
  76.1 2.6 %shard_map.60 = (bf16[256,1024]{1,0:T(8,128)(2,1)S(1)}, bf16[1024,256]{1,0:T(8,128)(2,1)S(1)}, bf16[1024,256]{1,0:T(8,128)(2,1)S(1)}, bf16[1024,256]{1,0:T(8,128)(2,1)S(1)}, f32[2,128]{1,0:T(2,128)}) custom-call(s32[1]{0:T(128)} %bitcast.own, f32[256,1024]{1,0:T(8,128)S(1)} %get-tuple-element.26.student, bf16[256,1024]{1,0:T(8,128)(2,1)S(1)} %copy-done.1, ...), custom_call_target="tpu_custom_call" | custom-call | flops 1073741824 | bytes 8388608 | tf_op jit(solution)/shard_map/pallas_call | solution.py:52
  78.7 0.5 collective-permute-start.9
  79.2 1.2 %collective-permute-start.4 = (bf16[1024,256]{1,0:T(8,128)(2,1)S(1)}, bf16[1024,256]{1,0:T(8,128)(2,1)S(1)}, u32[]{:S(2)}, u32[]{:S(2)}) collective-permute-start(bf16[1024,256]{1,0:T(8,128)(2,1)S(1)} %get-tuple-element.32), channel_id=1, source_target_pairs={{0,16},{2,18},{4,20},{6,22},{8,24},{10,26},{12,28},{14,30},{16,32}... | collective-permute-start | bytes 1572872 | tf_op jit(solution)/shard_map/ppermute | solution.py:37
  80.4 2.0 %collective-permute-start.5 = (bf16[1024,256]{1,0:T(8,128)(2,1)S(1)}, bf16[1024,256]{1,0:T(8,128)(2,1)S(1)}, u32[]{:S(2)}, u32[]{:S(2)}) collective-permute-start(bf16[1024,256]{1,0:T(8,128)(2,1)S(1)} %get-tuple-element.33), channel_id=1, source_target_pairs={{0,48},{2,50},{4,52},{6,54},{8,56},{10,58},{12,60},{14,62},{16,0},... | collective-permute-start | bytes 1572872 | tf_op jit(solution)/shard_map/ppermute | solution.py:37
  82.3 0.0 slice-done
  82.3 0.0 slice-done.1
  82.4 1.3 %shard_map.61 = (bf16[512,256]{1,0:T(8,128)(2,1)S(1)}, bf16[512,256]{1,0:T(8,128)(2,1)S(1)}, f32[1024,256]{1,0:T(8,128)S(1)}) custom-call(s32[1]{0:T(128)} %bitcast.own, bf16[1024,256]{1,0:T(8,128)(2,1)S(1)} %get-tuple-element.30.score_t, bf16[4096,1024]{1,0:T(8,128)(2,1)S(1)} %bitcast.10), custom_call_target="tpu_custom_call" | custom-call | flops 1073741824 | bytes 7340032 | tf_op jit(solution)/shard_map/pallas_call | solution.py:52
  83.6 0.1 collective-permute-start.6
  83.7 0.0 collective-permute-done.9.score_theirs
  83.7 3.2 %collective-permute-start.7 = (bf16[512,256]{1,0:T(8,128)(2,1)S(1)}, bf16[512,256]{1,0:T(8,128)(2,1)S(1)}, u32[]{:S(2)}, u32[]{:S(2)}) collective-permute-start(bf16[512,256]{1,0:T(8,128)(2,1)S(1)} %get-tuple-element.35), channel_id=1, source_target_pairs={{0,192},{2,194},{4,196},{6,198},{8,200},{10,202},{12,204},{14,206}... | collective-permute-start | bytes 786440 | tf_op jit(solution)/shard_map/ppermute | solution.py:37
  86.9 0.0 collective-permute-done.8.theirs
  86.9 5.4 %shard_map.62 = bf16[2048,1024]{1,0:T(8,128)(2,1)} custom-call(bf16[2048,256]{1,0:T(8,128)(2,1)S(1)} %get-tuple-element.36.mine, bf16[2048,256]{1,0:T(8,128)(2,1)S(1)} %collective-permute-done.8.theirs, bf16[256,1024]{1,0:T(8,128)(2,1)S(1)} %get-tuple-element.38.score, bf16[256,1024]{1,0:T(8,128)(2,1)S(1)} %collective-permute-done.9.score_theirs), custom_call_target="tpu_custom_call" | custom-call | flops 2147483648 | bytes 7340032 | tf_op jit(solution)/shard_map/pallas_call | solution.py:155
  92.3 0.5 collective-permute-done.6
  92.8 0.0 collective-permute-done.7
  92.8 1.6 %collective-permute-done.4 = bf16[1024,256]{1,0:T(8,128)(2,1)S(1)} collective-permute-done((bf16[1024,256]{1,0:T(8,128)(2,1)S(1)}, bf16[1024,256]{1,0:T(8,128)(2,1)S(1)}, u32[]{:S(2)}, u32[]{:S(2)}) %collective-permute-start.4) | collective-permute-done | bytes 524320 | tf_op jit(solution)/shard_map/ppermute | solution.py:37
  94.4 0.0 collective-permute-done.5
  94.4 0.3 add_convert_fusion
  94.7 25.3 %all_to_all.17 = bf16[32,32,256]{2,1,0:T(8,128)(2,1)S(1)} all-to-all(bf16[32,32,256]{2,1,0:T(8,128)(2,1)S(1)} %bitcast.14), channel_id=1, replica_groups={{0,2,4,6,8,10,12,14,96,98,100,102,104,106,108,110,128,130,132,134,136,1..., dimensions={0} | all-to-all | bytes 1048576 | tf_op jit(solution)/shard_map/all_to_all | solution.py:27
  120.0 0.7 reduce_sum.12
  (2 shorter events, 0.0 us)
Async XLA Ops:
  33.3 10.8 %collective-permute-start = (bf16[1024,256]{1,0:T(8,128)(2,1)S(1)}, bf16[1024,256]{1,0:T(8,128)(2,1)S(1)}, u32[]{:S(2)}, u32[]{:S(2)}) collective-permute-start(bf16[1024,256]{1,0:T(8,128)(2,1)S(1)} %bitcast.11), channel_id=1, source_target_pairs={{0,48},{2,50},{4,52},{6,54},{8,56},{10,58},{12,60},{14,62},{16,0},... | collective-permute-start | bytes 1572872 | tf_op jit(solution)/shard_map/ppermute | solution.py:37
  34.8 10.6 %collective-permute-start.1 = (bf16[1024,256]{1,0:T(8,128)(2,1)S(1)}, bf16[1024,256]{1,0:T(8,128)(2,1)S(1)}, u32[]{:S(2)}, u32[]{:S(2)}) collective-permute-start(bf16[1024,256]{1,0:T(8,128)(2,1)S(1)} %bitcast.12), channel_id=1, source_target_pairs={{0,16},{2,18},{4,20},{6,22},{8,24},{10,26},{12,28},{14,30},{16,32}... | collective-permute-start | bytes 1572872 | tf_op jit(solution)/shard_map/ppermute | solution.py:37
  35.4 8.2 %collective-permute-start.2 = (bf16[512,256]{1,0:T(8,128)(2,1)S(1)}, bf16[512,256]{1,0:T(8,128)(2,1)S(1)}, u32[]{:S(2)}, u32[]{:S(2)}) collective-permute-start(bf16[512,256]{1,0:T(8,128)(2,1)S(1)} %bitcast.16), channel_id=1, source_target_pairs={{0,64},{2,66},{4,68},{6,70},{8,72},{10,74},{12,76},{14,78},{16,80}... | collective-permute-start | bytes 786440 | tf_op jit(solution)/shard_map/ppermute | solution.py:37
  35.5 8.1 %collective-permute-start.3 = (bf16[512,256]{1,0:T(8,128)(2,1)S(1)}, bf16[512,256]{1,0:T(8,128)(2,1)S(1)}, u32[]{:S(2)}, u32[]{:S(2)}) collective-permute-start(bf16[512,256]{1,0:T(8,128)(2,1)S(1)} %bitcast.15), channel_id=1, source_target_pairs={{0,192},{2,194},{4,196},{6,198},{8,200},{10,202},{12,204},{14,206}... | collective-permute-start | bytes 786440 | tf_op jit(solution)/shard_map/ppermute | solution.py:37
  38.7 3.4 %copy-start = (bf16[4096,1024]{1,0:T(8,128)(2,1)S(1)}, bf16[4096,1024]{1,0:T(8,128)(2,1)}, u32[]{:S(2)}) copy-start(bf16[4096,1024]{1,0:T(8,128)(2,1)} %head.7) | copy-start | bytes 25165828
  42.1 1.0 copy-start.1
  45.3 37.0 %slice-start = ((s8[8388608]{0:T(1024)(128)(4,1)}), s8[4194304]{0:T(1024)(128)(4,1)S(1)}, s32[]{:S(2)}) async-start(s8[8388608]{0:T(1024)(128)(4,1)} %bitcast.9), calls=%async_computation.3 | async-start | bytes 8388608
  45.3 37.0 %slice-start.1 = ((s8[8388608]{0:T(1024)(128)(4,1)}), s8[4194304]{0:T(1024)(128)(4,1)S(1)}, s32[]{:S(2)}) async-start(s8[8388608]{0:T(1024)(128)(4,1)} %bitcast.9), calls=%async_computation.4 | async-start | bytes 8388608
  76.1 10.9 %collective-permute-start.8 = (bf16[2048,256]{1,0:T(8,128)(2,1)S(1)}, bf16[2048,256]{1,0:T(8,128)(2,1)S(1)}, u32[]{:S(2)}, u32[]{:S(2)}) collective-permute-start(bf16[2048,256]{1,0:T(8,128)(2,1)S(1)} %get-tuple-element.37), channel_id=1, source_target_pairs={{0,1},{1,0},{2,3},{3,2},{4,5},{5,4},{6,7},{7,6},{8,9},{9,8},{10,11... | collective-permute-start | bytes 3145736 | tf_op jit(solution)/shard_map/ppermute | solution.py:41
  78.7 5.0 %collective-permute-start.9 = (bf16[256,1024]{1,0:T(8,128)(2,1)S(1)}, bf16[256,1024]{1,0:T(8,128)(2,1)S(1)}, u32[]{:S(2)}, u32[]{:S(2)}) collective-permute-start(bf16[256,1024]{1,0:T(8,128)(2,1)S(1)} %get-tuple-element.38.score), channel_id=1, source_target_pairs={{0,1},{1,0},{2,3},{3,2},{4,5},{5,4},{6,7},{7,6},{8,9},{9,8},{10,11... | collective-permute-start | bytes 1572872 | tf_op jit(solution)/shard_map/ppermute | solution.py:41
  79.2 15.3 %collective-permute-start.4 = (bf16[1024,256]{1,0:T(8,128)(2,1)S(1)}, bf16[1024,256]{1,0:T(8,128)(2,1)S(1)}, u32[]{:S(2)}, u32[]{:S(2)}) collective-permute-start(bf16[1024,256]{1,0:T(8,128)(2,1)S(1)} %get-tuple-element.32), channel_id=1, source_target_pairs={{0,16},{2,18},{4,20},{6,22},{8,24},{10,26},{12,28},{14,30},{16,32}... | collective-permute-start | bytes 1572872 | tf_op jit(solution)/shard_map/ppermute | solution.py:37
  80.4 14.0 %collective-permute-start.5 = (bf16[1024,256]{1,0:T(8,128)(2,1)S(1)}, bf16[1024,256]{1,0:T(8,128)(2,1)S(1)}, u32[]{:S(2)}, u32[]{:S(2)}) collective-permute-start(bf16[1024,256]{1,0:T(8,128)(2,1)S(1)} %get-tuple-element.33), channel_id=1, source_target_pairs={{0,48},{2,50},{4,52},{6,54},{8,56},{10,58},{12,60},{14,62},{16,0},... | collective-permute-start | bytes 1572872 | tf_op jit(solution)/shard_map/ppermute | solution.py:37
  83.6 9.2 %collective-permute-start.6 = (bf16[512,256]{1,0:T(8,128)(2,1)S(1)}, bf16[512,256]{1,0:T(8,128)(2,1)S(1)}, u32[]{:S(2)}, u32[]{:S(2)}) collective-permute-start(bf16[512,256]{1,0:T(8,128)(2,1)S(1)} %get-tuple-element.34), channel_id=1, source_target_pairs={{0,64},{2,66},{4,68},{6,70},{8,72},{10,74},{12,76},{14,78},{16,80}... | collective-permute-start | bytes 786440 | tf_op jit(solution)/shard_map/ppermute | solution.py:37
  83.7 9.1 %collective-permute-start.7 = (bf16[512,256]{1,0:T(8,128)(2,1)S(1)}, bf16[512,256]{1,0:T(8,128)(2,1)S(1)}, u32[]{:S(2)}, u32[]{:S(2)}) collective-permute-start(bf16[512,256]{1,0:T(8,128)(2,1)S(1)} %get-tuple-element.35), channel_id=1, source_target_pairs={{0,192},{2,194},{4,196},{6,198},{8,200},{10,202},{12,204},{14,206}... | collective-permute-start | bytes 786440 | tf_op jit(solution)/shard_map/ppermute | solution.py:37

commit v4 on v3

--- a/solution.py
+++ b/solution.py
@@ -46,14 +46,14 @@
     return pl.multiple_of(slab * SLAB, SLAB)
 
 
-def call(body, outs, ins, flops, traffic, scratch=(), limit=8):
+def call(body, outs, ins, flops, traffic, scratch=(), limit=8, into="v"):
     smem, vmem, hbm = pltpu.SMEM, pltpu.VMEM, pltpu.HBM
     spaces = {"s": smem, "v": vmem, "h": hbm}
     return pl.pallas_call(
         body,
         out_shape=[jax.ShapeDtypeStruct(shape, dtype) for shape, dtype in outs],
         in_specs=[pl.BlockSpec(memory_space=spaces[kind]) for kind, _ in ins],
-        out_specs=[pl.BlockSpec(memory_space=vmem) for _ in outs],
+        out_specs=[pl.BlockSpec(memory_space=spaces[into]) for _ in outs],
         scratch_shapes=list(scratch),
         compiler_params=pltpu.CompilerParams(vmem_limit_bytes=limit * MIB),
         cost_estimate=pl.CostEstimate(flops=flops, bytes_accessed=traffic, transcendentals=0),
@@ -69,7 +69,7 @@
 
 
 def student_kernel(
-    own, core, a, b, c, d0, d1, head, mentor, prob, lse_t, student, stats, mine, theirs
+    own, core, a, b, c, d0, d1, head, mentor, prob, lse_t, rise, peak, stats, mine, theirs
 ):
     for offset, ref, first, count in [(0, a, 0, 4), (1, b, 0, 4), (3, c, 0, 4), (2, d0, 0, 2), (2, d1, 2, 2)]:
         for i in range(count):
@@ -94,22 +94,39 @@
         )
 
     scores = (product(mine, core[0]) + product(theirs, 1 - core[0])) / sharpness_divisor
-    student[...] = scores
     top = jnp.max(scores, axis=1, keepdims=True)
-    lse_s = top + jnp.log(jnp.sum(jnp.exp(scores - top), axis=1, keepdims=True))
+    grown = jnp.exp(scores - top)
+    rise[...] = grown
+    peak[...] = jnp.broadcast_to(top, peak.shape)
+    lse_s = top + jnp.log(jnp.sum(grown, axis=1, keepdims=True))
     target = mentor[...].astype(f32) / sharpness_divisor
     cross = jnp.sum(prob[...] * (target - scores), axis=1, keepdims=True)
     lane = lax.broadcasted_iota(jnp.int32, (ROWS, 128), 1)
     columns = jnp.where(lane == 0, lse_s, jnp.where(lane == 1, lse_t[...], cross))
     flat = jnp.transpose(columns)
     lines = [flat[i : i + 1, h * 128 : (h + 1) * 128] for i in range(3) for h in range(2)]
-    chunk = jnp.concatenate(lines, axis=0)
+    stats[...] = jnp.concatenate(lines + lines[:2], axis=0)
+
+
+def as_columns(first, second):
+    lines = [jnp.concatenate([v[0:1], v[1:2]], axis=1) for v in (first, second)]
+    flat = jnp.transpose(jnp.concatenate(lines * 4, axis=0))
+    return flat[:, 0:1], flat[:, 1:2]
+
+
+def merged(parts):
+    top = jnp.max(parts, axis=0)
+    weight = jnp.exp(parts - top[None])
+    total = jnp.sum(weight, axis=0)
+    lse = top + jnp.log(total)
+    cross = jnp.sum(weight[:, 2:4] * parts[:, 4:6], axis=0) / total[2:4]
+    return lse[0:2], lse[2:4], cross
+
+
+def merge_kernel(first, second, third, fourth, stats):
+    all_s, all_t, cross = merged(jnp.stack([r[...] for r in (first, second, third, fourth)]))
+    chunk = jnp.concatenate([all_s, all_t, cross, cross], axis=0)
     stats[...] = jnp.broadcast_to(chunk[None], stats.shape)
-
-
-def as_column(lines):
-    flat = jnp.concatenate([lines[0:1], lines[1:2]], axis=1)
-    return jnp.transpose(jnp.broadcast_to(flat, (128, ROWS)))[:, 0:1]
 
 
 def times_head(own, head, score_t, outs):
@@ -118,18 +135,14 @@
         ref[...] = jnp.dot(head[rows], score_t, preferred_element_type=f32).astype(ref.dtype)
 
 
-def score_kernel(own, student, mentor, stats, head, score, score_t, b, c, mismatch):
-    parts = stats[...]
-    top = jnp.max(parts, axis=0)
-    weight = jnp.exp(parts - top[None])
-    total = jnp.sum(weight, axis=0)
-    lse = top + jnp.log(total)
-    all_s, all_t = lse[0:2], lse[2:4]
-    cross = jnp.sum(weight[:, 2:4] * parts[:, 4:6], axis=0) / total[2:4]
+def score_kernel(own, rise, peak, prob, lse_t, stats, head, score, score_t, b, c, mismatch):
+    all_s, all_t, cross = merged(stats[...])
     mismatch[...] = sharpness_divisor * sharpness_divisor * (cross + all_s - all_t)
-    target = mentor[...].astype(f32) / sharpness_divisor
-    gap = jnp.exp(student[...] - as_column(all_s)) - jnp.exp(target - as_column(all_t))
-    rounded = (objective_factor * sharpness_divisor * gap).astype(bf16)
+    end_s, end_t = as_columns(all_s, all_t)
+    scale = objective_factor * sharpness_divisor
+    share_s = scale * jnp.exp(peak[:, 0:1] - end_s)
+    share_t = scale * jnp.exp(lse_t[:, 0:1] - end_t)
+    rounded = (rise[...] * share_s - prob[...] * share_t).astype(bf16)
     score[...] = rounded
     score_t[...] = jnp.transpose(rounded)
     outs = [(o, j, r.at[pl.ds(j * SLAB, SLAB)]) for o, r in ((1, b), (3, c)) for j in range(4)]
@@ -142,25 +155,26 @@
     times_head(own, head, score_t[...], outs)
 
 
-def weight_kernel(mine, theirs, score, score_theirs, out):
-    total = jnp.dot(mine[...], score[...], preferred_element_type=f32)
-    total += jnp.dot(theirs[...], score_theirs[...], preferred_element_type=f32)
-    out[...] = total.astype(out.dtype)
-
-
-def weight_grad_of(mine, theirs, score, score_theirs):
-    tile = 256
-    rows = pl.BlockSpec((tile, ROWS), lambda i: (i, 0))
-    whole = pl.BlockSpec((ROWS, COLS), lambda i: (0, 0))
-    return pl.pallas_call(
-        weight_kernel,
-        grid=(FULL // 2 // tile,),
-        out_shape=jax.ShapeDtypeStruct((FULL // 2, COLS), bf16),
-        in_specs=[rows, rows, whole, whole],
-        out_specs=pl.BlockSpec((tile, COLS), lambda i: (i, 0)),
-        compiler_params=pltpu.CompilerParams(vmem_limit_bytes=8 * MIB),
-        cost_estimate=pl.CostEstimate(flops=2 * FULL * ROWS * COLS, bytes_accessed=7 * MIB, transcendentals=0),
-    )(mine, theirs, score, score_theirs)
+def weight_kernel(mine, theirs, score, score_theirs, out, held, sems):
+    def send(i):
+        return pltpu.make_async_copy(held.at[i], out.at[pl.ds(i * SLAB, SLAB)], sems.at[i])
+
+    for i in range(8):
+        rows = pl.ds(i * SLAB, SLAB)
+        total = jnp.dot(mine[rows], score[...], preferred_element_type=f32)
+        total += jnp.dot(theirs[rows], score_theirs[...], preferred_element_type=f32)
+        held[i] = total.astype(bf16)
+        send(i).start()
+    for i in range(8):
+        send(i).wait()
+
+
+def stats_of_all(stats):
+    near = [stats, step(stats, 0, 1), step(stats, 0, -1), step(stats, 1, 0)]
+    (stats,) = call(
+        merge_kernel, [((32, 8, 128), f32)], [("v", value) for value in near], 1000, 1000
+    )
+    return trade(stats, class_groups)
 
 
 def shards(hidden, head_weight, mentor_outputs):
@@ -179,21 +193,21 @@
     b, c = step(a, 0, -1), step(a, 0, 1)
     d0, d1 = step(a[:512], 1, 0), step(a[512:], -1, 0)
 
-    student, stats, mine, theirs = call(
+    rise, peak, stats, mine, theirs = call(
         student_kernel,
-        [((ROWS, COLS), f32), ((128, 6, 128), f32)] + [((FULL // 2, ROWS), bf16)] * 2,
+        [((ROWS, COLS), f32), ((ROWS, 128), f32), ((8, 128), f32)] + [((FULL // 2, ROWS), bf16)] * 2,
         [("s", own), ("s", core), ("v", a), ("v", b), ("v", c), ("v", d0), ("v", d1), ("v", head_weight)]
         + [("v", mentor_outputs), ("v", prob), ("v", lse_t)],
         2 * FULL * ROWS * COLS,
         12 * MIB,
     )
-    stats, theirs = lax.optimization_barrier((trade(stats, None), theirs))
+    stats, theirs = lax.optimization_barrier((stats_of_all(stats), theirs))
     theirs = other_core(theirs)
 
     score, score_t, b, c, mismatch = call(
         score_kernel,
         [((ROWS, COLS), bf16), ((COLS, ROWS), bf16)] + [((1024, ROWS), bf16)] * 2 + [((2, 128), f32)],
-        [("s", own), ("v", student), ("v", mentor_outputs), ("v", stats), ("v", head_weight)],
+        [("s", own), ("v", rise), ("v", peak), ("v", prob), ("v", lse_t), ("v", stats), ("v", head_weight)],
         FULL * ROWS * COLS,
         8 * MIB,
     )
@@ -207,7 +221,15 @@
         7 * MIB,
     )
     d0, d1 = step(d0, 1, 0), step(d1, -1, 0)
-    weight_grad = weight_grad_of(mine, theirs, score, score_theirs)
+    (weight_grad,) = call(
+        weight_kernel,
+        [((FULL // 2, COLS), bf16)],
+        [("v", mine), ("v", theirs), ("v", score), ("v", score_theirs)],
+        2 * FULL * ROWS * COLS,
+        7 * MIB,
+        [pltpu.VMEM((8, SLAB, COLS), bf16), pltpu.SemaphoreType.DMA((8,))],
+        into="h",
+    )
     b, c, d0, d1, weight_grad = lax.optimization_barrier((b, c, d0, d1, weight_grad))
     part = a + b.astype(f32) + c.astype(f32) + jnp.concatenate([d0, d1], axis=0).astype(f32)
     part = trade(part.astype(bf16).reshape(32, 32, ROWS), class_groups)

time: 121 us -> 119 us (0.983)
  waiting for transfers between devices: 3.88 us -> 12.9 us
  blocking collectives: 84.7 us -> 76.3 us
  Pallas kernels: 12.8 us -> 10.5 us
    ppermute x8 -> x11, waiting for transfers between devices: 3.88 us -> 12.9 us  [step(): return lax.ppermute(value, 'vocab', pairs)]
    all_to_all x3, blocking collectives: 84.7 us -> 76.3 us  [trade(): lax.all_to_all(chunks, 'vocab', 0, 0, tiled=True, axis_index_groups=groups)]
    pallas_call x1 -> x0, Pallas kernels: 5.38 us -> none  [weight_grad_of(): pl.pallas_call(weight_kernel, grid=(FULL // 2 // tile,), out_shape=jax.Sh...]
    pallas_call x4 -> x6, Pallas kernels: 7.45 us -> 10.5 us  [call(): pl.pallas_call(body, out_shape=[jax.ShapeDtypeStruct(shape, dtype) for sh...]
    ppermute x8 -> x11, starting transfers between devices: 11.8 us -> 12 us  [step(): return lax.ppermute(value, 'vocab', pairs)]
  transfers between devices with their start and end apart: 10 -> 13, of which waited for: 4 -> 9; matrix products, arithmetic and copies ran while one was open for 0% -> 0% of each run, Pallas kernels for 8% -> 6%
where the time goes in v4:
time: 119 us
  blocking collectives  76.3 us (64%)
  waiting for transfers between devices  12.9 us (11%)
  starting transfers between devices  12.4 us (10%)
  Pallas kernels  10.5 us (9%)
  local copies, waits for them, and re-layouts  5.23 us (4%)
    all_to_all x3, blocking collectives, trade(): lax.all_to_all(chunks, 'vocab', 0, 0, tiled=True, axis_index_groups=groups)  76.3 us
    ppermute x11, waiting for transfers between devices, step(): return lax.ppermute(value, 'vocab', pairs)  12.9 us
    ppermute x11, starting transfers between devices, step(): return lax.ppermute(value, 'vocab', pairs)  12 us
    pallas_call x6, Pallas kernels, call(): pl.pallas_call(body, out_shape=[jax.ShapeDtypeStruct(shape, dtype) for sh...  10.5 us
    unnamed x8, local copies, waits for them, and re-layouts  4.43 us
  transfers between devices with their start and end apart: 13, of which 9 were waited for; matrix products, arithmetic and copies ran while one was open for 0% of the time, Pallas kernels for 6%

profile of v4, /device:TPU:2, one launch (start us, length us, event | category | flops | bytes accessed | tf_op | source)
XLA Modules:
  0.0 119.0 jit_solution(4520830933418797658)
XLA Ops:
  0.6 0.8 broadcast_in_dim.14
  1.4 31.9 %all_to_all.15 = bf16[32,32,256]{2,1,0:T(8,128)(2,1)S(1)} all-to-all(bf16[32,32,256]{2,1,0:T(8,128)(2,1)S(1)} %broadcast_in_dim.14), channel_id=1, replica_groups={{0,2,4,6,8,10,12,14,96,98,100,102,104,106,108,110,128,130,132,134,136,1..., dimensions={0} | all-to-all | bytes 1048576 | tf_op jit(solution)/shard_map/all_to_all | solution.py:27
  33.3 1.4 %collective-permute-start = (bf16[1024,256]{1,0:T(8,128)(2,1)S(1)}, bf16[1024,256]{1,0:T(8,128)(2,1)S(1)}, u32[]{:S(2)}, u32[]{:S(2)}) collective-permute-start(bf16[1024,256]{1,0:T(8,128)(2,1)S(1)} %bitcast.11), channel_id=1, source_target_pairs={{0,48},{2,50},{4,52},{6,54},{8,56},{10,58},{12,60},{14,62},{16,0},... | collective-permute-start | bytes 1572872 | tf_op jit(solution)/shard_map/ppermute | solution.py:37
  34.8 0.6 collective-permute-start.1
  35.4 0.1 collective-permute-start.2
  35.5 3.2 %collective-permute-start.3 = (bf16[512,256]{1,0:T(8,128)(2,1)S(1)}, bf16[512,256]{1,0:T(8,128)(2,1)S(1)}, u32[]{:S(2)}, u32[]{:S(2)}) collective-permute-start(bf16[512,256]{1,0:T(8,128)(2,1)S(1)} %bitcast.15), channel_id=1, source_target_pairs={{0,192},{2,194},{4,196},{6,198},{8,200},{10,202},{12,204},{14,206}... | collective-permute-start | bytes 786440 | tf_op jit(solution)/shard_map/ppermute | solution.py:37
  38.7 0.0 copy-start
  38.7 3.4 %copy-done = bf16[4096,1024]{1,0:T(8,128)(2,1)S(1)} copy-done((bf16[4096,1024]{1,0:T(8,128)(2,1)S(1)}, bf16[4096,1024]{1,0:T(8,128)(2,1)}, u32[]{:S(2)}) %copy-start) | copy-done | bytes 8388632
  42.1 0.0 copy-start.1
  42.1 1.0 copy-done.1
  43.1 0.0 slice-start
  43.1 0.4 shard_map.58
  43.6 0.0 collective-permute-done.2.d0
  43.6 0.0 collective-permute-done.3.d1
  43.6 0.6 collective-permute-done.b
  44.2 1.2 collective-permute-done.1.c
  45.3 0.0 slice-start.1
  45.3 3.2 %shard_map.59 = (f32[256,1024]{1,0:T(8,128)S(1)}, f32[256,128]{1,0:T(8,128)S(1)}, f32[8,128]{1,0:T(8,128)S(1)}, bf16[2048,256]{1,0:T(8,128)(2,1)S(1)}, bf16[2048,256]{1,0:T(8,128)(2,1)S(1)}) custom-call(s32[1]{0:T(128)} %bitcast.own, s32[1]{0:T(128)} %bitcast.1.core, bf16[1024,256]{1,0:T(8,128)(2,1)S(1)} %bitcast.13, ...), custom_call_target="tpu_custom_call" | custom-call | flops 2147483648 | bytes 12582912 | tf_op jit(solution)/shard_map/pallas_call | solution.py:52
  48.5 0.6 collective-permute-start.4
  49.2 1.8 %collective-permute-start.5 = (f32[8,128]{1,0:T(8,128)S(1)}, f32[8,128]{1,0:T(8,128)S(1)}, u32[]{:S(2)}, u32[]{:S(2)}) collective-permute-start(f32[8,128]{1,0:T(8,128)S(1)} %get-tuple-element.29.first), channel_id=1, source_target_pairs={{0,48},{2,50},{4,52},{6,54},{8,56},{10,58},{12,60},{14,62},{16,0},... | collective-permute-start | bytes 12296 | tf_op jit(solution)/shard_map/ppermute | solution.py:37
  51.0 0.0 collective-permute-start.6
  51.0 1.5 %collective-permute-done.4.second = f32[8,128]{1,0:T(8,128)S(1)} collective-permute-done((f32[8,128]{1,0:T(8,128)S(1)}, f32[8,128]{1,0:T(8,128)S(1)}, u32[]{:S(2)}, u32[]{:S(2)}) %collective-permute-start.4) | collective-permute-done | bytes 4128 | tf_op jit(solution)/shard_map/ppermute | solution.py:37
  52.5 0.3 collective-permute-done.5.third
  52.8 3.1 %collective-permute-done.6.fourth = f32[8,128]{1,0:T(8,128)S(1)} collective-permute-done((f32[8,128]{1,0:T(8,128)S(1)}, f32[8,128]{1,0:T(8,128)S(1)}, u32[]{:S(2)}, u32[]{:S(2)}) %collective-permute-start.6) | collective-permute-done | bytes 4128 | tf_op jit(solution)/shard_map/ppermute | solution.py:37
  55.9 20.1 %all_to_all.16.stats = f32[32,8,128]{2,1,0:T(8,128)S(1)} all-to-all(f32[32,8,128]{2,1,0:T(8,128)S(1)} %shard_map.60), channel_id=1, replica_groups={{0,2,4,6,8,10,12,14,96,98,100,102,104,106,108,110,128,130,132,134,136,1..., dimensions={0} | all-to-all | bytes 262144 | tf_op jit(solution)/shard_map/all_to_all | solution.py:27
  76.0 0.0 collective-permute-start.11
  76.0 0.0 slice-done
  76.0 0.0 slice-done.1
  76.0 2.4 %shard_map.61 = (bf16[256,1024]{1,0:T(8,128)(2,1)S(1)}, bf16[1024,256]{1,0:T(8,128)(2,1)S(1)}, bf16[1024,256]{1,0:T(8,128)(2,1)S(1)}, bf16[1024,256]{1,0:T(8,128)(2,1)S(1)}, f32[2,128]{1,0:T(2,128)}) custom-call(s32[1]{0:T(128)} %bitcast.own, f32[256,1024]{1,0:T(8,128)S(1)} %get-tuple-element.27.rise, f32[256,128]{1,0:T(8,128)S(1)} %get-tuple-element.28.peak, ...), custom_call_target="tpu_custom_call" | custom-call | flops 1073741824 | bytes 8388608 | tf_op jit(solution)/shard_map/pallas_call | solution.py:52
  78.4 0.5 collective-permute-start.12
  78.9 1.4 %collective-permute-start.7 = (bf16[1024,256]{1,0:T(8,128)(2,1)S(1)}, bf16[1024,256]{1,0:T(8,128)(2,1)S(1)}, u32[]{:S(2)}, u32[]{:S(2)}) collective-permute-start(bf16[1024,256]{1,0:T(8,128)(2,1)S(1)} %get-tuple-element.34), channel_id=1, source_target_pairs={{0,16},{2,18},{4,20},{6,22},{8,24},{10,26},{12,28},{14,30},{16,32}... | collective-permute-start | bytes 1572872 | tf_op jit(solution)/shard_map/ppermute | solution.py:37
  80.3 0.6 collective-permute-start.8
  80.9 1.3 %shard_map.62 = (bf16[512,256]{1,0:T(8,128)(2,1)S(1)}, bf16[512,256]{1,0:T(8,128)(2,1)S(1)}, f32[1024,256]{1,0:T(8,128)S(1)}) custom-call(s32[1]{0:T(128)} %bitcast.own, bf16[1024,256]{1,0:T(8,128)(2,1)S(1)} %get-tuple-element.32.score_t, bf16[4096,1024]{1,0:T(8,128)(2,1)S(1)} %bitcast.10), custom_call_target="tpu_custom_call" | custom-call | flops 1073741824 | bytes 7340032 | tf_op jit(solution)/shard_map/pallas_call | solution.py:52
  82.2 0.4 collective-permute-start.10
  82.5 0.0 collective-permute-done.12.score_theirs
  82.6 1.7 %collective-permute-start.9 = (bf16[512,256]{1,0:T(8,128)(2,1)S(1)}, bf16[512,256]{1,0:T(8,128)(2,1)S(1)}, u32[]{:S(2)}, u32[]{:S(2)}) collective-permute-start(bf16[512,256]{1,0:T(8,128)(2,1)S(1)} %get-tuple-element.36), channel_id=1, source_target_pairs={{0,64},{2,66},{4,68},{6,70},{8,72},{10,74},{12,76},{14,78},{16,80}... | collective-permute-start | bytes 786440 | tf_op jit(solution)/shard_map/ppermute | solution.py:37
  84.3 0.0 collective-permute-done.11.theirs
  84.3 3.2 %shard_map.63 = bf16[2048,1024]{1,0:T(8,128)(2,1)} custom-call(bf16[2048,256]{1,0:T(8,128)(2,1)S(1)} %get-tuple-element.38.mine, bf16[2048,256]{1,0:T(8,128)(2,1)S(1)} %collective-permute-done.11.theirs, bf16[256,1024]{1,0:T(8,128)(2,1)S(1)} %get-tuple-element.40.score, bf16[256,1024]{1,0:T(8,128)(2,1)S(1)} %collective-permute-done.12.score_theirs), custom_call_target="tpu_custom_call" | custom-call | flops 2147483648 | bytes 7340032 | tf_op jit(solution)/shard_map/pallas_call | solution.py:52
  87.5 2.4 %collective-permute-done.10 = bf16[512,256]{1,0:T(8,128)(2,1)S(1)} collective-permute-done((bf16[512,256]{1,0:T(8,128)(2,1)S(1)}, bf16[512,256]{1,0:T(8,128)(2,1)S(1)}, u32[]{:S(2)}, u32[]{:S(2)}) %collective-permute-start.10) | collective-permute-done | bytes 262176 | tf_op jit(solution)/shard_map/ppermute | solution.py:37
  89.9 1.3 %collective-permute-done.9 = bf16[512,256]{1,0:T(8,128)(2,1)S(1)} collective-permute-done((bf16[512,256]{1,0:T(8,128)(2,1)S(1)}, bf16[512,256]{1,0:T(8,128)(2,1)S(1)}, u32[]{:S(2)}, u32[]{:S(2)}) %collective-permute-start.9) | collective-permute-done | bytes 262176 | tf_op jit(solution)/shard_map/ppermute | solution.py:37
  91.2 1.5 %collective-permute-done.7 = bf16[1024,256]{1,0:T(8,128)(2,1)S(1)} collective-permute-done((bf16[1024,256]{1,0:T(8,128)(2,1)S(1)}, bf16[1024,256]{1,0:T(8,128)(2,1)S(1)}, u32[]{:S(2)}, u32[]{:S(2)}) %collective-permute-start.7) | collective-permute-done | bytes 524320 | tf_op jit(solution)/shard_map/ppermute | solution.py:37
  92.7 1.1 collective-permute-done.8
  93.9 0.2 add_convert_fusion
  94.1 24.2 %all_to_all.17 = bf16[32,32,256]{2,1,0:T(8,128)(2,1)S(1)} all-to-all(bf16[32,32,256]{2,1,0:T(8,128)(2,1)S(1)} %bitcast.14), channel_id=1, replica_groups={{0,2,4,6,8,10,12,14,96,98,100,102,104,106,108,110,128,130,132,134,136,1..., dimensions={0} | all-to-all | bytes 1048576 | tf_op jit(solution)/shard_map/all_to_all | solution.py:27
  118.3 0.7 reduce_sum.12
  (3 shorter events, 0.1 us)
Async XLA Ops:
  33.3 10.8 %collective-permute-start = (bf16[1024,256]{1,0:T(8,128)(2,1)S(1)}, bf16[1024,256]{1,0:T(8,128)(2,1)S(1)}, u32[]{:S(2)}, u32[]{:S(2)}) collective-permute-start(bf16[1024,256]{1,0:T(8,128)(2,1)S(1)} %bitcast.11), channel_id=1, source_target_pairs={{0,48},{2,50},{4,52},{6,54},{8,56},{10,58},{12,60},{14,62},{16,0},... | collective-permute-start | bytes 1572872 | tf_op jit(solution)/shard_map/ppermute | solution.py:37
  34.8 10.6 %collective-permute-start.1 = (bf16[1024,256]{1,0:T(8,128)(2,1)S(1)}, bf16[1024,256]{1,0:T(8,128)(2,1)S(1)}, u32[]{:S(2)}, u32[]{:S(2)}) collective-permute-start(bf16[1024,256]{1,0:T(8,128)(2,1)S(1)} %bitcast.12), channel_id=1, source_target_pairs={{0,16},{2,18},{4,20},{6,22},{8,24},{10,26},{12,28},{14,30},{16,32}... | collective-permute-start | bytes 1572872 | tf_op jit(solution)/shard_map/ppermute | solution.py:37
  35.4 8.2 %collective-permute-start.2 = (bf16[512,256]{1,0:T(8,128)(2,1)S(1)}, bf16[512,256]{1,0:T(8,128)(2,1)S(1)}, u32[]{:S(2)}, u32[]{:S(2)}) collective-permute-start(bf16[512,256]{1,0:T(8,128)(2,1)S(1)} %bitcast.16), channel_id=1, source_target_pairs={{0,64},{2,66},{4,68},{6,70},{8,72},{10,74},{12,76},{14,78},{16,80}... | collective-permute-start | bytes 786440 | tf_op jit(solution)/shard_map/ppermute | solution.py:37
  35.5 8.1 %collective-permute-start.3 = (bf16[512,256]{1,0:T(8,128)(2,1)S(1)}, bf16[512,256]{1,0:T(8,128)(2,1)S(1)}, u32[]{:S(2)}, u32[]{:S(2)}) collective-permute-start(bf16[512,256]{1,0:T(8,128)(2,1)S(1)} %bitcast.15), channel_id=1, source_target_pairs={{0,192},{2,194},{4,196},{6,198},{8,200},{10,202},{12,204},{14,206}... | collective-permute-start | bytes 786440 | tf_op jit(solution)/shard_map/ppermute | solution.py:37
  38.7 3.4 %copy-start = (bf16[4096,1024]{1,0:T(8,128)(2,1)S(1)}, bf16[4096,1024]{1,0:T(8,128)(2,1)}, u32[]{:S(2)}) copy-start(bf16[4096,1024]{1,0:T(8,128)(2,1)} %head.7) | copy-start | bytes 25165828
  42.1 1.0 copy-start.1
  43.1 32.9 %slice-start = ((s8[8388608]{0:T(1024)(128)(4,1)}), s8[4194304]{0:T(1024)(128)(4,1)S(1)}, s32[]{:S(2)}) async-start(s8[8388608]{0:T(1024)(128)(4,1)} %bitcast.9), calls=%async_computation.3 | async-start | bytes 8388608
  45.3 30.7 %slice-start.1 = ((s8[8388608]{0:T(1024)(128)(4,1)}), s8[4194304]{0:T(1024)(128)(4,1)S(1)}, s32[]{:S(2)}) async-start(s8[8388608]{0:T(1024)(128)(4,1)} %bitcast.9), calls=%async_computation.4 | async-start | bytes 8388608
  48.5 4.0 %collective-permute-start.4 = (f32[8,128]{1,0:T(8,128)S(1)}, f32[8,128]{1,0:T(8,128)S(1)}, u32[]{:S(2)}, u32[]{:S(2)}) collective-permute-start(f32[8,128]{1,0:T(8,128)S(1)} %get-tuple-element.29.first), channel_id=1, source_target_pairs={{0,16},{2,18},{4,20},{6,22},{8,24},{10,26},{12,28},{14,30},{16,32}... | collective-permute-start | bytes 12296 | tf_op jit(solution)/shard_map/ppermute | solution.py:37
  49.2 3.6 %collective-permute-start.5 = (f32[8,128]{1,0:T(8,128)S(1)}, f32[8,128]{1,0:T(8,128)S(1)}, u32[]{:S(2)}, u32[]{:S(2)}) collective-permute-start(f32[8,128]{1,0:T(8,128)S(1)} %get-tuple-element.29.first), channel_id=1, source_target_pairs={{0,48},{2,50},{4,52},{6,54},{8,56},{10,58},{12,60},{14,62},{16,0},... | collective-permute-start | bytes 12296 | tf_op jit(solution)/shard_map/ppermute | solution.py:37
  51.0 4.8 %collective-permute-start.6 = (f32[8,128]{1,0:T(8,128)S(1)}, f32[8,128]{1,0:T(8,128)S(1)}, u32[]{:S(2)}, u32[]{:S(2)}) collective-permute-start(f32[8,128]{1,0:T(8,128)S(1)} %get-tuple-element.29.first), channel_id=1, source_target_pairs={{0,64},{2,66},{4,68},{6,70},{8,72},{10,74},{12,76},{14,78},{16,80}... | collective-permute-start | bytes 12296 | tf_op jit(solution)/shard_map/ppermute | solution.py:37
  76.0 8.3 %collective-permute-start.11 = (bf16[2048,256]{1,0:T(8,128)(2,1)S(1)}, bf16[2048,256]{1,0:T(8,128)(2,1)S(1)}, u32[]{:S(2)}, u32[]{:S(2)}) collective-permute-start(bf16[2048,256]{1,0:T(8,128)(2,1)S(1)} %get-tuple-element.39), channel_id=1, source_target_pairs={{0,1},{1,0},{2,3},{3,2},{4,5},{5,4},{6,7},{7,6},{8,9},{9,8},{10,11... | collective-permute-start | bytes 3145736 | tf_op jit(solution)/shard_map/ppermute | solution.py:41
  78.4 4.2 %collective-permute-start.12 = (bf16[256,1024]{1,0:T(8,128)(2,1)S(1)}, bf16[256,1024]{1,0:T(8,128)(2,1)S(1)}, u32[]{:S(2)}, u32[]{:S(2)}) collective-permute-start(bf16[256,1024]{1,0:T(8,128)(2,1)S(1)} %get-tuple-element.40.score), channel_id=1, source_target_pairs={{0,1},{1,0},{2,3},{3,2},{4,5},{5,4},{6,7},{7,6},{8,9},{9,8},{10,11... | collective-permute-start | bytes 1572872 | tf_op jit(solution)/shard_map/ppermute | solution.py:41
  78.9 13.8 %collective-permute-start.7 = (bf16[1024,256]{1,0:T(8,128)(2,1)S(1)}, bf16[1024,256]{1,0:T(8,128)(2,1)S(1)}, u32[]{:S(2)}, u32[]{:S(2)}) collective-permute-start(bf16[1024,256]{1,0:T(8,128)(2,1)S(1)} %get-tuple-element.34), channel_id=1, source_target_pairs={{0,16},{2,18},{4,20},{6,22},{8,24},{10,26},{12,28},{14,30},{16,32}... | collective-permute-start | bytes 1572872 | tf_op jit(solution)/shard_map/ppermute | solution.py:37
  80.3 13.6 %collective-permute-start.8 = (bf16[1024,256]{1,0:T(8,128)(2,1)S(1)}, bf16[1024,256]{1,0:T(8,128)(2,1)S(1)}, u32[]{:S(2)}, u32[]{:S(2)}) collective-permute-start(bf16[1024,256]{1,0:T(8,128)(2,1)S(1)} %get-tuple-element.35), channel_id=1, source_target_pairs={{0,48},{2,50},{4,52},{6,54},{8,56},{10,58},{12,60},{14,62},{16,0},... | collective-permute-start | bytes 1572872 | tf_op jit(solution)/shard_map/ppermute | solution.py:37
  82.2 7.7 %collective-permute-start.10 = (bf16[512,256]{1,0:T(8,128)(2,1)S(1)}, bf16[512,256]{1,0:T(8,128)(2,1)S(1)}, u32[]{:S(2)}, u32[]{:S(2)}) collective-permute-start(bf16[512,256]{1,0:T(8,128)(2,1)S(1)} %get-tuple-element.37), channel_id=1, source_target_pairs={{0,192},{2,194},{4,196},{6,198},{8,200},{10,202},{12,204},{14,206}... | collective-permute-start | bytes 786440 | tf_op jit(solution)/shard_map/ppermute | solution.py:37
  82.6 8.7 %collective-permute-start.9 = (bf16[512,256]{1,0:T(8,128)(2,1)S(1)}, bf16[512,256]{1,0:T(8,128)(2,1)S(1)}, u32[]{:S(2)}, u32[]{:S(2)}) collective-permute-start(bf16[512,256]{1,0:T(8,128)(2,1)S(1)} %get-tuple-element.36), channel_id=1, source_target_pairs={{0,64},{2,66},{4,68},{6,70},{8,72},{10,74},{12,76},{14,78},{16,80}... | collective-permute-start | bytes 786440 | tf_op jit(solution)/shard_map/ppermute | solution.py:37

commit v5 on v4

--- a/solution.py
+++ b/solution.py
@@ -18,32 +18,46 @@
     return ((y % NY) * NX + x % NX) * NZ + z % NZ
 
 
+BOTH = ("vocab", "rows")
+
+
+def spot(along, across, z, core):
+    return place(*((across, along) if core == 0 else (along, across)), z) * 2 + core
+
+
 class_groups = [
-    [place(y, c - 2 * y, z) for y in range(NY) for z in range(NZ)] for c in range(4)
+    [spot((c - 2 * across) % 4, across, z, core) for across in range(4) for z in range(NZ)]
+    for core in range(2)
+    for c in range(4)
 ]
 
 
-def trade(chunks, groups):
-    return lax.all_to_all(chunks, "vocab", 0, 0, tiled=True, axis_index_groups=groups)
-
-
-def step(value, dy, dx):
+def trade(chunks):
+    return lax.all_to_all(chunks, BOTH, 0, 0, tiled=True, axis_index_groups=class_groups)
+
+
+def step(value, across_by, along_by):
     pairs = [
-        (place(y, x, z), place(y + dy, x + dx, z))
-        for y in range(NY)
-        for x in range(NX)
+        (spot(along, across, z, core), spot(along + along_by, across + across_by, z, core))
+        for along in range(4)
+        for across in range(4)
         for z in range(NZ)
+        for core in range(2)
     ]
-    return lax.ppermute(value, "vocab", pairs)
+    return lax.ppermute(value, BOTH, pairs)
 
 
 def other_core(value):
     return lax.ppermute(value, "rows", [(0, 1), (1, 0)])
 
 
-def slab_row(own, offset, j):
-    slab = 4 * j + lax.rem(own + offset - 2 * j + 8, 4)
-    return pl.multiple_of(slab * SLAB, SLAB)
+def slab_of(own, core, offset, j):
+    k = lax.rem(own[0] + offset - 2 * j + 8, 4)
+    return (4 - 3 * core[0]) * j + (1 + 3 * core[0]) * k
+
+
+def slab_row(own, core, offset, j):
+    return pl.multiple_of(slab_of(own, core, offset, j) * SLAB, SLAB)
 
 
 def call(body, outs, ins, flops, traffic, scratch=(), limit=8, into="v"):
@@ -73,15 +87,15 @@
 ):
     for offset, ref, first, count in [(0, a, 0, 4), (1, b, 0, 4), (3, c, 0, 4), (2, d0, 0, 2), (2, d1, 2, 2)]:
         for i in range(count):
-            j = first + i
-            slab = 4 * (j % 2) + lax.rem(own[0] + offset - 2 * j + 8, 4)
-            rows = pl.ds(pl.multiple_of(slab * SLAB, SLAB), SLAB)
-
-            @pl.when(core[0] == j // 2)
+            slab = slab_of(own, core, offset, first + i)
+            half = lax.shift_right_logical(slab, 3)
+            rows = pl.ds(pl.multiple_of((slab - 8 * half) * SLAB, SLAB), SLAB)
+
+            @pl.when(core[0] == half)
             def _(ref=ref, rows=rows, i=i):
                 mine[rows] = ref[pl.ds(i * SLAB, SLAB)]
 
-            @pl.when(core[0] != j // 2)
+            @pl.when(core[0] != half)
             def _(ref=ref, rows=rows, i=i):
                 theirs[rows] = ref[pl.ds(i * SLAB, SLAB)]
 
@@ -105,7 +119,7 @@
     columns = jnp.where(lane == 0, lse_s, jnp.where(lane == 1, lse_t[...], cross))
     flat = jnp.transpose(columns)
     lines = [flat[i : i + 1, h * 128 : (h + 1) * 128] for i in range(3) for h in range(2)]
-    stats[...] = jnp.concatenate(lines + lines[:2], axis=0)
+    stats[...] = jnp.concatenate(lines, axis=0)
 
 
 def as_columns(first, second):
@@ -125,17 +139,17 @@
 
 def merge_kernel(first, second, third, fourth, stats):
     all_s, all_t, cross = merged(jnp.stack([r[...] for r in (first, second, third, fourth)]))
-    chunk = jnp.concatenate([all_s, all_t, cross, cross], axis=0)
+    chunk = jnp.concatenate([all_s, all_t, cross], axis=0)
     stats[...] = jnp.broadcast_to(chunk[None], stats.shape)
 
 
-def times_head(own, head, score_t, outs):
+def times_head(own, core, head, score_t, outs):
     for offset, j, ref in outs:
-        rows = pl.ds(slab_row(own[0], offset, j), SLAB)
+        rows = pl.ds(slab_row(own, core, offset, j), SLAB)
         ref[...] = jnp.dot(head[rows], score_t, preferred_element_type=f32).astype(ref.dtype)
 
 
-def score_kernel(own, rise, peak, prob, lse_t, stats, head, score, score_t, b, c, mismatch):
+def score_kernel(own, core, rise, peak, prob, lse_t, stats, head, score, score_t, b, c, mismatch):
     all_s, all_t, cross = merged(stats[...])
     mismatch[...] = sharpness_divisor * sharpness_divisor * (cross + all_s - all_t)
     end_s, end_t = as_columns(all_s, all_t)
@@ -146,13 +160,13 @@
     score[...] = rounded
     score_t[...] = jnp.transpose(rounded)
     outs = [(o, j, r.at[pl.ds(j * SLAB, SLAB)]) for o, r in ((1, b), (3, c)) for j in range(4)]
-    times_head(own, head, score_t[...], outs)
-
-
-def rest_kernel(own, score_t, head, d0, d1, a):
+    times_head(own, core, head, score_t[...], outs)
+
+
+def rest_kernel(own, core, score_t, head, d0, d1, a):
     outs = [(2, j, (d0, d1)[j // 2].at[pl.ds((j % 2) * SLAB, SLAB)]) for j in range(4)]
     outs += [(0, j, a.at[pl.ds(j * SLAB, SLAB)]) for j in range(4)]
-    times_head(own, head, score_t[...], outs)
+    times_head(own, core, head, score_t[...], outs)
 
 
 def weight_kernel(mine, theirs, score, score_theirs, out, held, sems):
@@ -172,17 +186,19 @@
 def stats_of_all(stats):
     near = [stats, step(stats, 0, 1), step(stats, 0, -1), step(stats, 1, 0)]
     (stats,) = call(
-        merge_kernel, [((32, 8, 128), f32)], [("v", value) for value in near], 1000, 1000
-    )
-    return trade(stats, class_groups)
+        merge_kernel, [((32, 6, 128), f32)], [("v", value) for value in near], 1000, 1000
+    )
+    return trade(stats)
 
 
 def shards(hidden, head_weight, mentor_outputs):
     here = lax.axis_index("vocab")
-    core = lax.axis_index("rows").astype(jnp.int32)[None]
-    own = lax.rem(here // NZ % NX + 2 * (here // (NZ * NX)), 4).astype(jnp.int32)[None]
-
-    a = trade(jnp.broadcast_to(hidden.T[None], (32, 32, ROWS)), class_groups).reshape(1024, ROWS)
+    core = lax.axis_index("rows").astype(jnp.int32)
+    x, y = lax.rem(lax.div(here, NZ), NX), lax.div(here, NZ * NX)
+    own = lax.rem(jnp.where(core == 0, x + 2 * y, y + 2 * x), 4).astype(jnp.int32)[None]
+    core = core[None]
+
+    a = trade(jnp.broadcast_to(hidden.T[None], (32, 32, ROWS))).reshape(1024, ROWS)
     prob, lse_t = call(
         target_kernel,
         [((ROWS, COLS), f32), ((ROWS, 128), f32)],
@@ -195,7 +211,7 @@
 
     rise, peak, stats, mine, theirs = call(
         student_kernel,
-        [((ROWS, COLS), f32), ((ROWS, 128), f32), ((8, 128), f32)] + [((FULL // 2, ROWS), bf16)] * 2,
+        [((ROWS, COLS), f32), ((ROWS, 128), f32), ((6, 128), f32)] + [((FULL // 2, ROWS), bf16)] * 2,
         [("s", own), ("s", core), ("v", a), ("v", b), ("v", c), ("v", d0), ("v", d1), ("v", head_weight)]
         + [("v", mentor_outputs), ("v", prob), ("v", lse_t)],
         2 * FULL * ROWS * COLS,
@@ -207,7 +223,7 @@
     score, score_t, b, c, mismatch = call(
         score_kernel,
         [((ROWS, COLS), bf16), ((COLS, ROWS), bf16)] + [((1024, ROWS), bf16)] * 2 + [((2, 128), f32)],
-        [("s", own), ("v", rise), ("v", peak), ("v", prob), ("v", lse_t), ("v", stats), ("v", head_weight)],
+        [("s", own), ("s", core), ("v", rise), ("v", peak), ("v", prob), ("v", lse_t), ("v", stats), ("v", head_weight)],
         FULL * ROWS * COLS,
         8 * MIB,
     )
@@ -216,7 +232,7 @@
     d0, d1, a = call(
         rest_kernel,
         [((512, ROWS), bf16), ((512, ROWS), bf16), ((1024, ROWS), f32)],
-        [("s", own), ("v", score_t), ("v", head_weight)],
+        [("s", own), ("s", core), ("v", score_t), ("v", head_weight)],
         FULL * ROWS * COLS,
         7 * MIB,
     )
@@ -232,7 +248,7 @@
     )
     b, c, d0, d1, weight_grad = lax.optimization_barrier((b, c, d0, d1, weight_grad))
     part = a + b.astype(f32) + c.astype(f32) + jnp.concatenate([d0, d1], axis=0).astype(f32)
-    part = trade(part.astype(bf16).reshape(32, 32, ROWS), class_groups)
+    part = trade(part.astype(bf16).reshape(32, 32, ROWS))
     hidden_grad = jnp.sum(part.astype(f32), axis=0).astype(bf16).T
     return (hidden_grad, weight_grad, mismatch.reshape(ROWS))
 

time: 119 us -> 116 us (0.975)
  waiting for transfers between devices: 12.9 us -> 11.1 us
  blocking collectives: 76.3 us -> 74.5 us
    ppermute x11, waiting for transfers between devices: 12.9 us -> 11.1 us  [step(): return lax.ppermute(value, BOTH, pairs)]
    all_to_all x3, blocking collectives: 76.3 us -> 74.5 us  [trade(): lax.all_to_all(chunks, BOTH, 0, 0, tiled=True, axis_index_groups=class_gr...]
  transfers between devices with their start and end apart: 13 -> 13, of which waited for: 9 -> 7; matrix products, arithmetic and copies ran while one was open for 0% -> 0% of each run, Pallas kernels for 6% -> 6%
where the time goes in v5:
time: 116 us
  blocking collectives  74.5 us (64%)
  starting transfers between devices  12.9 us (11%)
  waiting for transfers between devices  11.1 us (10%)
  Pallas kernels  10.5 us (9%)
  local copies, waits for them, and re-layouts  5.23 us (5%)
    all_to_all x3, blocking collectives, trade(): lax.all_to_all(chunks, BOTH, 0, 0, tiled=True, axis_index_groups=class_gr...  74.5 us
    ppermute x11, starting transfers between devices, step(): return lax.ppermute(value, BOTH, pairs)  12.4 us
    ppermute x11, waiting for transfers between devices, step(): return lax.ppermute(value, BOTH, pairs)  11.1 us
    pallas_call x6, Pallas kernels, call(): pl.pallas_call(body, out_shape=[jax.ShapeDtypeStruct(shape, dtype) for sh...  10.5 us
    unnamed x8, local copies, waits for them, and re-layouts  4.43 us
  transfers between devices with their start and end apart: 13, of which 7 were waited for; matrix products, arithmetic and copies ran while one was open for 0% of the time, Pallas kernels for 6%

profile of v5, /device:TPU:2, one launch (start us, length us, event | category | flops | bytes accessed | tf_op | source)
XLA Modules:
  0.0 115.9 jit_solution(4779936972479029466)
XLA Ops:
  0.6 0.8 broadcast_in_dim.14
  1.4 31.9 %all_to_all.15 = bf16[32,32,256]{2,1,0:T(8,128)(2,1)S(1)} all-to-all(bf16[32,32,256]{2,1,0:T(8,128)(2,1)S(1)} %broadcast_in_dim.14), channel_id=1, replica_groups={{0,2,4,6,8,10,12,14,96,98,100,102,104,106,108,110,128,130,132,134,136,1..., dimensions={0} | all-to-all | bytes 1048576 | tf_op jit(solution)/shard_map/all_to_all | solution.py:36
  33.3 0.0 collective-permute-start
  33.3 2.0 %collective-permute-start.1 = (bf16[1024,256]{1,0:T(8,128)(2,1)S(1)}, bf16[1024,256]{1,0:T(8,128)(2,1)S(1)}, u32[]{:S(2)}, u32[]{:S(2)}) collective-permute-start(bf16[1024,256]{1,0:T(8,128)(2,1)S(1)} %bitcast.12), channel_id=1, source_target_pairs={{0,16},{1,65},{2,18},{3,67},{4,20},{5,69},{6,22},{7,71},{8,24},{9,... | collective-permute-start | bytes 1572872 | tf_op jit(solution)/shard_map/ppermute | solution.py:47
  35.4 0.1 collective-permute-start.2
  35.5 3.2 %collective-permute-start.3 = (bf16[512,256]{1,0:T(8,128)(2,1)S(1)}, bf16[512,256]{1,0:T(8,128)(2,1)S(1)}, u32[]{:S(2)}, u32[]{:S(2)}) collective-permute-start(bf16[512,256]{1,0:T(8,128)(2,1)S(1)} %bitcast.15), channel_id=1, source_target_pairs={{0,192},{1,49},{2,194},{3,51},{4,196},{5,53},{6,198},{7,55},{8,200... | collective-permute-start | bytes 786440 | tf_op jit(solution)/shard_map/ppermute | solution.py:47
  38.7 0.0 copy-start
  38.7 3.4 %copy-done = bf16[4096,1024]{1,0:T(8,128)(2,1)S(1)} copy-done((bf16[4096,1024]{1,0:T(8,128)(2,1)S(1)}, bf16[4096,1024]{1,0:T(8,128)(2,1)}, u32[]{:S(2)}) %copy-start) | copy-done | bytes 8388632
  42.1 0.0 copy-start.1
  42.1 1.0 copy-done.1
  43.1 0.0 slice-start
  43.1 0.4 shard_map.58
  43.6 0.0 collective-permute-done.2.d0
  43.6 0.0 collective-permute-done.3.d1
  43.6 1.8 %collective-permute-done.b = bf16[1024,256]{1,0:T(8,128)(2,1)S(1)} collective-permute-done((bf16[1024,256]{1,0:T(8,128)(2,1)S(1)}, bf16[1024,256]{1,0:T(8,128)(2,1)S(1)}, u32[]{:S(2)}, u32[]{:S(2)}) %collective-permute-start) | collective-permute-done | bytes 524320 | tf_op jit(solution)/shard_map/ppermute | solution.py:47
  45.3 0.0 collective-permute-done.1.c
  45.3 0.0 slice-start.1
  45.3 3.2 %shard_map.59 = (f32[256,1024]{1,0:T(8,128)S(1)}, f32[256,128]{1,0:T(8,128)S(1)}, f32[6,128]{1,0:T(8,128)S(1)}, bf16[2048,256]{1,0:T(8,128)(2,1)S(1)}, bf16[2048,256]{1,0:T(8,128)(2,1)S(1)}) custom-call(s32[1]{0:T(128)} %bitcast.own, s32[1]{0:T(128)} %bitcast.1.core, bf16[1024,256]{1,0:T(8,128)(2,1)S(1)} %bitcast.13, ...), custom_call_target="tpu_custom_call" | custom-call | flops 2147483648 | bytes 12582912 | tf_op jit(solution)/shard_map/pallas_call | solution.py:66
  48.6 0.9 collective-permute-start.4
  49.4 1.8 %collective-permute-start.5 = (f32[6,128]{1,0:T(8,128)S(1)}, f32[6,128]{1,0:T(8,128)S(1)}, u32[]{:S(2)}, u32[]{:S(2)}) collective-permute-start(f32[6,128]{1,0:T(8,128)S(1)} %get-tuple-element.29.first), channel_id=1, source_target_pairs={{0,48},{1,193},{2,50},{3,195},{4,52},{5,197},{6,54},{7,199},{8,56}... | collective-permute-start | bytes 9224 | tf_op jit(solution)/shard_map/ppermute | solution.py:47
  51.3 0.3 collective-permute-start.6
  51.5 1.2 %collective-permute-done.4.second = f32[6,128]{1,0:T(8,128)S(1)} collective-permute-done((f32[6,128]{1,0:T(8,128)S(1)}, f32[6,128]{1,0:T(8,128)S(1)}, u32[]{:S(2)}, u32[]{:S(2)}) %collective-permute-start.4) | collective-permute-done | bytes 3104 | tf_op jit(solution)/shard_map/ppermute | solution.py:47
  52.8 0.5 collective-permute-done.5.third
  53.2 2.9 %collective-permute-done.6.fourth = f32[6,128]{1,0:T(8,128)S(1)} collective-permute-done((f32[6,128]{1,0:T(8,128)S(1)}, f32[6,128]{1,0:T(8,128)S(1)}, u32[]{:S(2)}, u32[]{:S(2)}) %collective-permute-start.6) | collective-permute-done | bytes 3104 | tf_op jit(solution)/shard_map/ppermute | solution.py:47
  56.1 18.6 %all_to_all.16.stats = f32[32,6,128]{2,1,0:T(8,128)S(1)} all-to-all(f32[32,6,128]{2,1,0:T(8,128)S(1)} %shard_map.60), channel_id=1, replica_groups={{0,2,4,6,8,10,12,14,96,98,100,102,104,106,108,110,128,130,132,134,136,1..., dimensions={0} | all-to-all | bytes 196608 | tf_op jit(solution)/shard_map/all_to_all | solution.py:36
  74.7 0.0 collective-permute-start.11
  74.7 0.0 slice-done
  74.7 0.0 slice-done.1
  74.8 2.4 %shard_map.61 = (bf16[256,1024]{1,0:T(8,128)(2,1)S(1)}, bf16[1024,256]{1,0:T(8,128)(2,1)S(1)}, bf16[1024,256]{1,0:T(8,128)(2,1)S(1)}, bf16[1024,256]{1,0:T(8,128)(2,1)S(1)}, f32[2,128]{1,0:T(2,128)}) custom-call(s32[1]{0:T(128)} %bitcast.own, s32[1]{0:T(128)} %bitcast.1.core, f32[256,1024]{1,0:T(8,128)S(1)} %get-tuple-element.27.rise, ...), custom_call_target="tpu_custom_call" | custom-call | flops 1073741824 | bytes 8388608 | tf_op jit(solution)/shard_map/pallas_call | solution.py:66
  77.1 0.5 collective-permute-start.12
  77.6 1.4 %collective-permute-start.7 = (bf16[1024,256]{1,0:T(8,128)(2,1)S(1)}, bf16[1024,256]{1,0:T(8,128)(2,1)S(1)}, u32[]{:S(2)}, u32[]{:S(2)}) collective-permute-start(bf16[1024,256]{1,0:T(8,128)(2,1)S(1)} %get-tuple-element.34), channel_id=1, source_target_pairs={{0,16},{1,65},{2,18},{3,67},{4,20},{5,69},{6,22},{7,71},{8,24},{9,... | collective-permute-start | bytes 1572872 | tf_op jit(solution)/shard_map/ppermute | solution.py:47
  79.1 0.6 collective-permute-start.8
  79.7 1.3 %shard_map.62 = (bf16[512,256]{1,0:T(8,128)(2,1)S(1)}, bf16[512,256]{1,0:T(8,128)(2,1)S(1)}, f32[1024,256]{1,0:T(8,128)S(1)}) custom-call(s32[1]{0:T(128)} %bitcast.own, s32[1]{0:T(128)} %bitcast.1.core, bf16[1024,256]{1,0:T(8,128)(2,1)S(1)} %get-tuple-element.32.score_t, bf16[4096,1024]{1,0:T(8,128)(2,1)S(1)} %bitcast.10), custom_call_target="tpu_custom_call" | custom-call | flops 1073741824 | bytes 7340032 | tf_op jit(solution)/shard_map/pallas_call | solution.py:66
  80.9 0.1 collective-permute-start.10
  81.0 0.0 collective-permute-done.12.score_theirs
  81.0 2.0 %collective-permute-start.9 = (bf16[512,256]{1,0:T(8,128)(2,1)S(1)}, bf16[512,256]{1,0:T(8,128)(2,1)S(1)}, u32[]{:S(2)}, u32[]{:S(2)}) collective-permute-start(bf16[512,256]{1,0:T(8,128)(2,1)S(1)} %get-tuple-element.36), channel_id=1, source_target_pairs={{0,64},{1,17},{2,66},{3,19},{4,68},{5,21},{6,70},{7,23},{8,72},{9,... | collective-permute-start | bytes 786440 | tf_op jit(solution)/shard_map/ppermute | solution.py:47
  83.0 0.0 collective-permute-done.11.theirs
  83.0 3.2 %shard_map.63 = bf16[2048,1024]{1,0:T(8,128)(2,1)} custom-call(bf16[2048,256]{1,0:T(8,128)(2,1)S(1)} %get-tuple-element.38.mine, bf16[2048,256]{1,0:T(8,128)(2,1)S(1)} %collective-permute-done.11.theirs, bf16[256,1024]{1,0:T(8,128)(2,1)S(1)} %get-tuple-element.40.score, bf16[256,1024]{1,0:T(8,128)(2,1)S(1)} %collective-permute-done.12.score_theirs), custom_call_target="tpu_custom_call" | custom-call | flops 2147483648 | bytes 7340032 | tf_op jit(solution)/shard_map/pallas_call | solution.py:66
  86.3 2.4 %collective-permute-done.10 = bf16[512,256]{1,0:T(8,128)(2,1)S(1)} collective-permute-done((bf16[512,256]{1,0:T(8,128)(2,1)S(1)}, bf16[512,256]{1,0:T(8,128)(2,1)S(1)}, u32[]{:S(2)}, u32[]{:S(2)}) %collective-permute-start.10) | collective-permute-done | bytes 262176 | tf_op jit(solution)/shard_map/ppermute | solution.py:47
  88.7 1.2 %collective-permute-done.9 = bf16[512,256]{1,0:T(8,128)(2,1)S(1)} collective-permute-done((bf16[512,256]{1,0:T(8,128)(2,1)S(1)}, bf16[512,256]{1,0:T(8,128)(2,1)S(1)}, u32[]{:S(2)}, u32[]{:S(2)}) %collective-permute-start.9) | collective-permute-done | bytes 262176 | tf_op jit(solution)/shard_map/ppermute | solution.py:47
  89.9 0.0 collective-permute-done.7
  89.9 1.2 %collective-permute-done.8 = bf16[1024,256]{1,0:T(8,128)(2,1)S(1)} collective-permute-done((bf16[1024,256]{1,0:T(8,128)(2,1)S(1)}, bf16[1024,256]{1,0:T(8,128)(2,1)S(1)}, u32[]{:S(2)}, u32[]{:S(2)}) %collective-permute-start.8) | collective-permute-done | bytes 524320 | tf_op jit(solution)/shard_map/ppermute | solution.py:47
  91.0 0.2 add_convert_fusion
  91.3 24.0 %all_to_all.17 = bf16[32,32,256]{2,1,0:T(8,128)(2,1)S(1)} all-to-all(bf16[32,32,256]{2,1,0:T(8,128)(2,1)S(1)} %bitcast.14), channel_id=1, replica_groups={{0,2,4,6,8,10,12,14,96,98,100,102,104,106,108,110,128,130,132,134,136,1..., dimensions={0} | all-to-all | bytes 1048576 | tf_op jit(solution)/shard_map/all_to_all | solution.py:36
  115.2 0.7 reduce_sum.12
  (3 shorter events, 0.1 us)
Async XLA Ops:
  33.3 12.0 %collective-permute-start = (bf16[1024,256]{1,0:T(8,128)(2,1)S(1)}, bf16[1024,256]{1,0:T(8,128)(2,1)S(1)}, u32[]{:S(2)}, u32[]{:S(2)}) collective-permute-start(bf16[1024,256]{1,0:T(8,128)(2,1)S(1)} %bitcast.11), channel_id=1, source_target_pairs={{0,48},{1,193},{2,50},{3,195},{4,52},{5,197},{6,54},{7,199},{8,56}... | collective-permute-start | bytes 1572872 | tf_op jit(solution)/shard_map/ppermute | solution.py:47
  33.3 12.0 %collective-permute-start.1 = (bf16[1024,256]{1,0:T(8,128)(2,1)S(1)}, bf16[1024,256]{1,0:T(8,128)(2,1)S(1)}, u32[]{:S(2)}, u32[]{:S(2)}) collective-permute-start(bf16[1024,256]{1,0:T(8,128)(2,1)S(1)} %bitcast.12), channel_id=1, source_target_pairs={{0,16},{1,65},{2,18},{3,67},{4,20},{5,69},{6,22},{7,71},{8,24},{9,... | collective-permute-start | bytes 1572872 | tf_op jit(solution)/shard_map/ppermute | solution.py:47
  35.4 8.2 %collective-permute-start.2 = (bf16[512,256]{1,0:T(8,128)(2,1)S(1)}, bf16[512,256]{1,0:T(8,128)(2,1)S(1)}, u32[]{:S(2)}, u32[]{:S(2)}) collective-permute-start(bf16[512,256]{1,0:T(8,128)(2,1)S(1)} %bitcast.16), channel_id=1, source_target_pairs={{0,64},{1,17},{2,66},{3,19},{4,68},{5,21},{6,70},{7,23},{8,72},{9,... | collective-permute-start | bytes 786440 | tf_op jit(solution)/shard_map/ppermute | solution.py:47
  35.5 8.1 %collective-permute-start.3 = (bf16[512,256]{1,0:T(8,128)(2,1)S(1)}, bf16[512,256]{1,0:T(8,128)(2,1)S(1)}, u32[]{:S(2)}, u32[]{:S(2)}) collective-permute-start(bf16[512,256]{1,0:T(8,128)(2,1)S(1)} %bitcast.15), channel_id=1, source_target_pairs={{0,192},{1,49},{2,194},{3,51},{4,196},{5,53},{6,198},{7,55},{8,200... | collective-permute-start | bytes 786440 | tf_op jit(solution)/shard_map/ppermute | solution.py:47
  38.7 3.4 %copy-start = (bf16[4096,1024]{1,0:T(8,128)(2,1)S(1)}, bf16[4096,1024]{1,0:T(8,128)(2,1)}, u32[]{:S(2)}) copy-start(bf16[4096,1024]{1,0:T(8,128)(2,1)} %head.7) | copy-start | bytes 25165828
  42.1 1.0 copy-start.1
  43.1 31.6 %slice-start = ((s8[8388608]{0:T(1024)(128)(4,1)}), s8[4194304]{0:T(1024)(128)(4,1)S(1)}, s32[]{:S(2)}) async-start(s8[8388608]{0:T(1024)(128)(4,1)} %bitcast.9), calls=%async_computation.3 | async-start | bytes 8388608
  45.3 29.4 %slice-start.1 = ((s8[8388608]{0:T(1024)(128)(4,1)}), s8[4194304]{0:T(1024)(128)(4,1)S(1)}, s32[]{:S(2)}) async-start(s8[8388608]{0:T(1024)(128)(4,1)} %bitcast.9), calls=%async_computation.4 | async-start | bytes 8388608
  48.6 4.2 %collective-permute-start.4 = (f32[6,128]{1,0:T(8,128)S(1)}, f32[6,128]{1,0:T(8,128)S(1)}, u32[]{:S(2)}, u32[]{:S(2)}) collective-permute-start(f32[6,128]{1,0:T(8,128)S(1)} %get-tuple-element.29.first), channel_id=1, source_target_pairs={{0,16},{1,65},{2,18},{3,67},{4,20},{5,69},{6,22},{7,71},{8,24},{9,... | collective-permute-start | bytes 9224 | tf_op jit(solution)/shard_map/ppermute | solution.py:47
  49.4 3.8 %collective-permute-start.5 = (f32[6,128]{1,0:T(8,128)S(1)}, f32[6,128]{1,0:T(8,128)S(1)}, u32[]{:S(2)}, u32[]{:S(2)}) collective-permute-start(f32[6,128]{1,0:T(8,128)S(1)} %get-tuple-element.29.first), channel_id=1, source_target_pairs={{0,48},{1,193},{2,50},{3,195},{4,52},{5,197},{6,54},{7,199},{8,56}... | collective-permute-start | bytes 9224 | tf_op jit(solution)/shard_map/ppermute | solution.py:47
  51.3 4.8 %collective-permute-start.6 = (f32[6,128]{1,0:T(8,128)S(1)}, f32[6,128]{1,0:T(8,128)S(1)}, u32[]{:S(2)}, u32[]{:S(2)}) collective-permute-start(f32[6,128]{1,0:T(8,128)S(1)} %get-tuple-element.29.first), channel_id=1, source_target_pairs={{0,64},{1,17},{2,66},{3,19},{4,68},{5,21},{6,70},{7,23},{8,72},{9,... | collective-permute-start | bytes 9224 | tf_op jit(solution)/shard_map/ppermute | solution.py:47
  74.7 8.3 %collective-permute-start.11 = (bf16[2048,256]{1,0:T(8,128)(2,1)S(1)}, bf16[2048,256]{1,0:T(8,128)(2,1)S(1)}, u32[]{:S(2)}, u32[]{:S(2)}) collective-permute-start(bf16[2048,256]{1,0:T(8,128)(2,1)S(1)} %get-tuple-element.39), channel_id=1, source_target_pairs={{0,1},{1,0},{2,3},{3,2},{4,5},{5,4},{6,7},{7,6},{8,9},{9,8},{10,11... | collective-permute-start | bytes 3145736 | tf_op jit(solution)/shard_map/ppermute | solution.py:51
  77.1 3.9 %collective-permute-start.12 = (bf16[256,1024]{1,0:T(8,128)(2,1)S(1)}, bf16[256,1024]{1,0:T(8,128)(2,1)S(1)}, u32[]{:S(2)}, u32[]{:S(2)}) collective-permute-start(bf16[256,1024]{1,0:T(8,128)(2,1)S(1)} %get-tuple-element.40.score), channel_id=1, source_target_pairs={{0,1},{1,0},{2,3},{3,2},{4,5},{5,4},{6,7},{7,6},{8,9},{9,8},{10,11... | collective-permute-start | bytes 1572872 | tf_op jit(solution)/shard_map/ppermute | solution.py:51
  77.6 12.3 %collective-permute-start.7 = (bf16[1024,256]{1,0:T(8,128)(2,1)S(1)}, bf16[1024,256]{1,0:T(8,128)(2,1)S(1)}, u32[]{:S(2)}, u32[]{:S(2)}) collective-permute-start(bf16[1024,256]{1,0:T(8,128)(2,1)S(1)} %get-tuple-element.34), channel_id=1, source_target_pairs={{0,16},{1,65},{2,18},{3,67},{4,20},{5,69},{6,22},{7,71},{8,24},{9,... | collective-permute-start | bytes 1572872 | tf_op jit(solution)/shard_map/ppermute | solution.py:47
  79.1 12.0 %collective-permute-start.8 = (bf16[1024,256]{1,0:T(8,128)(2,1)S(1)}, bf16[1024,256]{1,0:T(8,128)(2,1)S(1)}, u32[]{:S(2)}, u32[]{:S(2)}) collective-permute-start(bf16[1024,256]{1,0:T(8,128)(2,1)S(1)} %get-tuple-element.35), channel_id=1, source_target_pairs={{0,48},{1,193},{2,50},{3,195},{4,52},{5,197},{6,54},{7,199},{8,56}... | collective-permute-start | bytes 1572872 | tf_op jit(solution)/shard_map/ppermute | solution.py:47
  80.9 7.8 %collective-permute-start.10 = (bf16[512,256]{1,0:T(8,128)(2,1)S(1)}, bf16[512,256]{1,0:T(8,128)(2,1)S(1)}, u32[]{:S(2)}, u32[]{:S(2)}) collective-permute-start(bf16[512,256]{1,0:T(8,128)(2,1)S(1)} %get-tuple-element.37), channel_id=1, source_target_pairs={{0,192},{1,49},{2,194},{3,51},{4,196},{5,53},{6,198},{7,55},{8,200... | collective-permute-start | bytes 786440 | tf_op jit(solution)/shard_map/ppermute | solution.py:47
  81.0 8.8 %collective-permute-start.9 = (bf16[512,256]{1,0:T(8,128)(2,1)S(1)}, bf16[512,256]{1,0:T(8,128)(2,1)S(1)}, u32[]{:S(2)}, u32[]{:S(2)}) collective-permute-start(bf16[512,256]{1,0:T(8,128)(2,1)S(1)} %get-tuple-element.36), channel_id=1, source_target_pairs={{0,64},{1,17},{2,66},{3,19},{4,68},{5,21},{6,70},{7,23},{8,72},{9,... | collective-permute-start | bytes 786440 | tf_op jit(solution)/shard_map/ppermute | solution.py:47

commit v6 on v5

--- a/solution.py
+++ b/solution.py
@@ -32,8 +32,18 @@
 ]
 
 
+z_groups = [[place(y, x, z) for z in range(NZ)] for y in range(NY) for x in range(NX)]
+
+
 def trade(chunks):
     return lax.all_to_all(chunks, BOTH, 0, 0, tiled=True, axis_index_groups=class_groups)
+
+
+def class_of(hidden_t):
+    slab = lax.all_to_all(
+        jnp.broadcast_to(hidden_t[None], (NZ, 32, ROWS)), "vocab", 0, 0, tiled=True, axis_index_groups=z_groups
+    ).reshape(SLAB, ROWS)
+    return jnp.concatenate([slab] + [step(slab, i, -2 * i) for i in (1, 2, 3)], axis=0)
 
 
 def step(value, across_by, along_by):
@@ -83,11 +93,12 @@
 
 
 def student_kernel(
-    own, core, a, b, c, d0, d1, head, mentor, prob, lse_t, rise, peak, stats, mine, theirs
+    own, core, column, a, b, c, d0, d1, head, mentor, prob, lse_t, rise, peak, stats, mine, theirs
 ):
-    for offset, ref, first, count in [(0, a, 0, 4), (1, b, 0, 4), (3, c, 0, 4), (2, d0, 0, 2), (2, d1, 2, 2)]:
+    for offset, ref, shift, count in [(0, a, 0, 4), (1, b, 0, 4), (3, c, 0, 4), (2, d0, -1, 2), (2, d1, 1, 2)]:
         for i in range(count):
-            slab = slab_of(own, core, offset, first + i)
+            j = lax.rem(column[0] + shift - i + 4, 4)
+            slab = slab_of(own, core, offset, j)
             half = lax.shift_right_logical(slab, 3)
             rows = pl.ds(pl.multiple_of((slab - 8 * half) * SLAB, SLAB), SLAB)
 
@@ -198,7 +209,8 @@
     own = lax.rem(jnp.where(core == 0, x + 2 * y, y + 2 * x), 4).astype(jnp.int32)[None]
     core = core[None]
 
-    a = trade(jnp.broadcast_to(hidden.T[None], (32, 32, ROWS))).reshape(1024, ROWS)
+    column = jnp.where(core[0] == 0, y, x).astype(jnp.int32)[None]
+    a = class_of(hidden.T)
     prob, lse_t = call(
         target_kernel,
         [((ROWS, COLS), f32), ((ROWS, 128), f32)],
@@ -207,12 +219,12 @@
         2 * MIB,
     )
     b, c = step(a, 0, -1), step(a, 0, 1)
-    d0, d1 = step(a[:512], 1, 0), step(a[512:], -1, 0)
+    d0, d1 = step(a[:512], 1, 0), step(a[:512], -1, 0)
 
     rise, peak, stats, mine, theirs = call(
         student_kernel,
         [((ROWS, COLS), f32), ((ROWS, 128), f32), ((6, 128), f32)] + [((FULL // 2, ROWS), bf16)] * 2,
-        [("s", own), ("s", core), ("v", a), ("v", b), ("v", c), ("v", d0), ("v", d1), ("v", head_weight)]
+        [("s", own), ("s", core), ("s", column), ("v", a), ("v", b), ("v", c), ("v", d0), ("v", d1), ("v", head_weight)]
         + [("v", mentor_outputs), ("v", prob), ("v", lse_t)],
         2 * FULL * ROWS * COLS,
         12 * MIB,

time: 116 us -> 114 us (0.983)
  blocking collectives: 74.5 us -> 59 us
  starting transfers between devices: 12.9 us -> 22 us
  waiting for transfers between devices: 11.1 us -> 14.9 us
    all_to_all x3 -> x2, blocking collectives: 74.5 us -> 41.6 us  [trade(): lax.all_to_all(chunks, BOTH, 0, 0, tiled=True, axis_index_groups=class_gr...]
    all_to_all x0 -> x1, blocking collectives: none -> 17.4 us  [class_of(): lax.all_to_all(jnp.broadcast_to(hidden_t[None], (NZ, 32, ROWS)), 'vocab',...]
    ppermute x11 -> x14, starting transfers between devices: 12.4 us -> 21.5 us  [step(): return lax.ppermute(value, BOTH, pairs)]
    ppermute x11 -> x14, waiting for transfers between devices: 11.1 us -> 14.9 us  [step(): return lax.ppermute(value, BOTH, pairs)]
  transfers between devices with their start and end apart: 13 -> 16, of which waited for: 7 -> 10; matrix products, arithmetic and copies ran while one was open for 0% -> 0% of each run, Pallas kernels for 6% -> 6%
where the time goes in v6:
time: 114 us; the launch traced here: 113 us
  blocking collectives  59 us (52%)
  starting transfers between devices  22 us (19%)
  waiting for transfers between devices  14.9 us (13%)
  Pallas kernels  10.5 us (9%)
  local copies, waits for them, and re-layouts  5.16 us (5%)
    all_to_all x2, blocking collectives, trade(): lax.all_to_all(chunks, BOTH, 0, 0, tiled=True, axis_index_groups=class_gr...  41.6 us
    ppermute x14, starting transfers between devices, step(): return lax.ppermute(value, BOTH, pairs)  21.5 us
    all_to_all x1, blocking collectives, class_of(): lax.all_to_all(jnp.broadcast_to(hidden_t[None], (NZ, 32, ROWS)), 'vocab',...  17.4 us
    ppermute x14, waiting for transfers between devices, step(): return lax.ppermute(value, BOTH, pairs)  14.9 us
    pallas_call x6, Pallas kernels, call(): pl.pallas_call(body, out_shape=[jax.ShapeDtypeStruct(shape, dtype) for sh...  10.5 us
    unnamed x8, local copies, waits for them, and re-layouts  4.43 us
  transfers between devices with their start and end apart: 16, of which 10 were waited for; matrix products, arithmetic and copies ran while one was open for 0% of the time, Pallas kernels for 6%

profile of v6, /device:TPU:2, one launch (start us, length us, event | category | flops | bytes accessed | tf_op | source)
XLA Modules:
  0.0 113.2 jit_solution(10847479326624695916)
XLA Ops:
  0.6 0.7 broadcast_in_dim.18
  1.4 17.4 %all_to_all.15 = bf16[8,32,256]{2,1,0:T(8,128)(2,1)S(1)} all-to-all(bf16[8,32,256]{2,1,0:T(8,128)(2,1)S(1)} %broadcast_in_dim.18), channel_id=1, replica_groups={{0,2,4,6,8,10,12,14},{16,18,20,22,24,26,28,30},{32,34,36,38,40,42,44,46..., dimensions={0} | all-to-all | bytes 262144 | tf_op jit(solution)/shard_map/all_to_all | solution.py:43
  18.7 3.1 %collective-permute-start = (bf16[256,256]{1,0:T(8,128)(2,1)S(1)}, bf16[256,256]{1,0:T(8,128)(2,1)S(1)}, u32[]{:S(2)}, u32[]{:S(2)}) collective-permute-start(bf16[256,256]{1,0:T(8,128)(2,1)S(1)} %bitcast.11), channel_id=1, source_target_pairs={{0,96},{1,145},{2,98},{3,147},{4,100},{5,149},{6,102},{7,151},{8,1... | collective-permute-start | bytes 393224 | tf_op jit(solution)/shard_map/ppermute | solution.py:57
  21.9 2.9 %collective-permute-start.1 = (bf16[256,256]{1,0:T(8,128)(2,1)S(1)}, bf16[256,256]{1,0:T(8,128)(2,1)S(1)}, u32[]{:S(2)}, u32[]{:S(2)}) collective-permute-start(bf16[256,256]{1,0:T(8,128)(2,1)S(1)} %bitcast.12), channel_id=1, source_target_pairs={{0,128},{1,33},{2,130},{3,35},{4,132},{5,37},{6,134},{7,39},{8,136... | collective-permute-start | bytes 393224 | tf_op jit(solution)/shard_map/ppermute | solution.py:57
  24.8 2.2 %collective-permute-start.2 = (bf16[256,256]{1,0:T(8,128)(2,1)S(1)}, bf16[256,256]{1,0:T(8,128)(2,1)S(1)}, u32[]{:S(2)}, u32[]{:S(2)}) collective-permute-start(bf16[256,256]{1,0:T(8,128)(2,1)S(1)} %bitcast.13), channel_id=1, source_target_pairs={{0,224},{1,177},{2,226},{3,179},{4,228},{5,181},{6,230},{7,183},{8... | collective-permute-start | bytes 393224 | tf_op jit(solution)/shard_map/ppermute | solution.py:57
  26.9 2.0 %collective-permute-done = bf16[256,256]{1,0:T(8,128)(2,1)S(1)} collective-permute-done((bf16[256,256]{1,0:T(8,128)(2,1)S(1)}, bf16[256,256]{1,0:T(8,128)(2,1)S(1)}, u32[]{:S(2)}, u32[]{:S(2)}) %collective-permute-start) | collective-permute-done | bytes 131104 | tf_op jit(solution)/shard_map/ppermute | solution.py:57
  29.0 1.9 %collective-permute-done.1 = bf16[256,256]{1,0:T(8,128)(2,1)S(1)} collective-permute-done((bf16[256,256]{1,0:T(8,128)(2,1)S(1)}, bf16[256,256]{1,0:T(8,128)(2,1)S(1)}, u32[]{:S(2)}, u32[]{:S(2)}) %collective-permute-start.1) | collective-permute-done | bytes 131104 | tf_op jit(solution)/shard_map/ppermute | solution.py:57
  30.8 1.3 %collective-permute-done.2 = bf16[256,256]{1,0:T(8,128)(2,1)S(1)} collective-permute-done((bf16[256,256]{1,0:T(8,128)(2,1)S(1)}, bf16[256,256]{1,0:T(8,128)(2,1)S(1)}, u32[]{:S(2)}, u32[]{:S(2)}) %collective-permute-start.2) | collective-permute-done | bytes 131104 | tf_op jit(solution)/shard_map/ppermute | solution.py:57
  32.2 1.5 %collective-permute-start.3 = (bf16[1024,256]{1,0:T(8,128)(2,1)S(1)}, bf16[1024,256]{1,0:T(8,128)(2,1)S(1)}, u32[]{:S(2)}, u32[]{:S(2)}) collective-permute-start(bf16[1024,256]{1,0:T(8,128)(2,1)S(1)} %pad_maximum_fusion.a), channel_id=1, source_target_pairs={{0,48},{1,193},{2,50},{3,195},{4,52},{5,197},{6,54},{7,199},{8,56}... | collective-permute-start | bytes 1572872 | tf_op jit(solution)/shard_map/ppermute | solution.py:57
  33.7 0.6 collective-permute-start.4
  34.3 0.5 collective-permute-start.5
  34.9 2.8 %collective-permute-start.6 = (bf16[512,256]{1,0:T(8,128)(2,1)S(1)}, bf16[512,256]{1,0:T(8,128)(2,1)S(1)}, u32[]{:S(2)}, u32[]{:S(2)}) collective-permute-start(bf16[512,256]{1,0:T(8,128)(2,1)S(1)} %pad_maximum_fusion.1), channel_id=1, source_target_pairs={{0,192},{1,49},{2,194},{3,51},{4,196},{5,53},{6,198},{7,55},{8,200... | collective-permute-start | bytes 786440 | tf_op jit(solution)/shard_map/ppermute | solution.py:57
  37.7 0.0 copy-start
  37.7 3.4 %copy-done = bf16[4096,1024]{1,0:T(8,128)(2,1)S(1)} copy-done((bf16[4096,1024]{1,0:T(8,128)(2,1)S(1)}, bf16[4096,1024]{1,0:T(8,128)(2,1)}, u32[]{:S(2)}) %copy-start) | copy-done | bytes 8388632
  41.0 0.0 copy-start.1
  41.0 1.0 copy-done.1
  42.1 0.0 slice-start
  42.1 0.4 shard_map.58
  42.5 1.3 %collective-permute-done.5.d0 = bf16[512,256]{1,0:T(8,128)(2,1)S(1)} collective-permute-done((bf16[512,256]{1,0:T(8,128)(2,1)S(1)}, bf16[512,256]{1,0:T(8,128)(2,1)S(1)}, u32[]{:S(2)}, u32[]{:S(2)}) %collective-permute-start.5) | collective-permute-done | bytes 262176 | tf_op jit(solution)/shard_map/ppermute | solution.py:57
  43.8 0.0 collective-permute-done.6.d1
  43.8 0.5 collective-permute-done.3.b
  44.3 0.0 collective-permute-done.4.c
  44.3 0.0 slice-start.1
  44.3 3.2 %shard_map.59 = (f32[256,1024]{1,0:T(8,128)S(1)}, f32[256,128]{1,0:T(8,128)S(1)}, f32[6,128]{1,0:T(8,128)S(1)}, bf16[2048,256]{1,0:T(8,128)(2,1)S(1)}, bf16[2048,256]{1,0:T(8,128)(2,1)S(1)}) custom-call(s32[1]{0:T(128)} %bitcast.own, s32[1]{0:T(128)} %bitcast.1.core, s32[1]{0:T(128)} %bitcast.2.column, bf16[1024,256]{1,0:T(8,128)(2,1)S(1)} %pad_maximum_fusion.a, ...), custom_call_target="tpu_custom_call" | custom-call | flops 2147483648 | bytes 12582912 | tf_op jit(solution)/shard_map/pallas_call | solution.py:76
  47.5 0.2 collective-permute-start.7
  47.7 1.9 %collective-permute-start.8 = (f32[6,128]{1,0:T(8,128)S(1)}, f32[6,128]{1,0:T(8,128)S(1)}, u32[]{:S(2)}, u32[]{:S(2)}) collective-permute-start(f32[6,128]{1,0:T(8,128)S(1)} %get-tuple-element.29.first), channel_id=1, source_target_pairs={{0,48},{1,193},{2,50},{3,195},{4,52},{5,197},{6,54},{7,199},{8,56}... | collective-permute-start | bytes 9224 | tf_op jit(solution)/shard_map/ppermute | solution.py:57
  49.6 0.4 collective-permute-start.9
  50.1 1.1 %collective-permute-done.7.second = f32[6,128]{1,0:T(8,128)S(1)} collective-permute-done((f32[6,128]{1,0:T(8,128)S(1)}, f32[6,128]{1,0:T(8,128)S(1)}, u32[]{:S(2)}, u32[]{:S(2)}) %collective-permute-start.7) | collective-permute-done | bytes 3104 | tf_op jit(solution)/shard_map/ppermute | solution.py:57
  51.2 1.1 collective-permute-done.8.third
  52.3 2.1 %collective-permute-done.9.fourth = f32[6,128]{1,0:T(8,128)S(1)} collective-permute-done((f32[6,128]{1,0:T(8,128)S(1)}, f32[6,128]{1,0:T(8,128)S(1)}, u32[]{:S(2)}, u32[]{:S(2)}) %collective-permute-start.9) | collective-permute-done | bytes 3104 | tf_op jit(solution)/shard_map/ppermute | solution.py:57
  54.5 17.0 %all_to_all.16.stats = f32[32,6,128]{2,1,0:T(8,128)S(1)} all-to-all(f32[32,6,128]{2,1,0:T(8,128)S(1)} %shard_map.60), channel_id=1, replica_groups={{0,2,4,6,8,10,12,14,96,98,100,102,104,106,108,110,128,130,132,134,136,1..., dimensions={0} | all-to-all | bytes 196608 | tf_op jit(solution)/shard_map/all_to_all | solution.py:39
  71.5 0.0 collective-permute-start.14
  71.5 0.0 slice-done
  71.5 0.0 slice-done.1
  71.5 2.3 %shard_map.61 = (bf16[256,1024]{1,0:T(8,128)(2,1)S(1)}, bf16[1024,256]{1,0:T(8,128)(2,1)S(1)}, bf16[1024,256]{1,0:T(8,128)(2,1)S(1)}, bf16[1024,256]{1,0:T(8,128)(2,1)S(1)}, f32[2,128]{1,0:T(2,128)}) custom-call(s32[1]{0:T(128)} %bitcast.own, s32[1]{0:T(128)} %bitcast.1.core, f32[256,1024]{1,0:T(8,128)S(1)} %get-tuple-element.27.rise, ...), custom_call_target="tpu_custom_call" | custom-call | flops 1073741824 | bytes 8388608 | tf_op jit(solution)/shard_map/pallas_call | solution.py:76
  73.8 0.5 collective-permute-start.15
  74.3 1.4 %collective-permute-start.10 = (bf16[1024,256]{1,0:T(8,128)(2,1)S(1)}, bf16[1024,256]{1,0:T(8,128)(2,1)S(1)}, u32[]{:S(2)}, u32[]{:S(2)}) collective-permute-start(bf16[1024,256]{1,0:T(8,128)(2,1)S(1)} %get-tuple-element.34), channel_id=1, source_target_pairs={{0,16},{1,65},{2,18},{3,67},{4,20},{5,69},{6,22},{7,71},{8,24},{9,... | collective-permute-start | bytes 1572872 | tf_op jit(solution)/shard_map/ppermute | solution.py:57
  75.7 0.6 collective-permute-start.11
  76.3 1.3 %shard_map.62 = (bf16[512,256]{1,0:T(8,128)(2,1)S(1)}, bf16[512,256]{1,0:T(8,128)(2,1)S(1)}, f32[1024,256]{1,0:T(8,128)S(1)}) custom-call(s32[1]{0:T(128)} %bitcast.own, s32[1]{0:T(128)} %bitcast.1.core, bf16[1024,256]{1,0:T(8,128)(2,1)S(1)} %get-tuple-element.32.score_t, bf16[4096,1024]{1,0:T(8,128)(2,1)S(1)} %bitcast.9), custom_call_target="tpu_custom_call" | custom-call | flops 1073741824 | bytes 7340032 | tf_op jit(solution)/shard_map/pallas_call | solution.py:76
  77.6 0.1 collective-permute-start.12
  77.7 0.0 collective-permute-done.15.score_theirs
  77.7 3.2 %collective-permute-start.13 = (bf16[512,256]{1,0:T(8,128)(2,1)S(1)}, bf16[512,256]{1,0:T(8,128)(2,1)S(1)}, u32[]{:S(2)}, u32[]{:S(2)}) collective-permute-start(bf16[512,256]{1,0:T(8,128)(2,1)S(1)} %get-tuple-element.37), channel_id=1, source_target_pairs={{0,192},{1,49},{2,194},{3,51},{4,196},{5,53},{6,198},{7,55},{8,200... | collective-permute-start | bytes 786440 | tf_op jit(solution)/shard_map/ppermute | solution.py:57
  80.9 0.0 collective-permute-done.14.theirs
  80.9 3.2 %shard_map.63 = bf16[2048,1024]{1,0:T(8,128)(2,1)} custom-call(bf16[2048,256]{1,0:T(8,128)(2,1)S(1)} %get-tuple-element.38.mine, bf16[2048,256]{1,0:T(8,128)(2,1)S(1)} %collective-permute-done.14.theirs, bf16[256,1024]{1,0:T(8,128)(2,1)S(1)} %get-tuple-element.40.score, bf16[256,1024]{1,0:T(8,128)(2,1)S(1)} %collective-permute-done.15.score_theirs), custom_call_target="tpu_custom_call" | custom-call | flops 2147483648 | bytes 7340032 | tf_op jit(solution)/shard_map/pallas_call | solution.py:76
  84.2 2.4 %collective-permute-done.12 = bf16[512,256]{1,0:T(8,128)(2,1)S(1)} collective-permute-done((bf16[512,256]{1,0:T(8,128)(2,1)S(1)}, bf16[512,256]{1,0:T(8,128)(2,1)S(1)}, u32[]{:S(2)}, u32[]{:S(2)}) %collective-permute-start.12) | collective-permute-done | bytes 262176 | tf_op jit(solution)/shard_map/ppermute | solution.py:57
  86.6 0.0 collective-permute-done.13
  86.6 0.0 collective-permute-done.10
  86.6 1.1 collective-permute-done.11
  87.7 0.2 add_convert_fusion
  87.9 24.6 %all_to_all.17 = bf16[32,32,256]{2,1,0:T(8,128)(2,1)S(1)} all-to-all(bf16[32,32,256]{2,1,0:T(8,128)(2,1)S(1)} %bitcast.10), channel_id=1, replica_groups={{0,2,4,6,8,10,12,14,96,98,100,102,104,106,108,110,128,130,132,134,136,1..., dimensions={0} | all-to-all | bytes 1048576 | tf_op jit(solution)/shard_map/all_to_all | solution.py:39
  112.5 0.7 reduce_sum.12
  (4 shorter events, 0.1 us)
Async XLA Ops:
  18.7 10.3 %collective-permute-start = (bf16[256,256]{1,0:T(8,128)(2,1)S(1)}, bf16[256,256]{1,0:T(8,128)(2,1)S(1)}, u32[]{:S(2)}, u32[]{:S(2)}) collective-permute-start(bf16[256,256]{1,0:T(8,128)(2,1)S(1)} %bitcast.11), channel_id=1, source_target_pairs={{0,96},{1,145},{2,98},{3,147},{4,100},{5,149},{6,102},{7,151},{8,1... | collective-permute-start | bytes 393224 | tf_op jit(solution)/shard_map/ppermute | solution.py:57
  21.9 9.0 %collective-permute-start.1 = (bf16[256,256]{1,0:T(8,128)(2,1)S(1)}, bf16[256,256]{1,0:T(8,128)(2,1)S(1)}, u32[]{:S(2)}, u32[]{:S(2)}) collective-permute-start(bf16[256,256]{1,0:T(8,128)(2,1)S(1)} %bitcast.12), channel_id=1, source_target_pairs={{0,128},{1,33},{2,130},{3,35},{4,132},{5,37},{6,134},{7,39},{8,136... | collective-permute-start | bytes 393224 | tf_op jit(solution)/shard_map/ppermute | solution.py:57
  24.8 7.4 %collective-permute-start.2 = (bf16[256,256]{1,0:T(8,128)(2,1)S(1)}, bf16[256,256]{1,0:T(8,128)(2,1)S(1)}, u32[]{:S(2)}, u32[]{:S(2)}) collective-permute-start(bf16[256,256]{1,0:T(8,128)(2,1)S(1)} %bitcast.13), channel_id=1, source_target_pairs={{0,224},{1,177},{2,226},{3,179},{4,228},{5,181},{6,230},{7,183},{8... | collective-permute-start | bytes 393224 | tf_op jit(solution)/shard_map/ppermute | solution.py:57
  32.2 12.1 %collective-permute-start.3 = (bf16[1024,256]{1,0:T(8,128)(2,1)S(1)}, bf16[1024,256]{1,0:T(8,128)(2,1)S(1)}, u32[]{:S(2)}, u32[]{:S(2)}) collective-permute-start(bf16[1024,256]{1,0:T(8,128)(2,1)S(1)} %pad_maximum_fusion.a), channel_id=1, source_target_pairs={{0,48},{1,193},{2,50},{3,195},{4,52},{5,197},{6,54},{7,199},{8,56}... | collective-permute-start | bytes 1572872 | tf_op jit(solution)/shard_map/ppermute | solution.py:57
  33.7 10.6 %collective-permute-start.4 = (bf16[1024,256]{1,0:T(8,128)(2,1)S(1)}, bf16[1024,256]{1,0:T(8,128)(2,1)S(1)}, u32[]{:S(2)}, u32[]{:S(2)}) collective-permute-start(bf16[1024,256]{1,0:T(8,128)(2,1)S(1)} %pad_maximum_fusion.a), channel_id=1, source_target_pairs={{0,16},{1,65},{2,18},{3,67},{4,20},{5,69},{6,22},{7,71},{8,24},{9,... | collective-permute-start | bytes 1572872 | tf_op jit(solution)/shard_map/ppermute | solution.py:57
  34.3 9.4 %collective-permute-start.5 = (bf16[512,256]{1,0:T(8,128)(2,1)S(1)}, bf16[512,256]{1,0:T(8,128)(2,1)S(1)}, u32[]{:S(2)}, u32[]{:S(2)}) collective-permute-start(bf16[512,256]{1,0:T(8,128)(2,1)S(1)} %pad_maximum_fusion.1), channel_id=1, source_target_pairs={{0,64},{1,17},{2,66},{3,19},{4,68},{5,21},{6,70},{7,23},{8,72},{9,... | collective-permute-start | bytes 786440 | tf_op jit(solution)/shard_map/ppermute | solution.py:57
  34.9 8.9 %collective-permute-start.6 = (bf16[512,256]{1,0:T(8,128)(2,1)S(1)}, bf16[512,256]{1,0:T(8,128)(2,1)S(1)}, u32[]{:S(2)}, u32[]{:S(2)}) collective-permute-start(bf16[512,256]{1,0:T(8,128)(2,1)S(1)} %pad_maximum_fusion.1), channel_id=1, source_target_pairs={{0,192},{1,49},{2,194},{3,51},{4,196},{5,53},{6,198},{7,55},{8,200... | collective-permute-start | bytes 786440 | tf_op jit(solution)/shard_map/ppermute | solution.py:57
  37.7 3.4 %copy-start = (bf16[4096,1024]{1,0:T(8,128)(2,1)S(1)}, bf16[4096,1024]{1,0:T(8,128)(2,1)}, u32[]{:S(2)}) copy-start(bf16[4096,1024]{1,0:T(8,128)(2,1)} %head.7) | copy-start | bytes 25165828
  41.0 1.0 copy-start.1
  42.1 29.4 %slice-start = ((s8[8388608]{0:T(1024)(128)(4,1)}), s8[4194304]{0:T(1024)(128)(4,1)S(1)}, s32[]{:S(2)}) async-start(s8[8388608]{0:T(1024)(128)(4,1)} %bitcast.8), calls=%async_computation.3 | async-start | bytes 8388608
  44.3 27.2 %slice-start.1 = ((s8[8388608]{0:T(1024)(128)(4,1)}), s8[4194304]{0:T(1024)(128)(4,1)S(1)}, s32[]{:S(2)}) async-start(s8[8388608]{0:T(1024)(128)(4,1)} %bitcast.8), calls=%async_computation.4 | async-start | bytes 8388608
  47.5 3.7 %collective-permute-start.7 = (f32[6,128]{1,0:T(8,128)S(1)}, f32[6,128]{1,0:T(8,128)S(1)}, u32[]{:S(2)}, u32[]{:S(2)}) collective-permute-start(f32[6,128]{1,0:T(8,128)S(1)} %get-tuple-element.29.first), channel_id=1, source_target_pairs={{0,16},{1,65},{2,18},{3,67},{4,20},{5,69},{6,22},{7,71},{8,24},{9,... | collective-permute-start | bytes 9224 | tf_op jit(solution)/shard_map/ppermute | solution.py:57
  47.7 4.6 %collective-permute-start.8 = (f32[6,128]{1,0:T(8,128)S(1)}, f32[6,128]{1,0:T(8,128)S(1)}, u32[]{:S(2)}, u32[]{:S(2)}) collective-permute-start(f32[6,128]{1,0:T(8,128)S(1)} %get-tuple-element.29.first), channel_id=1, source_target_pairs={{0,48},{1,193},{2,50},{3,195},{4,52},{5,197},{6,54},{7,199},{8,56}... | collective-permute-start | bytes 9224 | tf_op jit(solution)/shard_map/ppermute | solution.py:57
  49.6 4.8 %collective-permute-start.9 = (f32[6,128]{1,0:T(8,128)S(1)}, f32[6,128]{1,0:T(8,128)S(1)}, u32[]{:S(2)}, u32[]{:S(2)}) collective-permute-start(f32[6,128]{1,0:T(8,128)S(1)} %get-tuple-element.29.first), channel_id=1, source_target_pairs={{0,64},{1,17},{2,66},{3,19},{4,68},{5,21},{6,70},{7,23},{8,72},{9,... | collective-permute-start | bytes 9224 | tf_op jit(solution)/shard_map/ppermute | solution.py:57
  71.5 9.5 %collective-permute-start.14 = (bf16[2048,256]{1,0:T(8,128)(2,1)S(1)}, bf16[2048,256]{1,0:T(8,128)(2,1)S(1)}, u32[]{:S(2)}, u32[]{:S(2)}) collective-permute-start(bf16[2048,256]{1,0:T(8,128)(2,1)S(1)} %get-tuple-element.39), channel_id=1, source_target_pairs={{0,1},{1,0},{2,3},{3,2},{4,5},{5,4},{6,7},{7,6},{8,9},{9,8},{10,11... | collective-permute-start | bytes 3145736 | tf_op jit(solution)/shard_map/ppermute | solution.py:61
  73.8 3.9 %collective-permute-start.15 = (bf16[256,1024]{1,0:T(8,128)(2,1)S(1)}, bf16[256,1024]{1,0:T(8,128)(2,1)S(1)}, u32[]{:S(2)}, u32[]{:S(2)}) collective-permute-start(bf16[256,1024]{1,0:T(8,128)(2,1)S(1)} %get-tuple-element.40.score), channel_id=1, source_target_pairs={{0,1},{1,0},{2,3},{3,2},{4,5},{5,4},{6,7},{7,6},{8,9},{9,8},{10,11... | collective-permute-start | bytes 1572872 | tf_op jit(solution)/shard_map/ppermute | solution.py:61
  74.3 12.3 %collective-permute-start.10 = (bf16[1024,256]{1,0:T(8,128)(2,1)S(1)}, bf16[1024,256]{1,0:T(8,128)(2,1)S(1)}, u32[]{:S(2)}, u32[]{:S(2)}) collective-permute-start(bf16[1024,256]{1,0:T(8,128)(2,1)S(1)} %get-tuple-element.34), channel_id=1, source_target_pairs={{0,16},{1,65},{2,18},{3,67},{4,20},{5,69},{6,22},{7,71},{8,24},{9,... | collective-permute-start | bytes 1572872 | tf_op jit(solution)/shard_map/ppermute | solution.py:57
  75.7 11.9 %collective-permute-start.11 = (bf16[1024,256]{1,0:T(8,128)(2,1)S(1)}, bf16[1024,256]{1,0:T(8,128)(2,1)S(1)}, u32[]{:S(2)}, u32[]{:S(2)}) collective-permute-start(bf16[1024,256]{1,0:T(8,128)(2,1)S(1)} %get-tuple-element.35), channel_id=1, source_target_pairs={{0,48},{1,193},{2,50},{3,195},{4,52},{5,197},{6,54},{7,199},{8,56}... | collective-permute-start | bytes 1572872 | tf_op jit(solution)/shard_map/ppermute | solution.py:57
  77.6 8.9 %collective-permute-start.12 = (bf16[512,256]{1,0:T(8,128)(2,1)S(1)}, bf16[512,256]{1,0:T(8,128)(2,1)S(1)}, u32[]{:S(2)}, u32[]{:S(2)}) collective-permute-start(bf16[512,256]{1,0:T(8,128)(2,1)S(1)} %get-tuple-element.36), channel_id=1, source_target_pairs={{0,64},{1,17},{2,66},{3,19},{4,68},{5,21},{6,70},{7,23},{8,72},{9,... | collective-permute-start | bytes 786440 | tf_op jit(solution)/shard_map/ppermute | solution.py:57
  77.7 8.8 %collective-permute-start.13 = (bf16[512,256]{1,0:T(8,128)(2,1)S(1)}, bf16[512,256]{1,0:T(8,128)(2,1)S(1)}, u32[]{:S(2)}, u32[]{:S(2)}) collective-permute-start(bf16[512,256]{1,0:T(8,128)(2,1)S(1)} %get-tuple-element.37), channel_id=1, source_target_pairs={{0,192},{1,49},{2,194},{3,51},{4,196},{5,53},{6,198},{7,55},{8,200... | collective-permute-start | bytes 786440 | tf_op jit(solution)/shard_map/ppermute | solution.py:57

commit v7 on v5

--- a/solution.py
+++ b/solution.py
@@ -25,20 +25,22 @@
     return place(*((across, along) if core == 0 else (along, across)), z) * 2 + core
 
 
-class_groups = [
-    [spot((c - 2 * across) % 4, across, z, core) for across in range(4) for z in range(NZ)]
+octets = [
+    [spot(c + 2 * z, across, z, core) for z in range(NZ)]
     for core in range(2)
     for c in range(4)
+    for across in range(4)
 ]
-
-
-def trade(chunks):
-    return lax.all_to_all(chunks, BOTH, 0, 0, tiled=True, axis_index_groups=class_groups)
-
-
-def step(value, across_by, along_by):
+class_groups = [sum(octets[i : i + 4], []) for i in range(0, 32, 4)]
+
+
+def trade(chunks, groups):
+    return lax.all_to_all(chunks, BOTH, 0, 0, tiled=True, axis_index_groups=groups)
+
+
+def step(value, along_by, across_by, z_by):
     pairs = [
-        (spot(along, across, z, core), spot(along + along_by, across + across_by, z, core))
+        (spot(along, across, z, core), spot(along + along_by, across + across_by, z + z_by, core))
         for along in range(4)
         for across in range(4)
         for z in range(NZ)
@@ -47,17 +49,18 @@
     return lax.ppermute(value, BOTH, pairs)
 
 
+def class_of(hidden_t):
+    slab = trade(jnp.broadcast_to(hidden_t[None], (NZ, 32, ROWS)), octets).reshape(SLAB, ROWS)
+    return jnp.concatenate([slab] + [step(slab, 0, i, 0) for i in (1, 2, 3)], axis=0)
+
+
 def other_core(value):
     return lax.ppermute(value, "rows", [(0, 1), (1, 0)])
 
 
-def slab_of(own, core, offset, j):
-    k = lax.rem(own[0] + offset - 2 * j + 8, 4)
-    return (4 - 3 * core[0]) * j + (1 + 3 * core[0]) * k
-
-
-def slab_row(own, core, offset, j):
-    return pl.multiple_of(slab_of(own, core, offset, j) * SLAB, SLAB)
+def column_of(own, core, offset, j, odd):
+    along = lax.rem(own[0] + offset + 2 * odd, 4)
+    return (4 - 3 * core[0]) * j + (1 + 3 * core[0]) * along
 
 
 def call(body, outs, ins, flops, traffic, scratch=(), limit=8, into="v"):
@@ -83,21 +86,28 @@
 
 
 def student_kernel(
-    own, core, a, b, c, d0, d1, head, mentor, prob, lse_t, rise, peak, stats, mine, theirs
+    own, core, column, a, b, c, d0, d1, head, mentor, prob, lse_t, rise, peak, stats, mine, theirs
 ):
     for offset, ref, first, count in [(0, a, 0, 4), (1, b, 0, 4), (3, c, 0, 4), (2, d0, 0, 2), (2, d1, 2, 2)]:
         for i in range(count):
-            slab = slab_of(own, core, offset, first + i)
-            half = lax.shift_right_logical(slab, 3)
-            rows = pl.ds(pl.multiple_of((slab - 8 * half) * SLAB, SLAB), SLAB)
-
-            @pl.when(core[0] == half)
-            def _(ref=ref, rows=rows, i=i):
-                mine[rows] = ref[pl.ds(i * SLAB, SLAB)]
-
-            @pl.when(core[0] != half)
-            def _(ref=ref, rows=rows, i=i):
-                theirs[rows] = ref[pl.ds(i * SLAB, SLAB)]
+            j = lax.rem(column[0] - first - i + 4, 4)
+            for odd in range(2):
+                place_in = column_of(own, core, offset, j, odd)
+                half = lax.shift_right_logical(place_in, 3)
+                base = (place_in - 8 * half) * SLAB
+
+                def put(into, ref=ref, base=base, i=i, odd=odd):
+                    for z in range(odd, NZ, 2):
+                        rows = pl.ds(pl.multiple_of(base + 32 * z, 32), 32)
+                        into[rows] = ref[pl.ds(i * SLAB + 32 * z, 32)]
+
+                @pl.when(core[0] == half)
+                def _(put=put):
+                    put(mine)
+
+                @pl.when(core[0] != half)
+                def _(put=put):
+                    put(theirs)
 
     half = FULL // 2
 
@@ -145,8 +155,10 @@
 
 def times_head(own, core, head, score_t, outs):
     for offset, j, ref in outs:
-        rows = pl.ds(slab_row(own, core, offset, j), SLAB)
-        ref[...] = jnp.dot(head[rows], score_t, preferred_element_type=f32).astype(ref.dtype)
+        bases = [column_of(own, core, offset, j, odd) * SLAB for odd in range(2)]
+        eighths = [head[pl.ds(pl.multiple_of(bases[z % 2] + 32 * z, 32), 32)] for z in range(NZ)]
+        rows = jnp.concatenate(eighths, axis=0)
+        ref[...] = jnp.dot(rows, score_t, preferred_element_type=f32).astype(ref.dtype)
 
 
 def score_kernel(own, core, rise, peak, prob, lse_t, stats, head, score, score_t, b, c, mismatch):
@@ -184,21 +196,22 @@
 
 
 def stats_of_all(stats):
-    near = [stats, step(stats, 0, 1), step(stats, 0, -1), step(stats, 1, 0)]
+    near = [stats, step(stats, 1, 0, 0), step(stats, -1, 0, 0), step(stats, 0, 0, 1)]
     (stats,) = call(
         merge_kernel, [((32, 6, 128), f32)], [("v", value) for value in near], 1000, 1000
     )
-    return trade(stats)
+    return trade(stats, class_groups)
 
 
 def shards(hidden, head_weight, mentor_outputs):
     here = lax.axis_index("vocab")
     core = lax.axis_index("rows").astype(jnp.int32)
     x, y = lax.rem(lax.div(here, NZ), NX), lax.div(here, NZ * NX)
-    own = lax.rem(jnp.where(core == 0, x + 2 * y, y + 2 * x), 4).astype(jnp.int32)[None]
+    own = lax.rem(jnp.where(core == 0, x, y) + 2 * lax.rem(here, NZ), 4).astype(jnp.int32)[None]
     core = core[None]
 
-    a = trade(jnp.broadcast_to(hidden.T[None], (32, 32, ROWS))).reshape(1024, ROWS)
+    column = jnp.where(core[0] == 0, y, x).astype(jnp.int32)[None]
+    a = class_of(hidden.T)
     prob, lse_t = call(
         target_kernel,
         [((ROWS, COLS), f32), ((ROWS, 128), f32)],
@@ -206,13 +219,13 @@
         10 * ROWS * COLS,
         2 * MIB,
     )
-    b, c = step(a, 0, -1), step(a, 0, 1)
-    d0, d1 = step(a[:512], 1, 0), step(a[512:], -1, 0)
+    b, c = step(a, -1, 0, 0), step(a, 1, 0, 0)
+    d0, d1 = step(a[:512], 0, 0, 1), step(a[512:], 0, 0, -1)
 
     rise, peak, stats, mine, theirs = call(
         student_kernel,
         [((ROWS, COLS), f32), ((ROWS, 128), f32), ((6, 128), f32)] + [((FULL // 2, ROWS), bf16)] * 2,
-        [("s", own), ("s", core), ("v", a), ("v", b), ("v", c), ("v", d0), ("v", d1), ("v", head_weight)]
+        [("s", own), ("s", core), ("s", column), ("v", a), ("v", b), ("v", c), ("v", d0), ("v", d1), ("v", head_weight)]
         + [("v", mentor_outputs), ("v", prob), ("v", lse_t)],
         2 * FULL * ROWS * COLS,
         12 * MIB,
@@ -227,7 +240,7 @@
         FULL * ROWS * COLS,
         8 * MIB,
     )
-    b, c = step(b, 0, 1), step(c, 0, -1)
+    b, c = step(b, 1, 0, 0), step(c, -1, 0, 0)
     score_theirs = other_core(score)
     d0, d1, a = call(
         rest_kernel,
@@ -236,7 +249,7 @@
         FULL * ROWS * COLS,
         7 * MIB,
     )
-    d0, d1 = step(d0, 1, 0), step(d1, -1, 0)
+    d0, d1 = step(d0, 0, 0, 1), step(d1, 0, 0, -1)
     (weight_grad,) = call(
         weight_kernel,
         [((FULL // 2, COLS), bf16)],
@@ -248,7 +261,7 @@
     )
     b, c, d0, d1, weight_grad = lax.optimization_barrier((b, c, d0, d1, weight_grad))
     part = a + b.astype(f32) + c.astype(f32) + jnp.concatenate([d0, d1], axis=0).astype(f32)
-    part = trade(part.astype(bf16).reshape(32, 32, ROWS))
+    part = trade(part.astype(bf16).reshape(32, 32, ROWS), class_groups)
     hidden_grad = jnp.sum(part.astype(f32), axis=0).astype(bf16).T
     return (hidden_grad, weight_grad, mismatch.reshape(ROWS))
 

time: 116 us -> 113 us (0.974)
  blocking collectives: 74.5 us -> 63.1 us
  starting transfers between devices: 12.9 us -> 19.2 us
  waiting for transfers between devices: 11.1 us -> 12.8 us
    all_to_all x3, blocking collectives: 74.5 us -> 63.1 us  [trade(): lax.all_to_all(chunks, BOTH, 0, 0, tiled=True, axis_index_groups=groups)]
    ppermute x11 -> x14, starting transfers between devices: 12.4 us -> 18.8 us  [step(): return lax.ppermute(value, BOTH, pairs)]
    ppermute x11 -> x14, waiting for transfers between devices: 11.1 us -> 12.8 us  [step(): return lax.ppermute(value, BOTH, pairs)]
  transfers between devices with their start and end apart: 13 -> 16, of which waited for: 7 -> 10; matrix products, arithmetic and copies ran while one was open for 0% -> 0% of each run, Pallas kernels for 6% -> 6%
where the time goes in v7:
time: 113 us
  blocking collectives  63.1 us (56%)
  starting transfers between devices  19.2 us (17%)
  waiting for transfers between devices  12.8 us (11%)
  Pallas kernels  10.8 us (10%)
  local copies, waits for them, and re-layouts  5.16 us (5%)
    all_to_all x3, blocking collectives, trade(): lax.all_to_all(chunks, BOTH, 0, 0, tiled=True, axis_index_groups=groups)  63.1 us
    ppermute x14, starting transfers between devices, step(): return lax.ppermute(value, BOTH, pairs)  18.8 us
    ppermute x14, waiting for transfers between devices, step(): return lax.ppermute(value, BOTH, pairs)  12.8 us
    pallas_call x6, Pallas kernels, call(): pl.pallas_call(body, out_shape=[jax.ShapeDtypeStruct(shape, dtype) for sh...  10.8 us
    unnamed x8, local copies, waits for them, and re-layouts  4.43 us
  transfers between devices with their start and end apart: 16, of which 10 were waited for; matrix products, arithmetic and copies ran while one was open for 0% of the time, Pallas kernels for 6%

profile of v7, /device:TPU:2, one launch (start us, length us, event | category | flops | bytes accessed | tf_op | source)
XLA Modules:
  0.0 112.9 jit_solution(5340727039148434044)
XLA Ops:
  0.6 0.7 broadcast_in_dim.18
  1.4 19.5 %all_to_all.15 = bf16[8,32,256]{2,1,0:T(8,128)(2,1)S(1)} all-to-all(bf16[8,32,256]{2,1,0:T(8,128)(2,1)S(1)} %broadcast_in_dim.18), channel_id=1, replica_groups={{0,34,4,38,8,42,12,46},{64,98,68,102,72,106,76,110},{128,162,132,166,13..., dimensions={0} | all-to-all | bytes 262144 | tf_op jit(solution)/shard_map/all_to_all | solution.py:38
  20.9 1.0 collective-permute-start
  21.9 2.7 %collective-permute-start.1 = (bf16[256,256]{1,0:T(8,128)(2,1)S(1)}, bf16[256,256]{1,0:T(8,128)(2,1)S(1)}, u32[]{:S(2)}, u32[]{:S(2)}) collective-permute-start(bf16[256,256]{1,0:T(8,128)(2,1)S(1)} %bitcast.12), channel_id=1, source_target_pairs={{0,128},{1,33},{2,130},{3,35},{4,132},{5,37},{6,134},{7,39},{8,136... | collective-permute-start | bytes 393224 | tf_op jit(solution)/shard_map/ppermute | solution.py:49
  24.6 1.3 %collective-permute-start.2 = (bf16[256,256]{1,0:T(8,128)(2,1)S(1)}, bf16[256,256]{1,0:T(8,128)(2,1)S(1)}, u32[]{:S(2)}, u32[]{:S(2)}) collective-permute-start(bf16[256,256]{1,0:T(8,128)(2,1)S(1)} %bitcast.13), channel_id=1, source_target_pairs={{0,192},{1,49},{2,194},{3,51},{4,196},{5,53},{6,198},{7,55},{8,200... | collective-permute-start | bytes 393224 | tf_op jit(solution)/shard_map/ppermute | solution.py:49
  25.9 1.1 %collective-permute-done = bf16[256,256]{1,0:T(8,128)(2,1)S(1)} collective-permute-done((bf16[256,256]{1,0:T(8,128)(2,1)S(1)}, bf16[256,256]{1,0:T(8,128)(2,1)S(1)}, u32[]{:S(2)}, u32[]{:S(2)}) %collective-permute-start) | collective-permute-done | bytes 131104 | tf_op jit(solution)/shard_map/ppermute | solution.py:49
  27.1 1.9 %collective-permute-done.1 = bf16[256,256]{1,0:T(8,128)(2,1)S(1)} collective-permute-done((bf16[256,256]{1,0:T(8,128)(2,1)S(1)}, bf16[256,256]{1,0:T(8,128)(2,1)S(1)}, u32[]{:S(2)}, u32[]{:S(2)}) %collective-permute-start.1) | collective-permute-done | bytes 131104 | tf_op jit(solution)/shard_map/ppermute | solution.py:49
  28.9 0.6 collective-permute-done.2
  29.6 1.8 %collective-permute-start.3 = (bf16[1024,256]{1,0:T(8,128)(2,1)S(1)}, bf16[1024,256]{1,0:T(8,128)(2,1)S(1)}, u32[]{:S(2)}, u32[]{:S(2)}) collective-permute-start(bf16[1024,256]{1,0:T(8,128)(2,1)S(1)} %pad_maximum_fusion.a), channel_id=1, source_target_pairs={{0,48},{1,193},{2,50},{3,195},{4,52},{5,197},{6,54},{7,199},{8,56}... | collective-permute-start | bytes 1572872 | tf_op jit(solution)/shard_map/ppermute | solution.py:49
  31.4 0.3 collective-permute-start.4
  31.7 0.9 collective-permute-start.6
  32.6 1.3 %collective-permute-start.5 = (bf16[512,256]{1,0:T(8,128)(2,1)S(1)}, bf16[512,256]{1,0:T(8,128)(2,1)S(1)}, u32[]{:S(2)}, u32[]{:S(2)}) collective-permute-start(bf16[512,256]{1,0:T(8,128)(2,1)S(1)} %pad_maximum_fusion.1), channel_id=1, source_target_pairs={{0,2},{1,3},{2,4},{3,5},{4,6},{5,7},{6,8},{7,9},{8,10},{9,11},{10,... | collective-permute-start | bytes 786440 | tf_op jit(solution)/shard_map/ppermute | solution.py:49
  33.9 0.0 copy-start
  33.9 3.4 %copy-done = bf16[4096,1024]{1,0:T(8,128)(2,1)S(1)} copy-done((bf16[4096,1024]{1,0:T(8,128)(2,1)S(1)}, bf16[4096,1024]{1,0:T(8,128)(2,1)}, u32[]{:S(2)}) %copy-start) | copy-done | bytes 8388632
  37.3 0.0 copy-start.1
  37.3 1.0 copy-done.1
  38.3 0.0 slice-start
  38.3 0.4 shard_map.58
  38.7 0.0 collective-permute-done.6.d1
  38.8 1.5 %collective-permute-done.5.d0 = bf16[512,256]{1,0:T(8,128)(2,1)S(1)} collective-permute-done((bf16[512,256]{1,0:T(8,128)(2,1)S(1)}, bf16[512,256]{1,0:T(8,128)(2,1)S(1)}, u32[]{:S(2)}, u32[]{:S(2)}) %collective-permute-start.5) | collective-permute-done | bytes 262176 | tf_op jit(solution)/shard_map/ppermute | solution.py:49
  40.3 0.0 collective-permute-done.3.b
  40.3 0.3 collective-permute-done.4.c
  40.6 0.0 slice-start.1
  40.6 3.6 %shard_map.59 = (f32[256,1024]{1,0:T(8,128)S(1)}, f32[256,128]{1,0:T(8,128)S(1)}, f32[6,128]{1,0:T(8,128)S(1)}, bf16[2048,256]{1,0:T(8,128)(2,1)S(1)}, bf16[2048,256]{1,0:T(8,128)(2,1)S(1)}) custom-call(s32[1]{0:T(128)} %bitcast.own, s32[1]{0:T(128)} %bitcast.1.core, s32[1]{0:T(128)} %bitcast.2.column, bf16[1024,256]{1,0:T(8,128)(2,1)S(1)} %pad_maximum_fusion.a, ...), custom_call_target="tpu_custom_call" | custom-call | flops 2147483648 | bytes 12582912 | tf_op jit(solution)/shard_map/pallas_call | solution.py:69
  44.1 1.7 %collective-permute-start.7 = (f32[6,128]{1,0:T(8,128)S(1)}, f32[6,128]{1,0:T(8,128)S(1)}, u32[]{:S(2)}, u32[]{:S(2)}) collective-permute-start(f32[6,128]{1,0:T(8,128)S(1)} %get-tuple-element.29.first), channel_id=1, source_target_pairs={{0,16},{1,65},{2,18},{3,67},{4,20},{5,69},{6,22},{7,71},{8,24},{9,... | collective-permute-start | bytes 9224 | tf_op jit(solution)/shard_map/ppermute | solution.py:49
  45.8 0.8 collective-permute-start.8
  46.7 1.2 %collective-permute-start.9 = (f32[6,128]{1,0:T(8,128)S(1)}, f32[6,128]{1,0:T(8,128)S(1)}, u32[]{:S(2)}, u32[]{:S(2)}) collective-permute-start(f32[6,128]{1,0:T(8,128)S(1)} %get-tuple-element.29.first), channel_id=1, source_target_pairs={{0,2},{1,3},{2,4},{3,5},{4,6},{5,7},{6,8},{7,9},{8,10},{9,11},{10,... | collective-permute-start | bytes 9224 | tf_op jit(solution)/shard_map/ppermute | solution.py:49
  47.8 0.3 collective-permute-done.7.second
  48.2 1.3 %collective-permute-done.8.third = f32[6,128]{1,0:T(8,128)S(1)} collective-permute-done((f32[6,128]{1,0:T(8,128)S(1)}, f32[6,128]{1,0:T(8,128)S(1)}, u32[]{:S(2)}, u32[]{:S(2)}) %collective-permute-start.8) | collective-permute-done | bytes 3104 | tf_op jit(solution)/shard_map/ppermute | solution.py:49
  49.4 2.1 %collective-permute-done.9.fourth = f32[6,128]{1,0:T(8,128)S(1)} collective-permute-done((f32[6,128]{1,0:T(8,128)S(1)}, f32[6,128]{1,0:T(8,128)S(1)}, u32[]{:S(2)}, u32[]{:S(2)}) %collective-permute-start.9) | collective-permute-done | bytes 3104 | tf_op jit(solution)/shard_map/ppermute | solution.py:49
  51.5 17.9 %all_to_all.16.stats = f32[32,6,128]{2,1,0:T(8,128)S(1)} all-to-all(f32[32,6,128]{2,1,0:T(8,128)S(1)} %shard_map.60), channel_id=1, replica_groups={{0,34,4,38,8,42,12,46,64,98,68,102,72,106,76,110,128,162,132,166,136,17..., dimensions={0} | all-to-all | bytes 196608 | tf_op jit(solution)/shard_map/all_to_all | solution.py:38
  69.4 0.0 collective-permute-start.14
  69.4 0.0 slice-done
  69.5 0.0 slice-done.1
  69.5 2.3 %shard_map.61 = (bf16[256,1024]{1,0:T(8,128)(2,1)S(1)}, bf16[1024,256]{1,0:T(8,128)(2,1)S(1)}, bf16[1024,256]{1,0:T(8,128)(2,1)S(1)}, bf16[1024,256]{1,0:T(8,128)(2,1)S(1)}, f32[2,128]{1,0:T(2,128)}) custom-call(s32[1]{0:T(128)} %bitcast.own, s32[1]{0:T(128)} %bitcast.1.core, f32[256,1024]{1,0:T(8,128)S(1)} %get-tuple-element.27.rise, ...), custom_call_target="tpu_custom_call" | custom-call | flops 1073741824 | bytes 8388608 | tf_op jit(solution)/shard_map/pallas_call | solution.py:69
  71.8 0.5 collective-permute-start.15
  72.3 2.2 %collective-permute-start.10 = (bf16[1024,256]{1,0:T(8,128)(2,1)S(1)}, bf16[1024,256]{1,0:T(8,128)(2,1)S(1)}, u32[]{:S(2)}, u32[]{:S(2)}) collective-permute-start(bf16[1024,256]{1,0:T(8,128)(2,1)S(1)} %get-tuple-element.34), channel_id=1, source_target_pairs={{0,16},{1,65},{2,18},{3,67},{4,20},{5,69},{6,22},{7,71},{8,24},{9,... | collective-permute-start | bytes 1572872 | tf_op jit(solution)/shard_map/ppermute | solution.py:49
  74.5 0.2 collective-permute-start.11
  74.7 1.3 %shard_map.62 = (bf16[512,256]{1,0:T(8,128)(2,1)S(1)}, bf16[512,256]{1,0:T(8,128)(2,1)S(1)}, f32[1024,256]{1,0:T(8,128)S(1)}) custom-call(s32[1]{0:T(128)} %bitcast.own, s32[1]{0:T(128)} %bitcast.1.core, bf16[1024,256]{1,0:T(8,128)(2,1)S(1)} %get-tuple-element.32.score_t, bf16[4096,1024]{1,0:T(8,128)(2,1)S(1)} %bitcast.9), custom_call_target="tpu_custom_call" | custom-call | flops 1073741824 | bytes 7340032 | tf_op jit(solution)/shard_map/pallas_call | solution.py:69
  76.0 1.7 %collective-permute-start.12 = (bf16[512,256]{1,0:T(8,128)(2,1)S(1)}, bf16[512,256]{1,0:T(8,128)(2,1)S(1)}, u32[]{:S(2)}, u32[]{:S(2)}) collective-permute-start(bf16[512,256]{1,0:T(8,128)(2,1)S(1)} %get-tuple-element.36), channel_id=1, source_target_pairs={{0,2},{1,3},{2,4},{3,5},{4,6},{5,7},{6,8},{7,9},{8,10},{9,11},{10,... | collective-permute-start | bytes 786440 | tf_op jit(solution)/shard_map/ppermute | solution.py:49
  77.7 0.0 collective-permute-done.15.score_theirs
  77.7 1.6 %collective-permute-start.13 = (bf16[512,256]{1,0:T(8,128)(2,1)S(1)}, bf16[512,256]{1,0:T(8,128)(2,1)S(1)}, u32[]{:S(2)}, u32[]{:S(2)}) collective-permute-start(bf16[512,256]{1,0:T(8,128)(2,1)S(1)} %get-tuple-element.37), channel_id=1, source_target_pairs={{0,14},{1,15},{2,0},{3,1},{4,2},{5,3},{6,4},{7,5},{8,6},{9,7},{10,... | collective-permute-start | bytes 786440 | tf_op jit(solution)/shard_map/ppermute | solution.py:49
  79.3 0.0 collective-permute-done.14.theirs
  79.3 3.2 %shard_map.63 = bf16[2048,1024]{1,0:T(8,128)(2,1)} custom-call(bf16[2048,256]{1,0:T(8,128)(2,1)S(1)} %get-tuple-element.38.mine, bf16[2048,256]{1,0:T(8,128)(2,1)S(1)} %collective-permute-done.14.theirs, bf16[256,1024]{1,0:T(8,128)(2,1)S(1)} %get-tuple-element.40.score, bf16[256,1024]{1,0:T(8,128)(2,1)S(1)} %collective-permute-done.15.score_theirs), custom_call_target="tpu_custom_call" | custom-call | flops 2147483648 | bytes 7340032 | tf_op jit(solution)/shard_map/pallas_call | solution.py:69
  82.6 3.2 %collective-permute-done.12 = bf16[512,256]{1,0:T(8,128)(2,1)S(1)} collective-permute-done((bf16[512,256]{1,0:T(8,128)(2,1)S(1)}, bf16[512,256]{1,0:T(8,128)(2,1)S(1)}, u32[]{:S(2)}, u32[]{:S(2)}) %collective-permute-start.12) | collective-permute-done | bytes 262176 | tf_op jit(solution)/shard_map/ppermute | solution.py:49
  85.8 0.5 collective-permute-done.13
  86.3 0.0 collective-permute-done.10
  86.3 0.0 collective-permute-done.11
  86.3 0.2 add_convert_fusion
  86.5 25.7 %all_to_all.17 = bf16[32,32,256]{2,1,0:T(8,128)(2,1)S(1)} all-to-all(bf16[32,32,256]{2,1,0:T(8,128)(2,1)S(1)} %bitcast.10), channel_id=1, replica_groups={{0,34,4,38,8,42,12,46,64,98,68,102,72,106,76,110,128,162,132,166,136,17..., dimensions={0} | all-to-all | bytes 1048576 | tf_op jit(solution)/shard_map/all_to_all | solution.py:38
  112.2 0.7 reduce_sum.12
  (5 shorter events, 0.1 us)
Async XLA Ops:
  20.9 6.2 %collective-permute-start = (bf16[256,256]{1,0:T(8,128)(2,1)S(1)}, bf16[256,256]{1,0:T(8,128)(2,1)S(1)}, u32[]{:S(2)}, u32[]{:S(2)}) collective-permute-start(bf16[256,256]{1,0:T(8,128)(2,1)S(1)} %bitcast.11), channel_id=1, source_target_pairs={{0,64},{1,17},{2,66},{3,19},{4,68},{5,21},{6,70},{7,23},{8,72},{9,... | collective-permute-start | bytes 393224 | tf_op jit(solution)/shard_map/ppermute | solution.py:49
  21.9 7.0 %collective-permute-start.1 = (bf16[256,256]{1,0:T(8,128)(2,1)S(1)}, bf16[256,256]{1,0:T(8,128)(2,1)S(1)}, u32[]{:S(2)}, u32[]{:S(2)}) collective-permute-start(bf16[256,256]{1,0:T(8,128)(2,1)S(1)} %bitcast.12), channel_id=1, source_target_pairs={{0,128},{1,33},{2,130},{3,35},{4,132},{5,37},{6,134},{7,39},{8,136... | collective-permute-start | bytes 393224 | tf_op jit(solution)/shard_map/ppermute | solution.py:49
  24.6 5.0 %collective-permute-start.2 = (bf16[256,256]{1,0:T(8,128)(2,1)S(1)}, bf16[256,256]{1,0:T(8,128)(2,1)S(1)}, u32[]{:S(2)}, u32[]{:S(2)}) collective-permute-start(bf16[256,256]{1,0:T(8,128)(2,1)S(1)} %bitcast.13), channel_id=1, source_target_pairs={{0,192},{1,49},{2,194},{3,51},{4,196},{5,53},{6,198},{7,55},{8,200... | collective-permute-start | bytes 393224 | tf_op jit(solution)/shard_map/ppermute | solution.py:49
  29.6 10.7 %collective-permute-start.3 = (bf16[1024,256]{1,0:T(8,128)(2,1)S(1)}, bf16[1024,256]{1,0:T(8,128)(2,1)S(1)}, u32[]{:S(2)}, u32[]{:S(2)}) collective-permute-start(bf16[1024,256]{1,0:T(8,128)(2,1)S(1)} %pad_maximum_fusion.a), channel_id=1, source_target_pairs={{0,48},{1,193},{2,50},{3,195},{4,52},{5,197},{6,54},{7,199},{8,56}... | collective-permute-start | bytes 1572872 | tf_op jit(solution)/shard_map/ppermute | solution.py:49
  31.4 9.2 %collective-permute-start.4 = (bf16[1024,256]{1,0:T(8,128)(2,1)S(1)}, bf16[1024,256]{1,0:T(8,128)(2,1)S(1)}, u32[]{:S(2)}, u32[]{:S(2)}) collective-permute-start(bf16[1024,256]{1,0:T(8,128)(2,1)S(1)} %pad_maximum_fusion.a), channel_id=1, source_target_pairs={{0,16},{1,65},{2,18},{3,67},{4,20},{5,69},{6,22},{7,71},{8,24},{9,... | collective-permute-start | bytes 1572872 | tf_op jit(solution)/shard_map/ppermute | solution.py:49
  31.7 7.0 %collective-permute-start.6 = (bf16[512,256]{1,0:T(8,128)(2,1)S(1)}, bf16[512,256]{1,0:T(8,128)(2,1)S(1)}, u32[]{:S(2)}, u32[]{:S(2)}) collective-permute-start(bf16[512,256]{1,0:T(8,128)(2,1)S(1)} %pad_maximum_fusion.2), channel_id=1, source_target_pairs={{0,14},{1,15},{2,0},{3,1},{4,2},{5,3},{6,4},{7,5},{8,6},{9,7},{10,... | collective-permute-start | bytes 786440 | tf_op jit(solution)/shard_map/ppermute | solution.py:49
  32.6 7.7 %collective-permute-start.5 = (bf16[512,256]{1,0:T(8,128)(2,1)S(1)}, bf16[512,256]{1,0:T(8,128)(2,1)S(1)}, u32[]{:S(2)}, u32[]{:S(2)}) collective-permute-start(bf16[512,256]{1,0:T(8,128)(2,1)S(1)} %pad_maximum_fusion.1), channel_id=1, source_target_pairs={{0,2},{1,3},{2,4},{3,5},{4,6},{5,7},{6,8},{7,9},{8,10},{9,11},{10,... | collective-permute-start | bytes 786440 | tf_op jit(solution)/shard_map/ppermute | solution.py:49
  33.9 3.4 %copy-start = (bf16[4096,1024]{1,0:T(8,128)(2,1)S(1)}, bf16[4096,1024]{1,0:T(8,128)(2,1)}, u32[]{:S(2)}) copy-start(bf16[4096,1024]{1,0:T(8,128)(2,1)} %head.7) | copy-start | bytes 25165828
  37.3 1.0 copy-start.1
  38.3 31.1 %slice-start = ((s8[8388608]{0:T(1024)(128)(4,1)}), s8[4194304]{0:T(1024)(128)(4,1)S(1)}, s32[]{:S(2)}) async-start(s8[8388608]{0:T(1024)(128)(4,1)} %bitcast.8), calls=%async_computation.3 | async-start | bytes 8388608
  40.6 28.9 %slice-start.1 = ((s8[8388608]{0:T(1024)(128)(4,1)}), s8[4194304]{0:T(1024)(128)(4,1)S(1)}, s32[]{:S(2)}) async-start(s8[8388608]{0:T(1024)(128)(4,1)} %bitcast.8), calls=%async_computation.4 | async-start | bytes 8388608
  44.1 4.0 %collective-permute-start.7 = (f32[6,128]{1,0:T(8,128)S(1)}, f32[6,128]{1,0:T(8,128)S(1)}, u32[]{:S(2)}, u32[]{:S(2)}) collective-permute-start(f32[6,128]{1,0:T(8,128)S(1)} %get-tuple-element.29.first), channel_id=1, source_target_pairs={{0,16},{1,65},{2,18},{3,67},{4,20},{5,69},{6,22},{7,71},{8,24},{9,... | collective-permute-start | bytes 9224 | tf_op jit(solution)/shard_map/ppermute | solution.py:49
  45.8 3.6 %collective-permute-start.8 = (f32[6,128]{1,0:T(8,128)S(1)}, f32[6,128]{1,0:T(8,128)S(1)}, u32[]{:S(2)}, u32[]{:S(2)}) collective-permute-start(f32[6,128]{1,0:T(8,128)S(1)} %get-tuple-element.29.first), channel_id=1, source_target_pairs={{0,48},{1,193},{2,50},{3,195},{4,52},{5,197},{6,54},{7,199},{8,56}... | collective-permute-start | bytes 9224 | tf_op jit(solution)/shard_map/ppermute | solution.py:49
  46.7 4.8 %collective-permute-start.9 = (f32[6,128]{1,0:T(8,128)S(1)}, f32[6,128]{1,0:T(8,128)S(1)}, u32[]{:S(2)}, u32[]{:S(2)}) collective-permute-start(f32[6,128]{1,0:T(8,128)S(1)} %get-tuple-element.29.first), channel_id=1, source_target_pairs={{0,2},{1,3},{2,4},{3,5},{4,6},{5,7},{6,8},{7,9},{8,10},{9,11},{10,... | collective-permute-start | bytes 9224 | tf_op jit(solution)/shard_map/ppermute | solution.py:49
  69.4 9.9 %collective-permute-start.14 = (bf16[2048,256]{1,0:T(8,128)(2,1)S(1)}, bf16[2048,256]{1,0:T(8,128)(2,1)S(1)}, u32[]{:S(2)}, u32[]{:S(2)}) collective-permute-start(bf16[2048,256]{1,0:T(8,128)(2,1)S(1)} %get-tuple-element.39), channel_id=1, source_target_pairs={{0,1},{1,0},{2,3},{3,2},{4,5},{5,4},{6,7},{7,6},{8,9},{9,8},{10,11... | collective-permute-start | bytes 3145736 | tf_op jit(solution)/shard_map/ppermute | solution.py:58
  71.8 5.9 %collective-permute-start.15 = (bf16[256,1024]{1,0:T(8,128)(2,1)S(1)}, bf16[256,1024]{1,0:T(8,128)(2,1)S(1)}, u32[]{:S(2)}, u32[]{:S(2)}) collective-permute-start(bf16[256,1024]{1,0:T(8,128)(2,1)S(1)} %get-tuple-element.40.score), channel_id=1, source_target_pairs={{0,1},{1,0},{2,3},{3,2},{4,5},{5,4},{6,7},{7,6},{8,9},{9,8},{10,11... | collective-permute-start | bytes 1572872 | tf_op jit(solution)/shard_map/ppermute | solution.py:58
  72.3 14.0 %collective-permute-start.10 = (bf16[1024,256]{1,0:T(8,128)(2,1)S(1)}, bf16[1024,256]{1,0:T(8,128)(2,1)S(1)}, u32[]{:S(2)}, u32[]{:S(2)}) collective-permute-start(bf16[1024,256]{1,0:T(8,128)(2,1)S(1)} %get-tuple-element.34), channel_id=1, source_target_pairs={{0,16},{1,65},{2,18},{3,67},{4,20},{5,69},{6,22},{7,71},{8,24},{9,... | collective-permute-start | bytes 1572872 | tf_op jit(solution)/shard_map/ppermute | solution.py:49
  74.5 11.8 %collective-permute-start.11 = (bf16[1024,256]{1,0:T(8,128)(2,1)S(1)}, bf16[1024,256]{1,0:T(8,128)(2,1)S(1)}, u32[]{:S(2)}, u32[]{:S(2)}) collective-permute-start(bf16[1024,256]{1,0:T(8,128)(2,1)S(1)} %get-tuple-element.35), channel_id=1, source_target_pairs={{0,48},{1,193},{2,50},{3,195},{4,52},{5,197},{6,54},{7,199},{8,56}... | collective-permute-start | bytes 1572872 | tf_op jit(solution)/shard_map/ppermute | solution.py:49
  76.0 9.8 %collective-permute-start.12 = (bf16[512,256]{1,0:T(8,128)(2,1)S(1)}, bf16[512,256]{1,0:T(8,128)(2,1)S(1)}, u32[]{:S(2)}, u32[]{:S(2)}) collective-permute-start(bf16[512,256]{1,0:T(8,128)(2,1)S(1)} %get-tuple-element.36), channel_id=1, source_target_pairs={{0,2},{1,3},{2,4},{3,5},{4,6},{5,7},{6,8},{7,9},{8,10},{9,11},{10,... | collective-permute-start | bytes 786440 | tf_op jit(solution)/shard_map/ppermute | solution.py:49
  77.7 8.6 %collective-permute-start.13 = (bf16[512,256]{1,0:T(8,128)(2,1)S(1)}, bf16[512,256]{1,0:T(8,128)(2,1)S(1)}, u32[]{:S(2)}, u32[]{:S(2)}) collective-permute-start(bf16[512,256]{1,0:T(8,128)(2,1)S(1)} %get-tuple-element.37), channel_id=1, source_target_pairs={{0,14},{1,15},{2,0},{3,1},{4,2},{5,3},{6,4},{7,5},{8,6},{9,7},{10,... | collective-permute-start | bytes 786440 | tf_op jit(solution)/shard_map/ppermute | solution.py:49

commit v8 on v7

--- a/solution.py
+++ b/solution.py
@@ -153,15 +153,16 @@
     stats[...] = jnp.broadcast_to(chunk[None], stats.shape)
 
 
-def times_head(own, core, head, score_t, outs):
-    for offset, j, ref in outs:
+def times_head(own, core, column, head, score_t, outs):
+    for offset, back, ref in outs:
+        j = lax.rem(column[0] - back + 4, 4)
         bases = [column_of(own, core, offset, j, odd) * SLAB for odd in range(2)]
         eighths = [head[pl.ds(pl.multiple_of(bases[z % 2] + 32 * z, 32), 32)] for z in range(NZ)]
         rows = jnp.concatenate(eighths, axis=0)
         ref[...] = jnp.dot(rows, score_t, preferred_element_type=f32).astype(ref.dtype)
 
 
-def score_kernel(own, core, rise, peak, prob, lse_t, stats, head, score, score_t, b, c, mismatch):
+def score_kernel(own, core, column, rise, peak, prob, lse_t, stats, head, score, score_t, b, c, mismatch):
     all_s, all_t, cross = merged(stats[...])
     mismatch[...] = sharpness_divisor * sharpness_divisor * (cross + all_s - all_t)
     end_s, end_t = as_columns(all_s, all_t)
@@ -172,13 +173,13 @@
     score[...] = rounded
     score_t[...] = jnp.transpose(rounded)
     outs = [(o, j, r.at[pl.ds(j * SLAB, SLAB)]) for o, r in ((1, b), (3, c)) for j in range(4)]
-    times_head(own, core, head, score_t[...], outs)
-
-
-def rest_kernel(own, core, score_t, head, d0, d1, a):
+    times_head(own, core, column, head, score_t[...], outs)
+
+
+def rest_kernel(own, core, column, score_t, head, d0, d1, a):
     outs = [(2, j, (d0, d1)[j // 2].at[pl.ds((j % 2) * SLAB, SLAB)]) for j in range(4)]
     outs += [(0, j, a.at[pl.ds(j * SLAB, SLAB)]) for j in range(4)]
-    times_head(own, core, head, score_t[...], outs)
+    times_head(own, core, column, head, score_t[...], outs)
 
 
 def weight_kernel(mine, theirs, score, score_theirs, out, held, sems):
@@ -236,7 +237,7 @@
     score, score_t, b, c, mismatch = call(
         score_kernel,
         [((ROWS, COLS), bf16), ((COLS, ROWS), bf16)] + [((1024, ROWS), bf16)] * 2 + [((2, 128), f32)],
-        [("s", own), ("s", core), ("v", rise), ("v", peak), ("v", prob), ("v", lse_t), ("v", stats), ("v", head_weight)],
+        [("s", own), ("s", core), ("s", column), ("v", rise), ("v", peak), ("v", prob), ("v", lse_t), ("v", stats), ("v", head_weight)],
         FULL * ROWS * COLS,
         8 * MIB,
     )
@@ -245,7 +246,7 @@
     d0, d1, a = call(
         rest_kernel,
         [((512, ROWS), bf16), ((512, ROWS), bf16), ((1024, ROWS), f32)],
-        [("s", own), ("s", core), ("v", score_t), ("v", head_weight)],
+        [("s", own), ("s", core), ("s", column), ("v", score_t), ("v", head_weight)],
         FULL * ROWS * COLS,
         7 * MIB,
     )
@@ -261,8 +262,12 @@
     )
     b, c, d0, d1, weight_grad = lax.optimization_barrier((b, c, d0, d1, weight_grad))
     part = a + b.astype(f32) + c.astype(f32) + jnp.concatenate([d0, d1], axis=0).astype(f32)
-    part = trade(part.astype(bf16).reshape(32, 32, ROWS), class_groups)
-    hidden_grad = jnp.sum(part.astype(f32), axis=0).astype(bf16).T
+    slabs = [part[i * SLAB : (i + 1) * SLAB] for i in range(4)]
+    total = slabs[0]
+    for i in (1, 2, 3):
+        total += step(slabs[i].astype(bf16), 0, -i, 0).astype(f32)
+    total = trade(total.astype(bf16).reshape(NZ, 32, ROWS), octets)
+    hidden_grad = jnp.sum(total.astype(f32), axis=0).astype(bf16).T
     return (hidden_grad, weight_grad, mismatch.reshape(ROWS))
 
 

time: 113 us -> 111 us (0.982)
  blocking collectives: 63.1 us -> 52.4 us
  waiting for transfers between devices: 12.8 us -> 19 us
  starting transfers between devices: 19.2 us -> 21.4 us
    all_to_all x3, blocking collectives: 63.1 us -> 52.4 us  [trade(): lax.all_to_all(chunks, BOTH, 0, 0, tiled=True, axis_index_groups=groups)]
    ppermute x14 -> x17, waiting for transfers between devices: 12.8 us -> 19 us  [step(): return lax.ppermute(value, BOTH, pairs)]
    ppermute x14 -> x17, starting transfers between devices: 18.8 us -> 20.9 us  [step(): return lax.ppermute(value, BOTH, pairs)]
  transfers between devices with their start and end apart: 16 -> 19, of which waited for: 10 -> 13; matrix products, arithmetic and copies ran while one was open for 0% -> 0% of each run, Pallas kernels for 6% -> 7%
where the time goes in v8:
time: 111 us; the launch traced here: 110 us
  blocking collectives  52.4 us (47%)
  starting transfers between devices  21.4 us (19%)
  waiting for transfers between devices  19 us (17%)
  Pallas kernels  10.7 us (10%)
  local copies, waits for them, and re-layouts  5.18 us (5%)
    all_to_all x3, blocking collectives, trade(): lax.all_to_all(chunks, BOTH, 0, 0, tiled=True, axis_index_groups=groups)  52.4 us
    ppermute x17, starting transfers between devices, step(): return lax.ppermute(value, BOTH, pairs)  20.9 us
    ppermute x17, waiting for transfers between devices, step(): return lax.ppermute(value, BOTH, pairs)  19 us
    pallas_call x6, Pallas kernels, call(): pl.pallas_call(body, out_shape=[jax.ShapeDtypeStruct(shape, dtype) for sh...  10.7 us
    unnamed x8, local copies, waits for them, and re-layouts  4.43 us
  transfers between devices with their start and end apart: 19, of which 13 were waited for; matrix products, arithmetic and copies ran while one was open for 0% of the time, Pallas kernels for 7%

profile of v8, /device:TPU:2, one launch (start us, length us, event | category | flops | bytes accessed | tf_op | source)
XLA Modules:
  0.0 110.5 jit_solution(8983682277442955155)
XLA Ops:
  0.6 0.7 broadcast_in_dim.18
  1.4 19.5 %all_to_all.15 = bf16[8,32,256]{2,1,0:T(8,128)(2,1)S(1)} all-to-all(bf16[8,32,256]{2,1,0:T(8,128)(2,1)S(1)} %broadcast_in_dim.18), channel_id=1, replica_groups={{0,34,4,38,8,42,12,46},{64,98,68,102,72,106,76,110},{128,162,132,166,13..., dimensions={0} | all-to-all | bytes 262144 | tf_op jit(solution)/shard_map/all_to_all | solution.py:38
  20.9 1.0 collective-permute-start
  21.9 2.7 %collective-permute-start.1 = (bf16[256,256]{1,0:T(8,128)(2,1)S(1)}, bf16[256,256]{1,0:T(8,128)(2,1)S(1)}, u32[]{:S(2)}, u32[]{:S(2)}) collective-permute-start(bf16[256,256]{1,0:T(8,128)(2,1)S(1)} %bitcast.11), channel_id=1, source_target_pairs={{0,128},{1,33},{2,130},{3,35},{4,132},{5,37},{6,134},{7,39},{8,136... | collective-permute-start | bytes 393224 | tf_op jit(solution)/shard_map/ppermute | solution.py:49
  24.6 1.3 %collective-permute-start.2 = (bf16[256,256]{1,0:T(8,128)(2,1)S(1)}, bf16[256,256]{1,0:T(8,128)(2,1)S(1)}, u32[]{:S(2)}, u32[]{:S(2)}) collective-permute-start(bf16[256,256]{1,0:T(8,128)(2,1)S(1)} %bitcast.12), channel_id=1, source_target_pairs={{0,192},{1,49},{2,194},{3,51},{4,196},{5,53},{6,198},{7,55},{8,200... | collective-permute-start | bytes 393224 | tf_op jit(solution)/shard_map/ppermute | solution.py:49
  25.9 1.1 %collective-permute-done = bf16[256,256]{1,0:T(8,128)(2,1)S(1)} collective-permute-done((bf16[256,256]{1,0:T(8,128)(2,1)S(1)}, bf16[256,256]{1,0:T(8,128)(2,1)S(1)}, u32[]{:S(2)}, u32[]{:S(2)}) %collective-permute-start) | collective-permute-done | bytes 131104 | tf_op jit(solution)/shard_map/ppermute | solution.py:49
  27.1 1.9 %collective-permute-done.1 = bf16[256,256]{1,0:T(8,128)(2,1)S(1)} collective-permute-done((bf16[256,256]{1,0:T(8,128)(2,1)S(1)}, bf16[256,256]{1,0:T(8,128)(2,1)S(1)}, u32[]{:S(2)}, u32[]{:S(2)}) %collective-permute-start.1) | collective-permute-done | bytes 131104 | tf_op jit(solution)/shard_map/ppermute | solution.py:49
  28.9 0.6 collective-permute-done.2
  29.6 1.8 %collective-permute-start.3 = (bf16[1024,256]{1,0:T(8,128)(2,1)S(1)}, bf16[1024,256]{1,0:T(8,128)(2,1)S(1)}, u32[]{:S(2)}, u32[]{:S(2)}) collective-permute-start(bf16[1024,256]{1,0:T(8,128)(2,1)S(1)} %pad_maximum_fusion.a), channel_id=1, source_target_pairs={{0,48},{1,193},{2,50},{3,195},{4,52},{5,197},{6,54},{7,199},{8,56}... | collective-permute-start | bytes 1572872 | tf_op jit(solution)/shard_map/ppermute | solution.py:49
  31.4 0.3 collective-permute-start.4
  31.7 0.9 collective-permute-start.6
  32.6 1.3 %collective-permute-start.5 = (bf16[512,256]{1,0:T(8,128)(2,1)S(1)}, bf16[512,256]{1,0:T(8,128)(2,1)S(1)}, u32[]{:S(2)}, u32[]{:S(2)}) collective-permute-start(bf16[512,256]{1,0:T(8,128)(2,1)S(1)} %pad_maximum_fusion.1), channel_id=1, source_target_pairs={{0,2},{1,3},{2,4},{3,5},{4,6},{5,7},{6,8},{7,9},{8,10},{9,11},{10,... | collective-permute-start | bytes 786440 | tf_op jit(solution)/shard_map/ppermute | solution.py:49
  33.9 0.0 copy-start
  33.9 3.4 %copy-done = bf16[4096,1024]{1,0:T(8,128)(2,1)S(1)} copy-done((bf16[4096,1024]{1,0:T(8,128)(2,1)S(1)}, bf16[4096,1024]{1,0:T(8,128)(2,1)}, u32[]{:S(2)}) %copy-start) | copy-done | bytes 8388632
  37.3 0.0 copy-start.1
  37.3 1.0 copy-done.1
  38.3 0.0 slice-start
  38.3 0.4 shard_map.58
  38.7 0.0 collective-permute-done.6.d1
  38.8 1.5 %collective-permute-done.5.d0 = bf16[512,256]{1,0:T(8,128)(2,1)S(1)} collective-permute-done((bf16[512,256]{1,0:T(8,128)(2,1)S(1)}, bf16[512,256]{1,0:T(8,128)(2,1)S(1)}, u32[]{:S(2)}, u32[]{:S(2)}) %collective-permute-start.5) | collective-permute-done | bytes 262176 | tf_op jit(solution)/shard_map/ppermute | solution.py:49
  40.3 0.0 collective-permute-done.3.b
  40.3 0.3 collective-permute-done.4.c
  40.6 0.0 slice-start.1
  40.6 3.5 %shard_map.59 = (f32[256,1024]{1,0:T(8,128)S(1)}, f32[256,128]{1,0:T(8,128)S(1)}, f32[6,128]{1,0:T(8,128)S(1)}, bf16[2048,256]{1,0:T(8,128)(2,1)S(1)}, bf16[2048,256]{1,0:T(8,128)(2,1)S(1)}) custom-call(s32[1]{0:T(128)} %bitcast.own, s32[1]{0:T(128)} %bitcast.1.core, s32[1]{0:T(128)} %bitcast.2.column, bf16[1024,256]{1,0:T(8,128)(2,1)S(1)} %pad_maximum_fusion.a, ...), custom_call_target="tpu_custom_call" | custom-call | flops 2147483648 | bytes 12582912 | tf_op jit(solution)/shard_map/pallas_call | solution.py:69
  44.1 1.7 %collective-permute-start.7 = (f32[6,128]{1,0:T(8,128)S(1)}, f32[6,128]{1,0:T(8,128)S(1)}, u32[]{:S(2)}, u32[]{:S(2)}) collective-permute-start(f32[6,128]{1,0:T(8,128)S(1)} %get-tuple-element.29.first), channel_id=1, source_target_pairs={{0,16},{1,65},{2,18},{3,67},{4,20},{5,69},{6,22},{7,71},{8,24},{9,... | collective-permute-start | bytes 9224 | tf_op jit(solution)/shard_map/ppermute | solution.py:49
  45.8 0.8 collective-permute-start.8
  46.6 1.1 %collective-permute-start.9 = (f32[6,128]{1,0:T(8,128)S(1)}, f32[6,128]{1,0:T(8,128)S(1)}, u32[]{:S(2)}, u32[]{:S(2)}) collective-permute-start(f32[6,128]{1,0:T(8,128)S(1)} %get-tuple-element.29.first), channel_id=1, source_target_pairs={{0,2},{1,3},{2,4},{3,5},{4,6},{5,7},{6,8},{7,9},{8,10},{9,11},{10,... | collective-permute-start | bytes 9224 | tf_op jit(solution)/shard_map/ppermute | solution.py:49
  47.8 0.3 collective-permute-done.7.second
  48.1 1.3 %collective-permute-done.8.third = f32[6,128]{1,0:T(8,128)S(1)} collective-permute-done((f32[6,128]{1,0:T(8,128)S(1)}, f32[6,128]{1,0:T(8,128)S(1)}, u32[]{:S(2)}, u32[]{:S(2)}) %collective-permute-start.8) | collective-permute-done | bytes 3104 | tf_op jit(solution)/shard_map/ppermute | solution.py:49
  49.4 2.1 %collective-permute-done.9.fourth = f32[6,128]{1,0:T(8,128)S(1)} collective-permute-done((f32[6,128]{1,0:T(8,128)S(1)}, f32[6,128]{1,0:T(8,128)S(1)}, u32[]{:S(2)}, u32[]{:S(2)}) %collective-permute-start.9) | collective-permute-done | bytes 3104 | tf_op jit(solution)/shard_map/ppermute | solution.py:49
  51.5 17.9 %all_to_all.16.stats = f32[32,6,128]{2,1,0:T(8,128)S(1)} all-to-all(f32[32,6,128]{2,1,0:T(8,128)S(1)} %shard_map.60), channel_id=1, replica_groups={{0,34,4,38,8,42,12,46,64,98,68,102,72,106,76,110,128,162,132,166,136,17..., dimensions={0} | all-to-all | bytes 196608 | tf_op jit(solution)/shard_map/all_to_all | solution.py:38
  69.4 0.0 collective-permute-start.14
  69.4 0.0 slice-done
  69.4 0.0 slice-done.1
  69.4 2.3 %shard_map.61 = (bf16[256,1024]{1,0:T(8,128)(2,1)S(1)}, bf16[1024,256]{1,0:T(8,128)(2,1)S(1)}, bf16[1024,256]{1,0:T(8,128)(2,1)S(1)}, bf16[1024,256]{1,0:T(8,128)(2,1)S(1)}, f32[2,128]{1,0:T(2,128)}) custom-call(s32[1]{0:T(128)} %bitcast.own, s32[1]{0:T(128)} %bitcast.1.core, s32[1]{0:T(128)} %bitcast.2.column, f32[256,1024]{1,0:T(8,128)S(1)} %get-tuple-element.27.rise, ...), custom_call_target="tpu_custom_call" | custom-call | flops 1073741824 | bytes 8388608 | tf_op jit(solution)/shard_map/pallas_call | solution.py:69
  71.8 0.5 collective-permute-start.15
  72.2 2.2 %collective-permute-start.10 = (bf16[1024,256]{1,0:T(8,128)(2,1)S(1)}, bf16[1024,256]{1,0:T(8,128)(2,1)S(1)}, u32[]{:S(2)}, u32[]{:S(2)}) collective-permute-start(bf16[1024,256]{1,0:T(8,128)(2,1)S(1)} %get-tuple-element.34), channel_id=1, source_target_pairs={{0,16},{1,65},{2,18},{3,67},{4,20},{5,69},{6,22},{7,71},{8,24},{9,... | collective-permute-start | bytes 1572872 | tf_op jit(solution)/shard_map/ppermute | solution.py:49
  74.5 0.2 collective-permute-start.11
  74.7 1.3 %shard_map.62 = (bf16[512,256]{1,0:T(8,128)(2,1)S(1)}, bf16[512,256]{1,0:T(8,128)(2,1)S(1)}, f32[1024,256]{1,0:T(8,128)S(1)}) custom-call(s32[1]{0:T(128)} %bitcast.own, s32[1]{0:T(128)} %bitcast.1.core, s32[1]{0:T(128)} %bitcast.2.column, bf16[1024,256]{1,0:T(8,128)(2,1)S(1)} %get-tuple-element.32.score_t, bf16[4096,1024]{1,0:T(8,128)(2,1)S(1)} %bitcast.9), custom_call_target="tpu_custom_call" | custom-call | flops 1073741824 | bytes 7340032 | tf_op jit(solution)/shard_map/pallas_call | solution.py:69
  75.9 1.7 %collective-permute-start.12 = (bf16[512,256]{1,0:T(8,128)(2,1)S(1)}, bf16[512,256]{1,0:T(8,128)(2,1)S(1)}, u32[]{:S(2)}, u32[]{:S(2)}) collective-permute-start(bf16[512,256]{1,0:T(8,128)(2,1)S(1)} %get-tuple-element.36), channel_id=1, source_target_pairs={{0,2},{1,3},{2,4},{3,5},{4,6},{5,7},{6,8},{7,9},{8,10},{9,11},{10,... | collective-permute-start | bytes 786440 | tf_op jit(solution)/shard_map/ppermute | solution.py:49
  77.6 0.0 collective-permute-done.15.score_theirs
  77.6 1.6 %collective-permute-start.13 = (bf16[512,256]{1,0:T(8,128)(2,1)S(1)}, bf16[512,256]{1,0:T(8,128)(2,1)S(1)}, u32[]{:S(2)}, u32[]{:S(2)}) collective-permute-start(bf16[512,256]{1,0:T(8,128)(2,1)S(1)} %get-tuple-element.37), channel_id=1, source_target_pairs={{0,14},{1,15},{2,0},{3,1},{4,2},{5,3},{6,4},{7,5},{8,6},{9,7},{10,... | collective-permute-start | bytes 786440 | tf_op jit(solution)/shard_map/ppermute | solution.py:49
  79.2 0.0 collective-permute-done.14.theirs
  79.2 3.2 %shard_map.63 = bf16[2048,1024]{1,0:T(8,128)(2,1)} custom-call(bf16[2048,256]{1,0:T(8,128)(2,1)S(1)} %get-tuple-element.38.mine, bf16[2048,256]{1,0:T(8,128)(2,1)S(1)} %collective-permute-done.14.theirs, bf16[256,1024]{1,0:T(8,128)(2,1)S(1)} %get-tuple-element.40.score, bf16[256,1024]{1,0:T(8,128)(2,1)S(1)} %collective-permute-done.15.score_theirs), custom_call_target="tpu_custom_call" | custom-call | flops 2147483648 | bytes 7340032 | tf_op jit(solution)/shard_map/pallas_call | solution.py:69
  82.5 3.2 %collective-permute-done.12 = bf16[512,256]{1,0:T(8,128)(2,1)S(1)} collective-permute-done((bf16[512,256]{1,0:T(8,128)(2,1)S(1)}, bf16[512,256]{1,0:T(8,128)(2,1)S(1)}, u32[]{:S(2)}, u32[]{:S(2)}) %collective-permute-start.12) | collective-permute-done | bytes 262176 | tf_op jit(solution)/shard_map/ppermute | solution.py:49
  85.7 0.5 collective-permute-done.13
  86.2 0.0 collective-permute-done.10
  86.2 0.0 collective-permute-done.11
  86.2 0.3 fusion.3
  86.6 0.4 collective-permute-start.16
  86.9 1.2 %collective-permute-start.17 = (bf16[256,256]{1,0:T(8,128)(2,1)S(1)}, bf16[256,256]{1,0:T(8,128)(2,1)S(1)}, u32[]{:S(2)}, u32[]{:S(2)}) collective-permute-start(bf16[256,256]{1,0:T(8,128)(2,1)S(1)} %get-tuple-element.51), channel_id=1, source_target_pairs={{0,128},{1,33},{2,130},{3,35},{4,132},{5,37},{6,134},{7,39},{8,136... | collective-permute-start | bytes 393224 | tf_op jit(solution)/shard_map/ppermute | solution.py:49
  88.1 0.5 collective-permute-start.18
  88.7 2.9 %collective-permute-done.16 = bf16[256,256]{1,0:T(8,128)(2,1)S(1)} collective-permute-done((bf16[256,256]{1,0:T(8,128)(2,1)S(1)}, bf16[256,256]{1,0:T(8,128)(2,1)S(1)}, u32[]{:S(2)}, u32[]{:S(2)}) %collective-permute-start.16) | collective-permute-done | bytes 131104 | tf_op jit(solution)/shard_map/ppermute | solution.py:49
  91.6 1.8 %collective-permute-done.17 = bf16[256,256]{1,0:T(8,128)(2,1)S(1)} collective-permute-done((bf16[256,256]{1,0:T(8,128)(2,1)S(1)}, bf16[256,256]{1,0:T(8,128)(2,1)S(1)}, u32[]{:S(2)}, u32[]{:S(2)}) %collective-permute-start.17) | collective-permute-done | bytes 131104 | tf_op jit(solution)/shard_map/ppermute | solution.py:49
  93.5 1.4 %collective-permute-done.18 = bf16[256,256]{1,0:T(8,128)(2,1)S(1)} collective-permute-done((bf16[256,256]{1,0:T(8,128)(2,1)S(1)}, bf16[256,256]{1,0:T(8,128)(2,1)S(1)}, u32[]{:S(2)}, u32[]{:S(2)}) %collective-permute-start.18) | collective-permute-done | bytes 131104 | tf_op jit(solution)/shard_map/ppermute | solution.py:49
  94.8 0.1 fusion.2
  94.9 15.0 %all_to_all.17 = bf16[8,32,256]{2,1,0:T(8,128)(2,1)S(1)} all-to-all(bf16[8,32,256]{2,1,0:T(8,128)(2,1)S(1)} %bitcast.15), channel_id=1, replica_groups={{0,34,4,38,8,42,12,46},{64,98,68,102,72,106,76,110},{128,162,132,166,13..., dimensions={0} | all-to-all | bytes 262144 | tf_op jit(solution)/shard_map/all_to_all | solution.py:38
  109.9 0.6 reduce_sum.12
  (6 shorter events, 0.1 us)
Async XLA Ops:
  20.9 6.2 %collective-permute-start = (bf16[256,256]{1,0:T(8,128)(2,1)S(1)}, bf16[256,256]{1,0:T(8,128)(2,1)S(1)}, u32[]{:S(2)}, u32[]{:S(2)}) collective-permute-start(bf16[256,256]{1,0:T(8,128)(2,1)S(1)} %bitcast.10), channel_id=1, source_target_pairs={{0,64},{1,17},{2,66},{3,19},{4,68},{5,21},{6,70},{7,23},{8,72},{9,... | collective-permute-start | bytes 393224 | tf_op jit(solution)/shard_map/ppermute | solution.py:49
  21.9 7.0 %collective-permute-start.1 = (bf16[256,256]{1,0:T(8,128)(2,1)S(1)}, bf16[256,256]{1,0:T(8,128)(2,1)S(1)}, u32[]{:S(2)}, u32[]{:S(2)}) collective-permute-start(bf16[256,256]{1,0:T(8,128)(2,1)S(1)} %bitcast.11), channel_id=1, source_target_pairs={{0,128},{1,33},{2,130},{3,35},{4,132},{5,37},{6,134},{7,39},{8,136... | collective-permute-start | bytes 393224 | tf_op jit(solution)/shard_map/ppermute | solution.py:49
  24.6 5.0 %collective-permute-start.2 = (bf16[256,256]{1,0:T(8,128)(2,1)S(1)}, bf16[256,256]{1,0:T(8,128)(2,1)S(1)}, u32[]{:S(2)}, u32[]{:S(2)}) collective-permute-start(bf16[256,256]{1,0:T(8,128)(2,1)S(1)} %bitcast.12), channel_id=1, source_target_pairs={{0,192},{1,49},{2,194},{3,51},{4,196},{5,53},{6,198},{7,55},{8,200... | collective-permute-start | bytes 393224 | tf_op jit(solution)/shard_map/ppermute | solution.py:49
  29.6 10.7 %collective-permute-start.3 = (bf16[1024,256]{1,0:T(8,128)(2,1)S(1)}, bf16[1024,256]{1,0:T(8,128)(2,1)S(1)}, u32[]{:S(2)}, u32[]{:S(2)}) collective-permute-start(bf16[1024,256]{1,0:T(8,128)(2,1)S(1)} %pad_maximum_fusion.a), channel_id=1, source_target_pairs={{0,48},{1,193},{2,50},{3,195},{4,52},{5,197},{6,54},{7,199},{8,56}... | collective-permute-start | bytes 1572872 | tf_op jit(solution)/shard_map/ppermute | solution.py:49
  31.4 9.2 %collective-permute-start.4 = (bf16[1024,256]{1,0:T(8,128)(2,1)S(1)}, bf16[1024,256]{1,0:T(8,128)(2,1)S(1)}, u32[]{:S(2)}, u32[]{:S(2)}) collective-permute-start(bf16[1024,256]{1,0:T(8,128)(2,1)S(1)} %pad_maximum_fusion.a), channel_id=1, source_target_pairs={{0,16},{1,65},{2,18},{3,67},{4,20},{5,69},{6,22},{7,71},{8,24},{9,... | collective-permute-start | bytes 1572872 | tf_op jit(solution)/shard_map/ppermute | solution.py:49
  31.7 7.0 %collective-permute-start.6 = (bf16[512,256]{1,0:T(8,128)(2,1)S(1)}, bf16[512,256]{1,0:T(8,128)(2,1)S(1)}, u32[]{:S(2)}, u32[]{:S(2)}) collective-permute-start(bf16[512,256]{1,0:T(8,128)(2,1)S(1)} %pad_maximum_fusion.2), channel_id=1, source_target_pairs={{0,14},{1,15},{2,0},{3,1},{4,2},{5,3},{6,4},{7,5},{8,6},{9,7},{10,... | collective-permute-start | bytes 786440 | tf_op jit(solution)/shard_map/ppermute | solution.py:49
  32.6 7.7 %collective-permute-start.5 = (bf16[512,256]{1,0:T(8,128)(2,1)S(1)}, bf16[512,256]{1,0:T(8,128)(2,1)S(1)}, u32[]{:S(2)}, u32[]{:S(2)}) collective-permute-start(bf16[512,256]{1,0:T(8,128)(2,1)S(1)} %pad_maximum_fusion.1), channel_id=1, source_target_pairs={{0,2},{1,3},{2,4},{3,5},{4,6},{5,7},{6,8},{7,9},{8,10},{9,11},{10,... | collective-permute-start | bytes 786440 | tf_op jit(solution)/shard_map/ppermute | solution.py:49
  33.9 3.4 %copy-start = (bf16[4096,1024]{1,0:T(8,128)(2,1)S(1)}, bf16[4096,1024]{1,0:T(8,128)(2,1)}, u32[]{:S(2)}) copy-start(bf16[4096,1024]{1,0:T(8,128)(2,1)} %head.7) | copy-start | bytes 25165828
  37.3 1.0 copy-start.1
  38.3 31.1 %slice-start = ((s8[8388608]{0:T(1024)(128)(4,1)}), s8[4194304]{0:T(1024)(128)(4,1)S(1)}, s32[]{:S(2)}) async-start(s8[8388608]{0:T(1024)(128)(4,1)} %bitcast.8), calls=%async_computation.3 | async-start | bytes 8388608
  40.6 28.8 %slice-start.1 = ((s8[8388608]{0:T(1024)(128)(4,1)}), s8[4194304]{0:T(1024)(128)(4,1)S(1)}, s32[]{:S(2)}) async-start(s8[8388608]{0:T(1024)(128)(4,1)} %bitcast.8), calls=%async_computation.4 | async-start | bytes 8388608
  44.1 4.0 %collective-permute-start.7 = (f32[6,128]{1,0:T(8,128)S(1)}, f32[6,128]{1,0:T(8,128)S(1)}, u32[]{:S(2)}, u32[]{:S(2)}) collective-permute-start(f32[6,128]{1,0:T(8,128)S(1)} %get-tuple-element.29.first), channel_id=1, source_target_pairs={{0,16},{1,65},{2,18},{3,67},{4,20},{5,69},{6,22},{7,71},{8,24},{9,... | collective-permute-start | bytes 9224 | tf_op jit(solution)/shard_map/ppermute | solution.py:49
  45.8 3.6 %collective-permute-start.8 = (f32[6,128]{1,0:T(8,128)S(1)}, f32[6,128]{1,0:T(8,128)S(1)}, u32[]{:S(2)}, u32[]{:S(2)}) collective-permute-start(f32[6,128]{1,0:T(8,128)S(1)} %get-tuple-element.29.first), channel_id=1, source_target_pairs={{0,48},{1,193},{2,50},{3,195},{4,52},{5,197},{6,54},{7,199},{8,56}... | collective-permute-start | bytes 9224 | tf_op jit(solution)/shard_map/ppermute | solution.py:49
  46.6 4.8 %collective-permute-start.9 = (f32[6,128]{1,0:T(8,128)S(1)}, f32[6,128]{1,0:T(8,128)S(1)}, u32[]{:S(2)}, u32[]{:S(2)}) collective-permute-start(f32[6,128]{1,0:T(8,128)S(1)} %get-tuple-element.29.first), channel_id=1, source_target_pairs={{0,2},{1,3},{2,4},{3,5},{4,6},{5,7},{6,8},{7,9},{8,10},{9,11},{10,... | collective-permute-start | bytes 9224 | tf_op jit(solution)/shard_map/ppermute | solution.py:49
  69.4 9.8 %collective-permute-start.14 = (bf16[2048,256]{1,0:T(8,128)(2,1)S(1)}, bf16[2048,256]{1,0:T(8,128)(2,1)S(1)}, u32[]{:S(2)}, u32[]{:S(2)}) collective-permute-start(bf16[2048,256]{1,0:T(8,128)(2,1)S(1)} %get-tuple-element.39), channel_id=1, source_target_pairs={{0,1},{1,0},{2,3},{3,2},{4,5},{5,4},{6,7},{7,6},{8,9},{9,8},{10,11... | collective-permute-start | bytes 3145736 | tf_op jit(solution)/shard_map/ppermute | solution.py:58
  71.8 5.9 %collective-permute-start.15 = (bf16[256,1024]{1,0:T(8,128)(2,1)S(1)}, bf16[256,1024]{1,0:T(8,128)(2,1)S(1)}, u32[]{:S(2)}, u32[]{:S(2)}) collective-permute-start(bf16[256,1024]{1,0:T(8,128)(2,1)S(1)} %get-tuple-element.40.score), channel_id=1, source_target_pairs={{0,1},{1,0},{2,3},{3,2},{4,5},{5,4},{6,7},{7,6},{8,9},{9,8},{10,11... | collective-permute-start | bytes 1572872 | tf_op jit(solution)/shard_map/ppermute | solution.py:58
  72.2 14.0 %collective-permute-start.10 = (bf16[1024,256]{1,0:T(8,128)(2,1)S(1)}, bf16[1024,256]{1,0:T(8,128)(2,1)S(1)}, u32[]{:S(2)}, u32[]{:S(2)}) collective-permute-start(bf16[1024,256]{1,0:T(8,128)(2,1)S(1)} %get-tuple-element.34), channel_id=1, source_target_pairs={{0,16},{1,65},{2,18},{3,67},{4,20},{5,69},{6,22},{7,71},{8,24},{9,... | collective-permute-start | bytes 1572872 | tf_op jit(solution)/shard_map/ppermute | solution.py:49
  74.5 11.8 %collective-permute-start.11 = (bf16[1024,256]{1,0:T(8,128)(2,1)S(1)}, bf16[1024,256]{1,0:T(8,128)(2,1)S(1)}, u32[]{:S(2)}, u32[]{:S(2)}) collective-permute-start(bf16[1024,256]{1,0:T(8,128)(2,1)S(1)} %get-tuple-element.35), channel_id=1, source_target_pairs={{0,48},{1,193},{2,50},{3,195},{4,52},{5,197},{6,54},{7,199},{8,56}... | collective-permute-start | bytes 1572872 | tf_op jit(solution)/shard_map/ppermute | solution.py:49
  75.9 9.8 %collective-permute-start.12 = (bf16[512,256]{1,0:T(8,128)(2,1)S(1)}, bf16[512,256]{1,0:T(8,128)(2,1)S(1)}, u32[]{:S(2)}, u32[]{:S(2)}) collective-permute-start(bf16[512,256]{1,0:T(8,128)(2,1)S(1)} %get-tuple-element.36), channel_id=1, source_target_pairs={{0,2},{1,3},{2,4},{3,5},{4,6},{5,7},{6,8},{7,9},{8,10},{9,11},{10,... | collective-permute-start | bytes 786440 | tf_op jit(solution)/shard_map/ppermute | solution.py:49
  77.6 8.6 %collective-permute-start.13 = (bf16[512,256]{1,0:T(8,128)(2,1)S(1)}, bf16[512,256]{1,0:T(8,128)(2,1)S(1)}, u32[]{:S(2)}, u32[]{:S(2)}) collective-permute-start(bf16[512,256]{1,0:T(8,128)(2,1)S(1)} %get-tuple-element.37), channel_id=1, source_target_pairs={{0,14},{1,15},{2,0},{3,1},{4,2},{5,3},{6,4},{7,5},{8,6},{9,7},{10,... | collective-permute-start | bytes 786440 | tf_op jit(solution)/shard_map/ppermute | solution.py:49
  86.6 5.0 %collective-permute-start.16 = (bf16[256,256]{1,0:T(8,128)(2,1)S(1)}, bf16[256,256]{1,0:T(8,128)(2,1)S(1)}, u32[]{:S(2)}, u32[]{:S(2)}) collective-permute-start(bf16[256,256]{1,0:T(8,128)(2,1)S(1)} %get-tuple-element.49), channel_id=1, source_target_pairs={{0,192},{1,49},{2,194},{3,51},{4,196},{5,53},{6,198},{7,55},{8,200... | collective-permute-start | bytes 393224 | tf_op jit(solution)/shard_map/ppermute | solution.py:49
  86.9 6.5 %collective-permute-start.17 = (bf16[256,256]{1,0:T(8,128)(2,1)S(1)}, bf16[256,256]{1,0:T(8,128)(2,1)S(1)}, u32[]{:S(2)}, u32[]{:S(2)}) collective-permute-start(bf16[256,256]{1,0:T(8,128)(2,1)S(1)} %get-tuple-element.51), channel_id=1, source_target_pairs={{0,128},{1,33},{2,130},{3,35},{4,132},{5,37},{6,134},{7,39},{8,136... | collective-permute-start | bytes 393224 | tf_op jit(solution)/shard_map/ppermute | solution.py:49
  88.1 6.7 %collective-permute-start.18 = (bf16[256,256]{1,0:T(8,128)(2,1)S(1)}, bf16[256,256]{1,0:T(8,128)(2,1)S(1)}, u32[]{:S(2)}, u32[]{:S(2)}) collective-permute-start(bf16[256,256]{1,0:T(8,128)(2,1)S(1)} %get-tuple-element.50), channel_id=1, source_target_pairs={{0,64},{1,17},{2,66},{3,19},{4,68},{5,21},{6,70},{7,23},{8,72},{9,... | collective-permute-start | bytes 393224 | tf_op jit(solution)/shard_map/ppermute | solution.py:49

commit v9 on v8

--- a/solution.py
+++ b/solution.py
@@ -231,8 +231,7 @@
         2 * FULL * ROWS * COLS,
         12 * MIB,
     )
-    stats, theirs = lax.optimization_barrier((stats_of_all(stats), theirs))
-    theirs = other_core(theirs)
+    stats = stats_of_all(stats)
 
     score, score_t, b, c, mismatch = call(
         score_kernel,
@@ -242,7 +241,6 @@
         8 * MIB,
     )
     b, c = step(b, 1, 0, 0), step(c, -1, 0, 0)
-    score_theirs = other_core(score)
     d0, d1, a = call(
         rest_kernel,
         [((512, ROWS), bf16), ((512, ROWS), bf16), ((1024, ROWS), f32)],
@@ -251,6 +249,11 @@
         7 * MIB,
     )
     d0, d1 = step(d0, 0, 0, 1), step(d1, 0, 0, -1)
+    part = a + b.astype(f32) + c.astype(f32) + jnp.concatenate([d0, d1], axis=0).astype(f32)
+    part, theirs, score_theirs = lax.optimization_barrier((part, theirs, score))
+    slabs = [part[i * SLAB : (i + 1) * SLAB] for i in range(4)]
+    arrived = [step(slabs[i].astype(bf16), 0, -i, 0) for i in (1, 2, 3)]
+    theirs, score_theirs = other_core(theirs), other_core(score_theirs)
     (weight_grad,) = call(
         weight_kernel,
         [((FULL // 2, COLS), bf16)],
@@ -260,12 +263,10 @@
         [pltpu.VMEM((8, SLAB, COLS), bf16), pltpu.SemaphoreType.DMA((8,))],
         into="h",
     )
-    b, c, d0, d1, weight_grad = lax.optimization_barrier((b, c, d0, d1, weight_grad))
-    part = a + b.astype(f32) + c.astype(f32) + jnp.concatenate([d0, d1], axis=0).astype(f32)
-    slabs = [part[i * SLAB : (i + 1) * SLAB] for i in range(4)]
+    *arrived, weight_grad = lax.optimization_barrier((*arrived, weight_grad))
     total = slabs[0]
-    for i in (1, 2, 3):
-        total += step(slabs[i].astype(bf16), 0, -i, 0).astype(f32)
+    for value in arrived:
+        total += value.astype(f32)
     total = trade(total.astype(bf16).reshape(NZ, 32, ROWS), octets)
     hidden_grad = jnp.sum(total.astype(f32), axis=0).astype(bf16).T
     return (hidden_grad, weight_grad, mismatch.reshape(ROWS))

time: 111 us -> 111 us (level); the launches traced: 110 us -> 109 us
  waiting for transfers between devices: 19 us -> 16.8 us
    ppermute x17, waiting for transfers between devices: 19 us -> 16.8 us  [step(): return lax.ppermute(value, BOTH, pairs)]
  transfers between devices with their start and end apart: 19 -> 19, of which waited for: 13 -> 12; matrix products, arithmetic and copies ran while one was open for 0% -> 0% of each run, Pallas kernels for 7% -> 4%
where the time goes in v9:
time: 111 us; the launch traced here: 109 us
  blocking collectives  52.4 us (47%)
  starting transfers between devices  22.2 us (20%)
  waiting for transfers between devices  16.8 us (15%)
  Pallas kernels  10.8 us (10%)
  local copies, waits for them, and re-layouts  5.18 us (5%)
    all_to_all x3, blocking collectives, trade(): lax.all_to_all(chunks, BOTH, 0, 0, tiled=True, axis_index_groups=groups)  52.4 us
    ppermute x17, starting transfers between devices, step(): return lax.ppermute(value, BOTH, pairs)  21.6 us
    ppermute x17, waiting for transfers between devices, step(): return lax.ppermute(value, BOTH, pairs)  16.8 us
    pallas_call x6, Pallas kernels, call(): pl.pallas_call(body, out_shape=[jax.ShapeDtypeStruct(shape, dtype) for sh...  10.8 us
    unnamed x8, local copies, waits for them, and re-layouts  4.43 us
  transfers between devices with their start and end apart: 19, of which 12 were waited for; matrix products, arithmetic and copies ran while one was open for 0% of the time, Pallas kernels for 4%

profile of v9, /device:TPU:2, one launch (start us, length us, event | category | flops | bytes accessed | tf_op | source)
XLA Modules:
  0.0 109.2 jit_solution(13846597484705797994)
XLA Ops:
  0.6 0.7 broadcast_in_dim.18
  1.4 19.5 %all_to_all.15 = bf16[8,32,256]{2,1,0:T(8,128)(2,1)S(1)} all-to-all(bf16[8,32,256]{2,1,0:T(8,128)(2,1)S(1)} %broadcast_in_dim.18), channel_id=1, replica_groups={{0,34,4,38,8,42,12,46},{64,98,68,102,72,106,76,110},{128,162,132,166,13..., dimensions={0} | all-to-all | bytes 262144 | tf_op jit(solution)/shard_map/all_to_all | solution.py:38
  20.9 1.0 collective-permute-start
  21.9 2.7 %collective-permute-start.1 = (bf16[256,256]{1,0:T(8,128)(2,1)S(1)}, bf16[256,256]{1,0:T(8,128)(2,1)S(1)}, u32[]{:S(2)}, u32[]{:S(2)}) collective-permute-start(bf16[256,256]{1,0:T(8,128)(2,1)S(1)} %bitcast.11), channel_id=1, source_target_pairs={{0,128},{1,33},{2,130},{3,35},{4,132},{5,37},{6,134},{7,39},{8,136... | collective-permute-start | bytes 393224 | tf_op jit(solution)/shard_map/ppermute | solution.py:49
  24.6 1.3 %collective-permute-start.2 = (bf16[256,256]{1,0:T(8,128)(2,1)S(1)}, bf16[256,256]{1,0:T(8,128)(2,1)S(1)}, u32[]{:S(2)}, u32[]{:S(2)}) collective-permute-start(bf16[256,256]{1,0:T(8,128)(2,1)S(1)} %bitcast.12), channel_id=1, source_target_pairs={{0,192},{1,49},{2,194},{3,51},{4,196},{5,53},{6,198},{7,55},{8,200... | collective-permute-start | bytes 393224 | tf_op jit(solution)/shard_map/ppermute | solution.py:49
  25.9 1.1 %collective-permute-done = bf16[256,256]{1,0:T(8,128)(2,1)S(1)} collective-permute-done((bf16[256,256]{1,0:T(8,128)(2,1)S(1)}, bf16[256,256]{1,0:T(8,128)(2,1)S(1)}, u32[]{:S(2)}, u32[]{:S(2)}) %collective-permute-start) | collective-permute-done | bytes 131104 | tf_op jit(solution)/shard_map/ppermute | solution.py:49
  27.1 1.9 %collective-permute-done.1 = bf16[256,256]{1,0:T(8,128)(2,1)S(1)} collective-permute-done((bf16[256,256]{1,0:T(8,128)(2,1)S(1)}, bf16[256,256]{1,0:T(8,128)(2,1)S(1)}, u32[]{:S(2)}, u32[]{:S(2)}) %collective-permute-start.1) | collective-permute-done | bytes 131104 | tf_op jit(solution)/shard_map/ppermute | solution.py:49
  28.9 0.6 collective-permute-done.2
  29.6 1.8 %collective-permute-start.3 = (bf16[1024,256]{1,0:T(8,128)(2,1)S(1)}, bf16[1024,256]{1,0:T(8,128)(2,1)S(1)}, u32[]{:S(2)}, u32[]{:S(2)}) collective-permute-start(bf16[1024,256]{1,0:T(8,128)(2,1)S(1)} %pad_maximum_fusion.a), channel_id=1, source_target_pairs={{0,48},{1,193},{2,50},{3,195},{4,52},{5,197},{6,54},{7,199},{8,56}... | collective-permute-start | bytes 1572872 | tf_op jit(solution)/shard_map/ppermute | solution.py:49
  31.4 0.3 collective-permute-start.4
  31.7 0.9 collective-permute-start.6
  32.6 1.3 %collective-permute-start.5 = (bf16[512,256]{1,0:T(8,128)(2,1)S(1)}, bf16[512,256]{1,0:T(8,128)(2,1)S(1)}, u32[]{:S(2)}, u32[]{:S(2)}) collective-permute-start(bf16[512,256]{1,0:T(8,128)(2,1)S(1)} %pad_maximum_fusion.1), channel_id=1, source_target_pairs={{0,2},{1,3},{2,4},{3,5},{4,6},{5,7},{6,8},{7,9},{8,10},{9,11},{10,... | collective-permute-start | bytes 786440 | tf_op jit(solution)/shard_map/ppermute | solution.py:49
  33.9 0.0 copy-start
  33.9 3.4 %copy-done = bf16[4096,1024]{1,0:T(8,128)(2,1)S(1)} copy-done((bf16[4096,1024]{1,0:T(8,128)(2,1)S(1)}, bf16[4096,1024]{1,0:T(8,128)(2,1)}, u32[]{:S(2)}) %copy-start) | copy-done | bytes 8388632
  37.3 0.0 copy-start.1
  37.3 1.0 copy-done.1
  38.3 0.0 slice-start
  38.3 0.4 shard_map.58
  38.7 0.0 collective-permute-done.6.d1
  38.8 1.5 %collective-permute-done.5.d0 = bf16[512,256]{1,0:T(8,128)(2,1)S(1)} collective-permute-done((bf16[512,256]{1,0:T(8,128)(2,1)S(1)}, bf16[512,256]{1,0:T(8,128)(2,1)S(1)}, u32[]{:S(2)}, u32[]{:S(2)}) %collective-permute-start.5) | collective-permute-done | bytes 262176 | tf_op jit(solution)/shard_map/ppermute | solution.py:49
  40.3 0.0 collective-permute-done.3.b
  40.3 0.3 collective-permute-done.4.c
  40.6 0.0 slice-start.1
  40.6 3.5 %shard_map.59 = (f32[256,1024]{1,0:T(8,128)S(1)}, f32[256,128]{1,0:T(8,128)S(1)}, f32[6,128]{1,0:T(8,128)S(1)}, bf16[2048,256]{1,0:T(8,128)(2,1)S(1)}, bf16[2048,256]{1,0:T(8,128)(2,1)S(1)}) custom-call(s32[1]{0:T(128)} %bitcast.own, s32[1]{0:T(128)} %bitcast.1.core, s32[1]{0:T(128)} %bitcast.2.column, bf16[1024,256]{1,0:T(8,128)(2,1)S(1)} %pad_maximum_fusion.a, ...), custom_call_target="tpu_custom_call" | custom-call | flops 2147483648 | bytes 12582912 | tf_op jit(solution)/shard_map/pallas_call | solution.py:69
  44.1 1.7 %collective-permute-start.7 = (f32[6,128]{1,0:T(8,128)S(1)}, f32[6,128]{1,0:T(8,128)S(1)}, u32[]{:S(2)}, u32[]{:S(2)}) collective-permute-start(f32[6,128]{1,0:T(8,128)S(1)} %get-tuple-element.29.first), channel_id=1, source_target_pairs={{0,16},{1,65},{2,18},{3,67},{4,20},{5,69},{6,22},{7,71},{8,24},{9,... | collective-permute-start | bytes 9224 | tf_op jit(solution)/shard_map/ppermute | solution.py:49
  45.8 0.8 collective-permute-start.8
  46.6 1.1 %collective-permute-start.9 = (f32[6,128]{1,0:T(8,128)S(1)}, f32[6,128]{1,0:T(8,128)S(1)}, u32[]{:S(2)}, u32[]{:S(2)}) collective-permute-start(f32[6,128]{1,0:T(8,128)S(1)} %get-tuple-element.29.first), channel_id=1, source_target_pairs={{0,2},{1,3},{2,4},{3,5},{4,6},{5,7},{6,8},{7,9},{8,10},{9,11},{10,... | collective-permute-start | bytes 9224 | tf_op jit(solution)/shard_map/ppermute | solution.py:49
  47.8 0.3 collective-permute-done.7.second
  48.1 1.3 %collective-permute-done.8.third = f32[6,128]{1,0:T(8,128)S(1)} collective-permute-done((f32[6,128]{1,0:T(8,128)S(1)}, f32[6,128]{1,0:T(8,128)S(1)}, u32[]{:S(2)}, u32[]{:S(2)}) %collective-permute-start.8) | collective-permute-done | bytes 3104 | tf_op jit(solution)/shard_map/ppermute | solution.py:49
  49.4 2.1 %collective-permute-done.9.fourth = f32[6,128]{1,0:T(8,128)S(1)} collective-permute-done((f32[6,128]{1,0:T(8,128)S(1)}, f32[6,128]{1,0:T(8,128)S(1)}, u32[]{:S(2)}, u32[]{:S(2)}) %collective-permute-start.9) | collective-permute-done | bytes 3104 | tf_op jit(solution)/shard_map/ppermute | solution.py:49
  51.5 17.9 %all_to_all.16.stats = f32[32,6,128]{2,1,0:T(8,128)S(1)} all-to-all(f32[32,6,128]{2,1,0:T(8,128)S(1)} %shard_map.60), channel_id=1, replica_groups={{0,34,4,38,8,42,12,46,64,98,68,102,72,106,76,110,128,162,132,166,136,17..., dimensions={0} | all-to-all | bytes 196608 | tf_op jit(solution)/shard_map/all_to_all | solution.py:38
  69.4 0.0 slice-done
  69.4 0.0 slice-done.1
  69.4 2.3 %shard_map.61 = (bf16[256,1024]{1,0:T(8,128)(2,1)S(1)}, bf16[1024,256]{1,0:T(8,128)(2,1)S(1)}, bf16[1024,256]{1,0:T(8,128)(2,1)S(1)}, bf16[1024,256]{1,0:T(8,128)(2,1)S(1)}, f32[2,128]{1,0:T(2,128)}) custom-call(s32[1]{0:T(128)} %bitcast.own, s32[1]{0:T(128)} %bitcast.1.core, s32[1]{0:T(128)} %bitcast.2.column, f32[256,1024]{1,0:T(8,128)S(1)} %get-tuple-element.27.rise, ...), custom_call_target="tpu_custom_call" | custom-call | flops 1073741824 | bytes 8388608 | tf_op jit(solution)/shard_map/pallas_call | solution.py:69
  71.7 2.2 %collective-permute-start.10 = (bf16[1024,256]{1,0:T(8,128)(2,1)S(1)}, bf16[1024,256]{1,0:T(8,128)(2,1)S(1)}, u32[]{:S(2)}, u32[]{:S(2)}) collective-permute-start(bf16[1024,256]{1,0:T(8,128)(2,1)S(1)} %get-tuple-element.32), channel_id=1, source_target_pairs={{0,16},{1,65},{2,18},{3,67},{4,20},{5,69},{6,22},{7,71},{8,24},{9,... | collective-permute-start | bytes 1572872 | tf_op jit(solution)/shard_map/ppermute | solution.py:49
  73.9 0.2 collective-permute-start.11
  74.2 1.3 %shard_map.62 = (bf16[512,256]{1,0:T(8,128)(2,1)S(1)}, bf16[512,256]{1,0:T(8,128)(2,1)S(1)}, f32[1024,256]{1,0:T(8,128)S(1)}) custom-call(s32[1]{0:T(128)} %bitcast.own, s32[1]{0:T(128)} %bitcast.1.core, s32[1]{0:T(128)} %bitcast.2.column, bf16[1024,256]{1,0:T(8,128)(2,1)S(1)} %get-tuple-element.30.score_t, bf16[4096,1024]{1,0:T(8,128)(2,1)S(1)} %bitcast.9), custom_call_target="tpu_custom_call" | custom-call | flops 1073741824 | bytes 7340032 | tf_op jit(solution)/shard_map/pallas_call | solution.py:69
  75.4 1.7 %collective-permute-start.12 = (bf16[512,256]{1,0:T(8,128)(2,1)S(1)}, bf16[512,256]{1,0:T(8,128)(2,1)S(1)}, u32[]{:S(2)}, u32[]{:S(2)}) collective-permute-start(bf16[512,256]{1,0:T(8,128)(2,1)S(1)} %get-tuple-element.34), channel_id=1, source_target_pairs={{0,2},{1,3},{2,4},{3,5},{4,6},{5,7},{6,8},{7,9},{8,10},{9,11},{10,... | collective-permute-start | bytes 786440 | tf_op jit(solution)/shard_map/ppermute | solution.py:49
  77.1 1.6 %collective-permute-start.13 = (bf16[512,256]{1,0:T(8,128)(2,1)S(1)}, bf16[512,256]{1,0:T(8,128)(2,1)S(1)}, u32[]{:S(2)}, u32[]{:S(2)}) collective-permute-start(bf16[512,256]{1,0:T(8,128)(2,1)S(1)} %get-tuple-element.35), channel_id=1, source_target_pairs={{0,14},{1,15},{2,0},{3,1},{4,2},{5,3},{6,4},{7,5},{8,6},{9,7},{10,... | collective-permute-start | bytes 786440 | tf_op jit(solution)/shard_map/ppermute | solution.py:49
  78.7 4.3 %collective-permute-done.12 = bf16[512,256]{1,0:T(8,128)(2,1)S(1)} collective-permute-done((bf16[512,256]{1,0:T(8,128)(2,1)S(1)}, bf16[512,256]{1,0:T(8,128)(2,1)S(1)}, u32[]{:S(2)}, u32[]{:S(2)}) %collective-permute-start.12) | collective-permute-done | bytes 262176 | tf_op jit(solution)/shard_map/ppermute | solution.py:49
  83.1 0.4 collective-permute-done.13
  83.5 0.0 collective-permute-done.10
  83.5 0.0 collective-permute-done.11
  83.5 0.3 convert_add_fusion
  83.8 0.1 collective-permute-start.17
  83.9 0.5 collective-permute-start.18
  84.4 0.1 convert.6
  84.4 1.2 %collective-permute-start.14 = (bf16[256,256]{1,0:T(8,128)(2,1)S(1)}, bf16[256,256]{1,0:T(8,128)(2,1)S(1)}, u32[]{:S(2)}, u32[]{:S(2)}) collective-permute-start(bf16[256,256]{1,0:T(8,128)(2,1)S(1)} %get-tuple-element.49), channel_id=1, source_target_pairs={{0,192},{1,49},{2,194},{3,51},{4,196},{5,53},{6,198},{7,55},{8,200... | collective-permute-start | bytes 393224 | tf_op jit(solution)/shard_map/ppermute | solution.py:49
  85.7 1.6 %collective-permute-start.15 = (bf16[256,256]{1,0:T(8,128)(2,1)S(1)}, bf16[256,256]{1,0:T(8,128)(2,1)S(1)}, u32[]{:S(2)}, u32[]{:S(2)}) collective-permute-start(bf16[256,256]{1,0:T(8,128)(2,1)S(1)} %get-tuple-element.48), channel_id=1, source_target_pairs={{0,128},{1,33},{2,130},{3,35},{4,132},{5,37},{6,134},{7,39},{8,136... | collective-permute-start | bytes 393224 | tf_op jit(solution)/shard_map/ppermute | solution.py:49
  87.3 0.0 collective-permute-start.16
  87.3 0.0 collective-permute-done.18.score_theirs
  87.3 0.0 collective-permute-done.17.theirs
  87.3 3.3 %shard_map.63 = bf16[2048,1024]{1,0:T(8,128)(2,1)} custom-call(bf16[2048,256]{1,0:T(8,128)(2,1)S(1)} %get-tuple-element.39.mine, bf16[2048,256]{1,0:T(8,128)(2,1)S(1)} %collective-permute-done.17.theirs, bf16[256,1024]{1,0:T(8,128)(2,1)S(1)} %get-tuple-element.41.score, bf16[256,1024]{1,0:T(8,128)(2,1)S(1)} %collective-permute-done.18.score_theirs), custom_call_target="tpu_custom_call" | custom-call | flops 2147483648 | bytes 7340032 | tf_op jit(solution)/shard_map/pallas_call | solution.py:69
  90.6 0.0 collective-permute-done.14
  90.6 1.5 %collective-permute-done.15 = bf16[256,256]{1,0:T(8,128)(2,1)S(1)} collective-permute-done((bf16[256,256]{1,0:T(8,128)(2,1)S(1)}, bf16[256,256]{1,0:T(8,128)(2,1)S(1)}, u32[]{:S(2)}, u32[]{:S(2)}) %collective-permute-start.15) | collective-permute-done | bytes 131104 | tf_op jit(solution)/shard_map/ppermute | solution.py:49
  92.1 1.4 %collective-permute-done.16 = bf16[256,256]{1,0:T(8,128)(2,1)S(1)} collective-permute-done((bf16[256,256]{1,0:T(8,128)(2,1)S(1)}, bf16[256,256]{1,0:T(8,128)(2,1)S(1)}, u32[]{:S(2)}, u32[]{:S(2)}) %collective-permute-start.16) | collective-permute-done | bytes 131104 | tf_op jit(solution)/shard_map/ppermute | solution.py:49
  93.5 0.1 add_convert_fusion
  93.6 14.9 %all_to_all.17 = bf16[8,32,256]{2,1,0:T(8,128)(2,1)S(1)} all-to-all(bf16[8,32,256]{2,1,0:T(8,128)(2,1)S(1)} %bitcast.15), channel_id=1, replica_groups={{0,34,4,38,8,42,12,46},{64,98,68,102,72,106,76,110},{128,162,132,166,13..., dimensions={0} | all-to-all | bytes 262144 | tf_op jit(solution)/shard_map/all_to_all | solution.py:38
  108.6 0.6 reduce_sum.12
  (6 shorter events, 0.1 us)
Async XLA Ops:
  20.9 6.2 %collective-permute-start = (bf16[256,256]{1,0:T(8,128)(2,1)S(1)}, bf16[256,256]{1,0:T(8,128)(2,1)S(1)}, u32[]{:S(2)}, u32[]{:S(2)}) collective-permute-start(bf16[256,256]{1,0:T(8,128)(2,1)S(1)} %bitcast.10), channel_id=1, source_target_pairs={{0,64},{1,17},{2,66},{3,19},{4,68},{5,21},{6,70},{7,23},{8,72},{9,... | collective-permute-start | bytes 393224 | tf_op jit(solution)/shard_map/ppermute | solution.py:49
  21.9 7.0 %collective-permute-start.1 = (bf16[256,256]{1,0:T(8,128)(2,1)S(1)}, bf16[256,256]{1,0:T(8,128)(2,1)S(1)}, u32[]{:S(2)}, u32[]{:S(2)}) collective-permute-start(bf16[256,256]{1,0:T(8,128)(2,1)S(1)} %bitcast.11), channel_id=1, source_target_pairs={{0,128},{1,33},{2,130},{3,35},{4,132},{5,37},{6,134},{7,39},{8,136... | collective-permute-start | bytes 393224 | tf_op jit(solution)/shard_map/ppermute | solution.py:49
  24.6 5.0 %collective-permute-start.2 = (bf16[256,256]{1,0:T(8,128)(2,1)S(1)}, bf16[256,256]{1,0:T(8,128)(2,1)S(1)}, u32[]{:S(2)}, u32[]{:S(2)}) collective-permute-start(bf16[256,256]{1,0:T(8,128)(2,1)S(1)} %bitcast.12), channel_id=1, source_target_pairs={{0,192},{1,49},{2,194},{3,51},{4,196},{5,53},{6,198},{7,55},{8,200... | collective-permute-start | bytes 393224 | tf_op jit(solution)/shard_map/ppermute | solution.py:49
  29.6 10.7 %collective-permute-start.3 = (bf16[1024,256]{1,0:T(8,128)(2,1)S(1)}, bf16[1024,256]{1,0:T(8,128)(2,1)S(1)}, u32[]{:S(2)}, u32[]{:S(2)}) collective-permute-start(bf16[1024,256]{1,0:T(8,128)(2,1)S(1)} %pad_maximum_fusion.a), channel_id=1, source_target_pairs={{0,48},{1,193},{2,50},{3,195},{4,52},{5,197},{6,54},{7,199},{8,56}... | collective-permute-start | bytes 1572872 | tf_op jit(solution)/shard_map/ppermute | solution.py:49
  31.4 9.2 %collective-permute-start.4 = (bf16[1024,256]{1,0:T(8,128)(2,1)S(1)}, bf16[1024,256]{1,0:T(8,128)(2,1)S(1)}, u32[]{:S(2)}, u32[]{:S(2)}) collective-permute-start(bf16[1024,256]{1,0:T(8,128)(2,1)S(1)} %pad_maximum_fusion.a), channel_id=1, source_target_pairs={{0,16},{1,65},{2,18},{3,67},{4,20},{5,69},{6,22},{7,71},{8,24},{9,... | collective-permute-start | bytes 1572872 | tf_op jit(solution)/shard_map/ppermute | solution.py:49
  31.7 7.0 %collective-permute-start.6 = (bf16[512,256]{1,0:T(8,128)(2,1)S(1)}, bf16[512,256]{1,0:T(8,128)(2,1)S(1)}, u32[]{:S(2)}, u32[]{:S(2)}) collective-permute-start(bf16[512,256]{1,0:T(8,128)(2,1)S(1)} %pad_maximum_fusion.2), channel_id=1, source_target_pairs={{0,14},{1,15},{2,0},{3,1},{4,2},{5,3},{6,4},{7,5},{8,6},{9,7},{10,... | collective-permute-start | bytes 786440 | tf_op jit(solution)/shard_map/ppermute | solution.py:49
  32.6 7.7 %collective-permute-start.5 = (bf16[512,256]{1,0:T(8,128)(2,1)S(1)}, bf16[512,256]{1,0:T(8,128)(2,1)S(1)}, u32[]{:S(2)}, u32[]{:S(2)}) collective-permute-start(bf16[512,256]{1,0:T(8,128)(2,1)S(1)} %pad_maximum_fusion.1), channel_id=1, source_target_pairs={{0,2},{1,3},{2,4},{3,5},{4,6},{5,7},{6,8},{7,9},{8,10},{9,11},{10,... | collective-permute-start | bytes 786440 | tf_op jit(solution)/shard_map/ppermute | solution.py:49
  33.9 3.4 %copy-start = (bf16[4096,1024]{1,0:T(8,128)(2,1)S(1)}, bf16[4096,1024]{1,0:T(8,128)(2,1)}, u32[]{:S(2)}) copy-start(bf16[4096,1024]{1,0:T(8,128)(2,1)} %head.7) | copy-start | bytes 25165828
  37.3 1.0 copy-start.1
  38.3 31.1 %slice-start = ((s8[8388608]{0:T(1024)(128)(4,1)}), s8[4194304]{0:T(1024)(128)(4,1)S(1)}, s32[]{:S(2)}) async-start(s8[8388608]{0:T(1024)(128)(4,1)} %bitcast.8), calls=%async_computation.3 | async-start | bytes 8388608
  40.6 28.8 %slice-start.1 = ((s8[8388608]{0:T(1024)(128)(4,1)}), s8[4194304]{0:T(1024)(128)(4,1)S(1)}, s32[]{:S(2)}) async-start(s8[8388608]{0:T(1024)(128)(4,1)} %bitcast.8), calls=%async_computation.4 | async-start | bytes 8388608
  44.1 4.0 %collective-permute-start.7 = (f32[6,128]{1,0:T(8,128)S(1)}, f32[6,128]{1,0:T(8,128)S(1)}, u32[]{:S(2)}, u32[]{:S(2)}) collective-permute-start(f32[6,128]{1,0:T(8,128)S(1)} %get-tuple-element.29.first), channel_id=1, source_target_pairs={{0,16},{1,65},{2,18},{3,67},{4,20},{5,69},{6,22},{7,71},{8,24},{9,... | collective-permute-start | bytes 9224 | tf_op jit(solution)/shard_map/ppermute | solution.py:49
  45.8 3.6 %collective-permute-start.8 = (f32[6,128]{1,0:T(8,128)S(1)}, f32[6,128]{1,0:T(8,128)S(1)}, u32[]{:S(2)}, u32[]{:S(2)}) collective-permute-start(f32[6,128]{1,0:T(8,128)S(1)} %get-tuple-element.29.first), channel_id=1, source_target_pairs={{0,48},{1,193},{2,50},{3,195},{4,52},{5,197},{6,54},{7,199},{8,56}... | collective-permute-start | bytes 9224 | tf_op jit(solution)/shard_map/ppermute | solution.py:49
  46.6 4.8 %collective-permute-start.9 = (f32[6,128]{1,0:T(8,128)S(1)}, f32[6,128]{1,0:T(8,128)S(1)}, u32[]{:S(2)}, u32[]{:S(2)}) collective-permute-start(f32[6,128]{1,0:T(8,128)S(1)} %get-tuple-element.29.first), channel_id=1, source_target_pairs={{0,2},{1,3},{2,4},{3,5},{4,6},{5,7},{6,8},{7,9},{8,10},{9,11},{10,... | collective-permute-start | bytes 9224 | tf_op jit(solution)/shard_map/ppermute | solution.py:49
  71.7 11.7 %collective-permute-start.10 = (bf16[1024,256]{1,0:T(8,128)(2,1)S(1)}, bf16[1024,256]{1,0:T(8,128)(2,1)S(1)}, u32[]{:S(2)}, u32[]{:S(2)}) collective-permute-start(bf16[1024,256]{1,0:T(8,128)(2,1)S(1)} %get-tuple-element.32), channel_id=1, source_target_pairs={{0,16},{1,65},{2,18},{3,67},{4,20},{5,69},{6,22},{7,71},{8,24},{9,... | collective-permute-start | bytes 1572872 | tf_op jit(solution)/shard_map/ppermute | solution.py:49
  73.9 9.5 %collective-permute-start.11 = (bf16[1024,256]{1,0:T(8,128)(2,1)S(1)}, bf16[1024,256]{1,0:T(8,128)(2,1)S(1)}, u32[]{:S(2)}, u32[]{:S(2)}) collective-permute-start(bf16[1024,256]{1,0:T(8,128)(2,1)S(1)} %get-tuple-element.33), channel_id=1, source_target_pairs={{0,48},{1,193},{2,50},{3,195},{4,52},{5,197},{6,54},{7,199},{8,56}... | collective-permute-start | bytes 1572872 | tf_op jit(solution)/shard_map/ppermute | solution.py:49
  75.4 7.7 %collective-permute-start.12 = (bf16[512,256]{1,0:T(8,128)(2,1)S(1)}, bf16[512,256]{1,0:T(8,128)(2,1)S(1)}, u32[]{:S(2)}, u32[]{:S(2)}) collective-permute-start(bf16[512,256]{1,0:T(8,128)(2,1)S(1)} %get-tuple-element.34), channel_id=1, source_target_pairs={{0,2},{1,3},{2,4},{3,5},{4,6},{5,7},{6,8},{7,9},{8,10},{9,11},{10,... | collective-permute-start | bytes 786440 | tf_op jit(solution)/shard_map/ppermute | solution.py:49
  77.1 6.4 %collective-permute-start.13 = (bf16[512,256]{1,0:T(8,128)(2,1)S(1)}, bf16[512,256]{1,0:T(8,128)(2,1)S(1)}, u32[]{:S(2)}, u32[]{:S(2)}) collective-permute-start(bf16[512,256]{1,0:T(8,128)(2,1)S(1)} %get-tuple-element.35), channel_id=1, source_target_pairs={{0,14},{1,15},{2,0},{3,1},{4,2},{5,3},{6,4},{7,5},{8,6},{9,7},{10,... | collective-permute-start | bytes 786440 | tf_op jit(solution)/shard_map/ppermute | solution.py:49
  83.8 3.6 %collective-permute-start.17 = (bf16[2048,256]{1,0:T(8,128)(2,1)S(1)}, bf16[2048,256]{1,0:T(8,128)(2,1)S(1)}, u32[]{:S(2)}, u32[]{:S(2)}) collective-permute-start(bf16[2048,256]{1,0:T(8,128)(2,1)S(1)} %get-tuple-element.40), channel_id=1, source_target_pairs={{0,1},{1,0},{2,3},{3,2},{4,5},{5,4},{6,7},{7,6},{8,9},{9,8},{10,11... | collective-permute-start | bytes 3145736 | tf_op jit(solution)/shard_map/ppermute | solution.py:58
  83.9 3.5 %collective-permute-start.18 = (bf16[256,1024]{1,0:T(8,128)(2,1)S(1)}, bf16[256,1024]{1,0:T(8,128)(2,1)S(1)}, u32[]{:S(2)}, u32[]{:S(2)}) collective-permute-start(bf16[256,1024]{1,0:T(8,128)(2,1)S(1)} %get-tuple-element.41.score), channel_id=1, source_target_pairs={{0,1},{1,0},{2,3},{3,2},{4,5},{5,4},{6,7},{7,6},{8,9},{9,8},{10,11... | collective-permute-start | bytes 1572872 | tf_op jit(solution)/shard_map/ppermute | solution.py:58
  84.4 6.1 %collective-permute-start.14 = (bf16[256,256]{1,0:T(8,128)(2,1)S(1)}, bf16[256,256]{1,0:T(8,128)(2,1)S(1)}, u32[]{:S(2)}, u32[]{:S(2)}) collective-permute-start(bf16[256,256]{1,0:T(8,128)(2,1)S(1)} %get-tuple-element.49), channel_id=1, source_target_pairs={{0,192},{1,49},{2,194},{3,51},{4,196},{5,53},{6,198},{7,55},{8,200... | collective-permute-start | bytes 393224 | tf_op jit(solution)/shard_map/ppermute | solution.py:49
  85.7 6.5 %collective-permute-start.15 = (bf16[256,256]{1,0:T(8,128)(2,1)S(1)}, bf16[256,256]{1,0:T(8,128)(2,1)S(1)}, u32[]{:S(2)}, u32[]{:S(2)}) collective-permute-start(bf16[256,256]{1,0:T(8,128)(2,1)S(1)} %get-tuple-element.48), channel_id=1, source_target_pairs={{0,128},{1,33},{2,130},{3,35},{4,132},{5,37},{6,134},{7,39},{8,136... | collective-permute-start | bytes 393224 | tf_op jit(solution)/shard_map/ppermute | solution.py:49
  87.3 6.2 %collective-permute-start.16 = (bf16[256,256]{1,0:T(8,128)(2,1)S(1)}, bf16[256,256]{1,0:T(8,128)(2,1)S(1)}, u32[]{:S(2)}, u32[]{:S(2)}) collective-permute-start(bf16[256,256]{1,0:T(8,128)(2,1)S(1)} %get-tuple-element.47), channel_id=1, source_target_pairs={{0,64},{1,17},{2,66},{3,19},{4,68},{5,21},{6,70},{7,23},{8,72},{9,... | collective-permute-start | bytes 393224 | tf_op jit(solution)/shard_map/ppermute | solution.py:49

commit v10 on v9

--- a/solution.py
+++ b/solution.py
@@ -182,15 +182,18 @@
     times_head(own, core, column, head, score_t[...], outs)
 
 
-def weight_kernel(mine, theirs, score, score_theirs, out, held, sems):
+def own_weight_kernel(mine, score, total):
+    total[...] = jnp.dot(mine[...], score[...], preferred_element_type=f32)
+
+
+def weight_kernel(own_total, theirs, score_theirs, out, held, sems):
     def send(i):
         return pltpu.make_async_copy(held.at[i], out.at[pl.ds(i * SLAB, SLAB)], sems.at[i])
 
     for i in range(8):
         rows = pl.ds(i * SLAB, SLAB)
-        total = jnp.dot(mine[rows], score[...], preferred_element_type=f32)
-        total += jnp.dot(theirs[rows], score_theirs[...], preferred_element_type=f32)
-        held[i] = total.astype(bf16)
+        total = jnp.dot(theirs[rows], score_theirs[...], preferred_element_type=f32)
+        held[i] = (own_total[rows] + total).astype(bf16)
         send(i).start()
     for i in range(8):
         send(i).wait()
@@ -249,6 +252,14 @@
         7 * MIB,
     )
     d0, d1 = step(d0, 0, 0, 1), step(d1, 0, 0, -1)
+    (own_total,) = call(
+        own_weight_kernel,
+        [((FULL // 2, COLS), f32)],
+        [("v", mine), ("v", score)],
+        FULL * ROWS * COLS,
+        9 * MIB,
+    )
+    b, c, d0, d1, own_total = lax.optimization_barrier((b, c, d0, d1, own_total))
     part = a + b.astype(f32) + c.astype(f32) + jnp.concatenate([d0, d1], axis=0).astype(f32)
     part, theirs, score_theirs = lax.optimization_barrier((part, theirs, score))
     slabs = [part[i * SLAB : (i + 1) * SLAB] for i in range(4)]
@@ -257,8 +268,8 @@
     (weight_grad,) = call(
         weight_kernel,
         [((FULL // 2, COLS), bf16)],
-        [("v", mine), ("v", theirs), ("v", score), ("v", score_theirs)],
-        2 * FULL * ROWS * COLS,
+        [("v", own_total), ("v", theirs), ("v", score_theirs)],
+        FULL * ROWS * COLS,
         7 * MIB,
         [pltpu.VMEM((8, SLAB, COLS), bf16), pltpu.SemaphoreType.DMA((8,))],
         into="h",

time: 111 us -> 111 us (level)
    pallas_call x6 -> x7, Pallas kernels: 10.8 us -> 11.2 us  [call(): pl.pallas_call(body, out_shape=[jax.ShapeDtypeStruct(shape, dtype) for sh...]
  transfers between devices with their start and end apart: 19 -> 19, of which waited for: 12 -> 12; matrix products, arithmetic and copies ran while one was open for 0% -> 0% of each run, Pallas kernels for 4% -> 5%
where the time goes in v10:
time: 111 us; the launch traced here: 109 us
  blocking collectives  52.4 us (47%)
  starting transfers between devices  22.2 us (20%)
  waiting for transfers between devices  16.4 us (15%)
  Pallas kernels  11.2 us (10%)
  local copies, waits for them, and re-layouts  5.18 us (5%)
    all_to_all x3, blocking collectives, trade(): lax.all_to_all(chunks, BOTH, 0, 0, tiled=True, axis_index_groups=groups)  52.4 us
    ppermute x17, starting transfers between devices, step(): return lax.ppermute(value, BOTH, pairs)  21.6 us
    ppermute x17, waiting for transfers between devices, step(): return lax.ppermute(value, BOTH, pairs)  16.4 us
    pallas_call x7, Pallas kernels, call(): pl.pallas_call(body, out_shape=[jax.ShapeDtypeStruct(shape, dtype) for sh...  11.2 us
    unnamed x8, local copies, waits for them, and re-layouts  4.43 us
  transfers between devices with their start and end apart: 19, of which 12 were waited for; matrix products, arithmetic and copies ran while one was open for 0% of the time, Pallas kernels for 5%

profile of v10, /device:TPU:2, one launch (start us, length us, event | category | flops | bytes accessed | tf_op | source)
XLA Modules:
  0.0 109.1 jit_solution(18004731375375233673)
XLA Ops:
  0.6 0.7 broadcast_in_dim.18
  1.4 19.5 %all_to_all.15 = bf16[8,32,256]{2,1,0:T(8,128)(2,1)S(1)} all-to-all(bf16[8,32,256]{2,1,0:T(8,128)(2,1)S(1)} %broadcast_in_dim.18), channel_id=1, replica_groups={{0,34,4,38,8,42,12,46},{64,98,68,102,72,106,76,110},{128,162,132,166,13..., dimensions={0} | all-to-all | bytes 262144 | tf_op jit(solution)/shard_map/all_to_all | solution.py:38
  20.9 1.0 collective-permute-start
  21.9 2.7 %collective-permute-start.1 = (bf16[256,256]{1,0:T(8,128)(2,1)S(1)}, bf16[256,256]{1,0:T(8,128)(2,1)S(1)}, u32[]{:S(2)}, u32[]{:S(2)}) collective-permute-start(bf16[256,256]{1,0:T(8,128)(2,1)S(1)} %bitcast.11), channel_id=1, source_target_pairs={{0,128},{1,33},{2,130},{3,35},{4,132},{5,37},{6,134},{7,39},{8,136... | collective-permute-start | bytes 393224 | tf_op jit(solution)/shard_map/ppermute | solution.py:49
  24.6 1.3 %collective-permute-start.2 = (bf16[256,256]{1,0:T(8,128)(2,1)S(1)}, bf16[256,256]{1,0:T(8,128)(2,1)S(1)}, u32[]{:S(2)}, u32[]{:S(2)}) collective-permute-start(bf16[256,256]{1,0:T(8,128)(2,1)S(1)} %bitcast.12), channel_id=1, source_target_pairs={{0,192},{1,49},{2,194},{3,51},{4,196},{5,53},{6,198},{7,55},{8,200... | collective-permute-start | bytes 393224 | tf_op jit(solution)/shard_map/ppermute | solution.py:49
  25.9 1.1 %collective-permute-done = bf16[256,256]{1,0:T(8,128)(2,1)S(1)} collective-permute-done((bf16[256,256]{1,0:T(8,128)(2,1)S(1)}, bf16[256,256]{1,0:T(8,128)(2,1)S(1)}, u32[]{:S(2)}, u32[]{:S(2)}) %collective-permute-start) | collective-permute-done | bytes 131104 | tf_op jit(solution)/shard_map/ppermute | solution.py:49
  27.1 1.9 %collective-permute-done.1 = bf16[256,256]{1,0:T(8,128)(2,1)S(1)} collective-permute-done((bf16[256,256]{1,0:T(8,128)(2,1)S(1)}, bf16[256,256]{1,0:T(8,128)(2,1)S(1)}, u32[]{:S(2)}, u32[]{:S(2)}) %collective-permute-start.1) | collective-permute-done | bytes 131104 | tf_op jit(solution)/shard_map/ppermute | solution.py:49
  28.9 0.6 collective-permute-done.2
  29.6 1.8 %collective-permute-start.3 = (bf16[1024,256]{1,0:T(8,128)(2,1)S(1)}, bf16[1024,256]{1,0:T(8,128)(2,1)S(1)}, u32[]{:S(2)}, u32[]{:S(2)}) collective-permute-start(bf16[1024,256]{1,0:T(8,128)(2,1)S(1)} %pad_maximum_fusion.a), channel_id=1, source_target_pairs={{0,48},{1,193},{2,50},{3,195},{4,52},{5,197},{6,54},{7,199},{8,56}... | collective-permute-start | bytes 1572872 | tf_op jit(solution)/shard_map/ppermute | solution.py:49
  31.4 0.3 collective-permute-start.4
  31.7 0.9 collective-permute-start.6
  32.6 1.3 %collective-permute-start.5 = (bf16[512,256]{1,0:T(8,128)(2,1)S(1)}, bf16[512,256]{1,0:T(8,128)(2,1)S(1)}, u32[]{:S(2)}, u32[]{:S(2)}) collective-permute-start(bf16[512,256]{1,0:T(8,128)(2,1)S(1)} %pad_maximum_fusion.1), channel_id=1, source_target_pairs={{0,2},{1,3},{2,4},{3,5},{4,6},{5,7},{6,8},{7,9},{8,10},{9,11},{10,... | collective-permute-start | bytes 786440 | tf_op jit(solution)/shard_map/ppermute | solution.py:49
  33.9 0.0 copy-start
  33.9 3.4 %copy-done = bf16[4096,1024]{1,0:T(8,128)(2,1)S(1)} copy-done((bf16[4096,1024]{1,0:T(8,128)(2,1)S(1)}, bf16[4096,1024]{1,0:T(8,128)(2,1)}, u32[]{:S(2)}) %copy-start) | copy-done | bytes 8388632
  37.3 0.0 copy-start.1
  37.3 1.0 copy-done.1
  38.3 0.0 slice-start
  38.3 0.4 shard_map.58
  38.7 0.0 collective-permute-done.6.d1
  38.8 1.5 %collective-permute-done.5.d0 = bf16[512,256]{1,0:T(8,128)(2,1)S(1)} collective-permute-done((bf16[512,256]{1,0:T(8,128)(2,1)S(1)}, bf16[512,256]{1,0:T(8,128)(2,1)S(1)}, u32[]{:S(2)}, u32[]{:S(2)}) %collective-permute-start.5) | collective-permute-done | bytes 262176 | tf_op jit(solution)/shard_map/ppermute | solution.py:49
  40.3 0.0 collective-permute-done.3.b
  40.3 0.3 collective-permute-done.4.c
  40.6 0.0 slice-start.1
  40.6 3.5 %shard_map.59 = (f32[256,1024]{1,0:T(8,128)S(1)}, f32[256,128]{1,0:T(8,128)S(1)}, f32[6,128]{1,0:T(8,128)S(1)}, bf16[2048,256]{1,0:T(8,128)(2,1)S(1)}, bf16[2048,256]{1,0:T(8,128)(2,1)S(1)}) custom-call(s32[1]{0:T(128)} %bitcast.own, s32[1]{0:T(128)} %bitcast.1.core, s32[1]{0:T(128)} %bitcast.2.column, bf16[1024,256]{1,0:T(8,128)(2,1)S(1)} %pad_maximum_fusion.a, ...), custom_call_target="tpu_custom_call" | custom-call | flops 2147483648 | bytes 12582912 | tf_op jit(solution)/shard_map/pallas_call | solution.py:69
  44.1 1.7 %collective-permute-start.7 = (f32[6,128]{1,0:T(8,128)S(1)}, f32[6,128]{1,0:T(8,128)S(1)}, u32[]{:S(2)}, u32[]{:S(2)}) collective-permute-start(f32[6,128]{1,0:T(8,128)S(1)} %get-tuple-element.34.first), channel_id=1, source_target_pairs={{0,16},{1,65},{2,18},{3,67},{4,20},{5,69},{6,22},{7,71},{8,24},{9,... | collective-permute-start | bytes 9224 | tf_op jit(solution)/shard_map/ppermute | solution.py:49
  45.8 0.8 collective-permute-start.8
  46.6 1.1 %collective-permute-start.9 = (f32[6,128]{1,0:T(8,128)S(1)}, f32[6,128]{1,0:T(8,128)S(1)}, u32[]{:S(2)}, u32[]{:S(2)}) collective-permute-start(f32[6,128]{1,0:T(8,128)S(1)} %get-tuple-element.34.first), channel_id=1, source_target_pairs={{0,2},{1,3},{2,4},{3,5},{4,6},{5,7},{6,8},{7,9},{8,10},{9,11},{10,... | collective-permute-start | bytes 9224 | tf_op jit(solution)/shard_map/ppermute | solution.py:49
  47.8 0.3 collective-permute-done.7.second
  48.1 1.3 %collective-permute-done.8.third = f32[6,128]{1,0:T(8,128)S(1)} collective-permute-done((f32[6,128]{1,0:T(8,128)S(1)}, f32[6,128]{1,0:T(8,128)S(1)}, u32[]{:S(2)}, u32[]{:S(2)}) %collective-permute-start.8) | collective-permute-done | bytes 3104 | tf_op jit(solution)/shard_map/ppermute | solution.py:49
  49.4 2.1 %collective-permute-done.9.fourth = f32[6,128]{1,0:T(8,128)S(1)} collective-permute-done((f32[6,128]{1,0:T(8,128)S(1)}, f32[6,128]{1,0:T(8,128)S(1)}, u32[]{:S(2)}, u32[]{:S(2)}) %collective-permute-start.9) | collective-permute-done | bytes 3104 | tf_op jit(solution)/shard_map/ppermute | solution.py:49
  51.5 17.9 %all_to_all.16.stats = f32[32,6,128]{2,1,0:T(8,128)S(1)} all-to-all(f32[32,6,128]{2,1,0:T(8,128)S(1)} %shard_map.60), channel_id=1, replica_groups={{0,34,4,38,8,42,12,46,64,98,68,102,72,106,76,110,128,162,132,166,136,17..., dimensions={0} | all-to-all | bytes 196608 | tf_op jit(solution)/shard_map/all_to_all | solution.py:38
  69.4 0.0 slice-done
  69.4 0.0 slice-done.1
  69.4 2.3 %shard_map.61 = (bf16[256,1024]{1,0:T(8,128)(2,1)S(1)}, bf16[1024,256]{1,0:T(8,128)(2,1)S(1)}, bf16[1024,256]{1,0:T(8,128)(2,1)S(1)}, bf16[1024,256]{1,0:T(8,128)(2,1)S(1)}, f32[2,128]{1,0:T(2,128)}) custom-call(s32[1]{0:T(128)} %bitcast.own, s32[1]{0:T(128)} %bitcast.1.core, s32[1]{0:T(128)} %bitcast.2.column, f32[256,1024]{1,0:T(8,128)S(1)} %get-tuple-element.32.rise, ...), custom_call_target="tpu_custom_call" | custom-call | flops 1073741824 | bytes 8388608 | tf_op jit(solution)/shard_map/pallas_call | solution.py:69
  71.7 2.2 %collective-permute-start.10 = (bf16[1024,256]{1,0:T(8,128)(2,1)S(1)}, bf16[1024,256]{1,0:T(8,128)(2,1)S(1)}, u32[]{:S(2)}, u32[]{:S(2)}) collective-permute-start(bf16[1024,256]{1,0:T(8,128)(2,1)S(1)} %get-tuple-element.37), channel_id=1, source_target_pairs={{0,16},{1,65},{2,18},{3,67},{4,20},{5,69},{6,22},{7,71},{8,24},{9,... | collective-permute-start | bytes 1572872 | tf_op jit(solution)/shard_map/ppermute | solution.py:49
  73.9 0.2 collective-permute-start.11
  74.2 1.3 %shard_map.62 = (bf16[512,256]{1,0:T(8,128)(2,1)S(1)}, bf16[512,256]{1,0:T(8,128)(2,1)S(1)}, f32[1024,256]{1,0:T(8,128)S(1)}) custom-call(s32[1]{0:T(128)} %bitcast.own, s32[1]{0:T(128)} %bitcast.1.core, s32[1]{0:T(128)} %bitcast.2.column, bf16[1024,256]{1,0:T(8,128)(2,1)S(1)} %get-tuple-element.35.score_t, bf16[4096,1024]{1,0:T(8,128)(2,1)S(1)} %bitcast.9), custom_call_target="tpu_custom_call" | custom-call | flops 1073741824 | bytes 7340032 | tf_op jit(solution)/shard_map/pallas_call | solution.py:69
  75.4 1.7 %collective-permute-start.12 = (bf16[512,256]{1,0:T(8,128)(2,1)S(1)}, bf16[512,256]{1,0:T(8,128)(2,1)S(1)}, u32[]{:S(2)}, u32[]{:S(2)}) collective-permute-start(bf16[512,256]{1,0:T(8,128)(2,1)S(1)} %get-tuple-element.39), channel_id=1, source_target_pairs={{0,2},{1,3},{2,4},{3,5},{4,6},{5,7},{6,8},{7,9},{8,10},{9,11},{10,... | collective-permute-start | bytes 786440 | tf_op jit(solution)/shard_map/ppermute | solution.py:49
  77.1 1.6 %collective-permute-start.13 = (bf16[512,256]{1,0:T(8,128)(2,1)S(1)}, bf16[512,256]{1,0:T(8,128)(2,1)S(1)}, u32[]{:S(2)}, u32[]{:S(2)}) collective-permute-start(bf16[512,256]{1,0:T(8,128)(2,1)S(1)} %get-tuple-element.40), channel_id=1, source_target_pairs={{0,14},{1,15},{2,0},{3,1},{4,2},{5,3},{6,4},{7,5},{8,6},{9,7},{10,... | collective-permute-start | bytes 786440 | tf_op jit(solution)/shard_map/ppermute | solution.py:49
  78.7 1.3 %shard_map.63.own_total = f32[2048,1024]{1,0:T(8,128)S(1)} custom-call(bf16[2048,256]{1,0:T(8,128)(2,1)S(1)} %get-tuple-element.41.mine, bf16[256,1024]{1,0:T(8,128)(2,1)S(1)} %get-tuple-element.51.score), custom_call_target="tpu_custom_call" | custom-call | flops 1073741824 | bytes 9437184 | tf_op jit(solution)/shard_map/pallas_call | solution.py:69
  80.0 3.1 %collective-permute-done.12 = bf16[512,256]{1,0:T(8,128)(2,1)S(1)} collective-permute-done((bf16[512,256]{1,0:T(8,128)(2,1)S(1)}, bf16[512,256]{1,0:T(8,128)(2,1)S(1)}, u32[]{:S(2)}, u32[]{:S(2)}) %collective-permute-start.12) | collective-permute-done | bytes 262176 | tf_op jit(solution)/shard_map/ppermute | solution.py:49
  83.1 0.4 collective-permute-done.13
  83.5 0.0 collective-permute-done.10
  83.5 0.0 collective-permute-done.11
  83.5 0.2 convert_add_fusion
  83.7 0.1 collective-permute-start.17
  83.8 0.5 collective-permute-start.18
  84.3 0.1 convert.6
  84.4 1.2 %collective-permute-start.14 = (bf16[256,256]{1,0:T(8,128)(2,1)S(1)}, bf16[256,256]{1,0:T(8,128)(2,1)S(1)}, u32[]{:S(2)}, u32[]{:S(2)}) collective-permute-start(bf16[256,256]{1,0:T(8,128)(2,1)S(1)} %get-tuple-element.59), channel_id=1, source_target_pairs={{0,192},{1,49},{2,194},{3,51},{4,196},{5,53},{6,198},{7,55},{8,200... | collective-permute-start | bytes 393224 | tf_op jit(solution)/shard_map/ppermute | solution.py:49
  85.6 1.6 %collective-permute-start.15 = (bf16[256,256]{1,0:T(8,128)(2,1)S(1)}, bf16[256,256]{1,0:T(8,128)(2,1)S(1)}, u32[]{:S(2)}, u32[]{:S(2)}) collective-permute-start(bf16[256,256]{1,0:T(8,128)(2,1)S(1)} %get-tuple-element.58), channel_id=1, source_target_pairs={{0,128},{1,33},{2,130},{3,35},{4,132},{5,37},{6,134},{7,39},{8,136... | collective-permute-start | bytes 393224 | tf_op jit(solution)/shard_map/ppermute | solution.py:49
  87.3 0.0 collective-permute-start.16
  87.3 0.0 collective-permute-done.18.score_theirs
  87.3 0.0 collective-permute-done.17.theirs
  87.3 2.4 %shard_map.64 = bf16[2048,1024]{1,0:T(8,128)(2,1)} custom-call(f32[2048,1024]{1,0:T(8,128)S(1)} %shard_map.63.own_total, bf16[2048,256]{1,0:T(8,128)(2,1)S(1)} %collective-permute-done.17.theirs, bf16[256,1024]{1,0:T(8,128)(2,1)S(1)} %collective-permute-done.18.score_theirs), custom_call_target="tpu_custom_call" | custom-call | flops 1073741824 | bytes 7340032 | tf_op jit(solution)/shard_map/pallas_call | solution.py:69
  89.7 0.0 collective-permute-done.14
  89.7 2.4 %collective-permute-done.15 = bf16[256,256]{1,0:T(8,128)(2,1)S(1)} collective-permute-done((bf16[256,256]{1,0:T(8,128)(2,1)S(1)}, bf16[256,256]{1,0:T(8,128)(2,1)S(1)}, u32[]{:S(2)}, u32[]{:S(2)}) %collective-permute-start.15) | collective-permute-done | bytes 131104 | tf_op jit(solution)/shard_map/ppermute | solution.py:49
  92.1 1.4 %collective-permute-done.16 = bf16[256,256]{1,0:T(8,128)(2,1)S(1)} collective-permute-done((bf16[256,256]{1,0:T(8,128)(2,1)S(1)}, bf16[256,256]{1,0:T(8,128)(2,1)S(1)}, u32[]{:S(2)}, u32[]{:S(2)}) %collective-permute-start.16) | collective-permute-done | bytes 131104 | tf_op jit(solution)/shard_map/ppermute | solution.py:49
  93.5 0.1 add_convert_fusion
  93.6 14.9 %all_to_all.17 = bf16[8,32,256]{2,1,0:T(8,128)(2,1)S(1)} all-to-all(bf16[8,32,256]{2,1,0:T(8,128)(2,1)S(1)} %bitcast.15), channel_id=1, replica_groups={{0,34,4,38,8,42,12,46},{64,98,68,102,72,106,76,110},{128,162,132,166,13..., dimensions={0} | all-to-all | bytes 262144 | tf_op jit(solution)/shard_map/all_to_all | solution.py:38
  108.5 0.6 reduce_sum.12
  (6 shorter events, 0.1 us)
Async XLA Ops:
  20.9 6.2 %collective-permute-start = (bf16[256,256]{1,0:T(8,128)(2,1)S(1)}, bf16[256,256]{1,0:T(8,128)(2,1)S(1)}, u32[]{:S(2)}, u32[]{:S(2)}) collective-permute-start(bf16[256,256]{1,0:T(8,128)(2,1)S(1)} %bitcast.10), channel_id=1, source_target_pairs={{0,64},{1,17},{2,66},{3,19},{4,68},{5,21},{6,70},{7,23},{8,72},{9,... | collective-permute-start | bytes 393224 | tf_op jit(solution)/shard_map/ppermute | solution.py:49
  21.9 7.0 %collective-permute-start.1 = (bf16[256,256]{1,0:T(8,128)(2,1)S(1)}, bf16[256,256]{1,0:T(8,128)(2,1)S(1)}, u32[]{:S(2)}, u32[]{:S(2)}) collective-permute-start(bf16[256,256]{1,0:T(8,128)(2,1)S(1)} %bitcast.11), channel_id=1, source_target_pairs={{0,128},{1,33},{2,130},{3,35},{4,132},{5,37},{6,134},{7,39},{8,136... | collective-permute-start | bytes 393224 | tf_op jit(solution)/shard_map/ppermute | solution.py:49
  24.6 5.0 %collective-permute-start.2 = (bf16[256,256]{1,0:T(8,128)(2,1)S(1)}, bf16[256,256]{1,0:T(8,128)(2,1)S(1)}, u32[]{:S(2)}, u32[]{:S(2)}) collective-permute-start(bf16[256,256]{1,0:T(8,128)(2,1)S(1)} %bitcast.12), channel_id=1, source_target_pairs={{0,192},{1,49},{2,194},{3,51},{4,196},{5,53},{6,198},{7,55},{8,200... | collective-permute-start | bytes 393224 | tf_op jit(solution)/shard_map/ppermute | solution.py:49
  29.6 10.7 %collective-permute-start.3 = (bf16[1024,256]{1,0:T(8,128)(2,1)S(1)}, bf16[1024,256]{1,0:T(8,128)(2,1)S(1)}, u32[]{:S(2)}, u32[]{:S(2)}) collective-permute-start(bf16[1024,256]{1,0:T(8,128)(2,1)S(1)} %pad_maximum_fusion.a), channel_id=1, source_target_pairs={{0,48},{1,193},{2,50},{3,195},{4,52},{5,197},{6,54},{7,199},{8,56}... | collective-permute-start | bytes 1572872 | tf_op jit(solution)/shard_map/ppermute | solution.py:49
  31.4 9.2 %collective-permute-start.4 = (bf16[1024,256]{1,0:T(8,128)(2,1)S(1)}, bf16[1024,256]{1,0:T(8,128)(2,1)S(1)}, u32[]{:S(2)}, u32[]{:S(2)}) collective-permute-start(bf16[1024,256]{1,0:T(8,128)(2,1)S(1)} %pad_maximum_fusion.a), channel_id=1, source_target_pairs={{0,16},{1,65},{2,18},{3,67},{4,20},{5,69},{6,22},{7,71},{8,24},{9,... | collective-permute-start | bytes 1572872 | tf_op jit(solution)/shard_map/ppermute | solution.py:49
  31.7 7.0 %collective-permute-start.6 = (bf16[512,256]{1,0:T(8,128)(2,1)S(1)}, bf16[512,256]{1,0:T(8,128)(2,1)S(1)}, u32[]{:S(2)}, u32[]{:S(2)}) collective-permute-start(bf16[512,256]{1,0:T(8,128)(2,1)S(1)} %pad_maximum_fusion.2), channel_id=1, source_target_pairs={{0,14},{1,15},{2,0},{3,1},{4,2},{5,3},{6,4},{7,5},{8,6},{9,7},{10,... | collective-permute-start | bytes 786440 | tf_op jit(solution)/shard_map/ppermute | solution.py:49
  32.6 7.7 %collective-permute-start.5 = (bf16[512,256]{1,0:T(8,128)(2,1)S(1)}, bf16[512,256]{1,0:T(8,128)(2,1)S(1)}, u32[]{:S(2)}, u32[]{:S(2)}) collective-permute-start(bf16[512,256]{1,0:T(8,128)(2,1)S(1)} %pad_maximum_fusion.1), channel_id=1, source_target_pairs={{0,2},{1,3},{2,4},{3,5},{4,6},{5,7},{6,8},{7,9},{8,10},{9,11},{10,... | collective-permute-start | bytes 786440 | tf_op jit(solution)/shard_map/ppermute | solution.py:49
  33.9 3.4 %copy-start = (bf16[4096,1024]{1,0:T(8,128)(2,1)S(1)}, bf16[4096,1024]{1,0:T(8,128)(2,1)}, u32[]{:S(2)}) copy-start(bf16[4096,1024]{1,0:T(8,128)(2,1)} %head.7) | copy-start | bytes 25165828
  37.3 1.0 copy-start.1
  38.3 31.1 %slice-start = ((s8[8388608]{0:T(1024)(128)(4,1)}), s8[4194304]{0:T(1024)(128)(4,1)S(1)}, s32[]{:S(2)}) async-start(s8[8388608]{0:T(1024)(128)(4,1)} %bitcast.8), calls=%async_computation.3 | async-start | bytes 8388608
  40.6 28.8 %slice-start.1 = ((s8[8388608]{0:T(1024)(128)(4,1)}), s8[4194304]{0:T(1024)(128)(4,1)S(1)}, s32[]{:S(2)}) async-start(s8[8388608]{0:T(1024)(128)(4,1)} %bitcast.8), calls=%async_computation.4 | async-start | bytes 8388608
  44.1 4.0 %collective-permute-start.7 = (f32[6,128]{1,0:T(8,128)S(1)}, f32[6,128]{1,0:T(8,128)S(1)}, u32[]{:S(2)}, u32[]{:S(2)}) collective-permute-start(f32[6,128]{1,0:T(8,128)S(1)} %get-tuple-element.34.first), channel_id=1, source_target_pairs={{0,16},{1,65},{2,18},{3,67},{4,20},{5,69},{6,22},{7,71},{8,24},{9,... | collective-permute-start | bytes 9224 | tf_op jit(solution)/shard_map/ppermute | solution.py:49
  45.8 3.6 %collective-permute-start.8 = (f32[6,128]{1,0:T(8,128)S(1)}, f32[6,128]{1,0:T(8,128)S(1)}, u32[]{:S(2)}, u32[]{:S(2)}) collective-permute-start(f32[6,128]{1,0:T(8,128)S(1)} %get-tuple-element.34.first), channel_id=1, source_target_pairs={{0,48},{1,193},{2,50},{3,195},{4,52},{5,197},{6,54},{7,199},{8,56}... | collective-permute-start | bytes 9224 | tf_op jit(solution)/shard_map/ppermute | solution.py:49
  46.6 4.8 %collective-permute-start.9 = (f32[6,128]{1,0:T(8,128)S(1)}, f32[6,128]{1,0:T(8,128)S(1)}, u32[]{:S(2)}, u32[]{:S(2)}) collective-permute-start(f32[6,128]{1,0:T(8,128)S(1)} %get-tuple-element.34.first), channel_id=1, source_target_pairs={{0,2},{1,3},{2,4},{3,5},{4,6},{5,7},{6,8},{7,9},{8,10},{9,11},{10,... | collective-permute-start | bytes 9224 | tf_op jit(solution)/shard_map/ppermute | solution.py:49
  71.7 11.7 %collective-permute-start.10 = (bf16[1024,256]{1,0:T(8,128)(2,1)S(1)}, bf16[1024,256]{1,0:T(8,128)(2,1)S(1)}, u32[]{:S(2)}, u32[]{:S(2)}) collective-permute-start(bf16[1024,256]{1,0:T(8,128)(2,1)S(1)} %get-tuple-element.37), channel_id=1, source_target_pairs={{0,16},{1,65},{2,18},{3,67},{4,20},{5,69},{6,22},{7,71},{8,24},{9,... | collective-permute-start | bytes 1572872 | tf_op jit(solution)/shard_map/ppermute | solution.py:49
  73.9 9.5 %collective-permute-start.11 = (bf16[1024,256]{1,0:T(8,128)(2,1)S(1)}, bf16[1024,256]{1,0:T(8,128)(2,1)S(1)}, u32[]{:S(2)}, u32[]{:S(2)}) collective-permute-start(bf16[1024,256]{1,0:T(8,128)(2,1)S(1)} %get-tuple-element.38), channel_id=1, source_target_pairs={{0,48},{1,193},{2,50},{3,195},{4,52},{5,197},{6,54},{7,199},{8,56}... | collective-permute-start | bytes 1572872 | tf_op jit(solution)/shard_map/ppermute | solution.py:49
  75.4 7.7 %collective-permute-start.12 = (bf16[512,256]{1,0:T(8,128)(2,1)S(1)}, bf16[512,256]{1,0:T(8,128)(2,1)S(1)}, u32[]{:S(2)}, u32[]{:S(2)}) collective-permute-start(bf16[512,256]{1,0:T(8,128)(2,1)S(1)} %get-tuple-element.39), channel_id=1, source_target_pairs={{0,2},{1,3},{2,4},{3,5},{4,6},{5,7},{6,8},{7,9},{8,10},{9,11},{10,... | collective-permute-start | bytes 786440 | tf_op jit(solution)/shard_map/ppermute | solution.py:49
  77.1 6.4 %collective-permute-start.13 = (bf16[512,256]{1,0:T(8,128)(2,1)S(1)}, bf16[512,256]{1,0:T(8,128)(2,1)S(1)}, u32[]{:S(2)}, u32[]{:S(2)}) collective-permute-start(bf16[512,256]{1,0:T(8,128)(2,1)S(1)} %get-tuple-element.40), channel_id=1, source_target_pairs={{0,14},{1,15},{2,0},{3,1},{4,2},{5,3},{6,4},{7,5},{8,6},{9,7},{10,... | collective-permute-start | bytes 786440 | tf_op jit(solution)/shard_map/ppermute | solution.py:49
  83.7 3.6 %collective-permute-start.17 = (bf16[2048,256]{1,0:T(8,128)(2,1)S(1)}, bf16[2048,256]{1,0:T(8,128)(2,1)S(1)}, u32[]{:S(2)}, u32[]{:S(2)}) collective-permute-start(bf16[2048,256]{1,0:T(8,128)(2,1)S(1)} %get-tuple-element.50), channel_id=1, source_target_pairs={{0,1},{1,0},{2,3},{3,2},{4,5},{5,4},{6,7},{7,6},{8,9},{9,8},{10,11... | collective-permute-start | bytes 3145736 | tf_op jit(solution)/shard_map/ppermute | solution.py:58
  83.8 3.5 %collective-permute-start.18 = (bf16[256,1024]{1,0:T(8,128)(2,1)S(1)}, bf16[256,1024]{1,0:T(8,128)(2,1)S(1)}, u32[]{:S(2)}, u32[]{:S(2)}) collective-permute-start(bf16[256,1024]{1,0:T(8,128)(2,1)S(1)} %get-tuple-element.51.score), channel_id=1, source_target_pairs={{0,1},{1,0},{2,3},{3,2},{4,5},{5,4},{6,7},{7,6},{8,9},{9,8},{10,11... | collective-permute-start | bytes 1572872 | tf_op jit(solution)/shard_map/ppermute | solution.py:58
  84.4 5.3 %collective-permute-start.14 = (bf16[256,256]{1,0:T(8,128)(2,1)S(1)}, bf16[256,256]{1,0:T(8,128)(2,1)S(1)}, u32[]{:S(2)}, u32[]{:S(2)}) collective-permute-start(bf16[256,256]{1,0:T(8,128)(2,1)S(1)} %get-tuple-element.59), channel_id=1, source_target_pairs={{0,192},{1,49},{2,194},{3,51},{4,196},{5,53},{6,198},{7,55},{8,200... | collective-permute-start | bytes 393224 | tf_op jit(solution)/shard_map/ppermute | solution.py:49
  85.6 6.5 %collective-permute-start.15 = (bf16[256,256]{1,0:T(8,128)(2,1)S(1)}, bf16[256,256]{1,0:T(8,128)(2,1)S(1)}, u32[]{:S(2)}, u32[]{:S(2)}) collective-permute-start(bf16[256,256]{1,0:T(8,128)(2,1)S(1)} %get-tuple-element.58), channel_id=1, source_target_pairs={{0,128},{1,33},{2,130},{3,35},{4,132},{5,37},{6,134},{7,39},{8,136... | collective-permute-start | bytes 393224 | tf_op jit(solution)/shard_map/ppermute | solution.py:49
  87.3 6.2 %collective-permute-start.16 = (bf16[256,256]{1,0:T(8,128)(2,1)S(1)}, bf16[256,256]{1,0:T(8,128)(2,1)S(1)}, u32[]{:S(2)}, u32[]{:S(2)}) collective-permute-start(bf16[256,256]{1,0:T(8,128)(2,1)S(1)} %get-tuple-element.57), channel_id=1, source_target_pairs={{0,64},{1,17},{2,66},{3,19},{4,68},{5,21},{6,70},{7,23},{8,72},{9,... | collective-permute-start | bytes 393224 | tf_op jit(solution)/shard_map/ppermute | solution.py:49
